TPU v7x, 32 devices: a whole 2x2x4 slice. The times are simulated.
32 devices in a mesh: groups: 2 (over x), tm: 16 (over z, y, core).
Axes of the slice: x: 2, y: 2, z: 4, core: 2. Of those that a mesh axis runs over, the one named last changes fastest.
Arguments:
- signal: float32 [2, 8192], P('groups', 'tm'), parts along dimension 0, may hold values from -6 to 6
- codes: bfloat16 [2, 1024, 8192], P('groups', None, 'tm'), parts along dimension 0, may hold values from -6 to 6
- dictionary: float32 [1024, 512], P('tm'), may hold values from -6 to 6
- thresholds: float32 [1024], replicated, may hold values from 0.02 to 0.2
Outputs:
- codes_out: bfloat16 [2, 1024, 8192], P('groups', None, 'tm'), parts along dimension 0
- dictionary_out: float32 [2048, 512], P(('groups', 'tm')), parts along dimension 0
- residual_out: float32 [2, 8192], P('groups', 'tm'), parts along dimension 0
There are 2 independent parts, one for each index of `groups`. A program takes and returns all parts, laid end to end along the dimension named above; an argument that names none is the same for every part. Nothing has to cross between parts.
All inputs are finite; a program needn't handle non-finite values.
Results may differ from a plain program's by a relative error of at most 0.0072.
Values may be sent and summed in bfloat16 or wider, within the bound.
No kernel may reach another device: no remote copies, remote signals or barrier semaphores. Data moves between devices by JAX's collectives and lax.ppermute only.
A program may use at most 64 MiB of HBM per device.

v0:
```python
import functools

import jax
import jax.numpy as jnp
from jax import lax
from jax.experimental import pallas as pl
from jax.experimental.pallas import tpu as pltpu
from jax.sharding import PartitionSpec as P

CODE_STEP = 6.0
EPSILON = 1e-06
LANES = 128
F32, BF16 = jnp.float32, jnp.bfloat16
VMEM_BYTES = 48 * 1024 * 1024


def dot(a, b, dims):
    return lax.dot_general(a, b, (dims, ((), ())), preferred_element_type=F32)


def repeat(count, body):
    if count <= 16:
        for i in range(count):
            body(i)
    else:
        def step(i, carry):
            body(i)
            return carry
        lax.fori_loop(0, count, step, 0)


def row_lane():
    shape = (LANES, LANES)
    return lax.broadcasted_iota(jnp.int32, shape, 0), lax.broadcasted_iota(jnp.int32, shape, 1)


def turned_left(row):
    group = jnp.broadcast_to(row, (8, LANES))
    q = lax.broadcasted_iota(jnp.int32, (8, LANES), 0)
    for bit in (1, 2, 4):
        group = jnp.where((q & bit) != 0, pltpu.roll(group, LANES - bit, 1), group)
    return jnp.concatenate([group] + [pltpu.roll(group, LANES - a, 1) for a in range(8, LANES, 8)], axis=0)


def fill_hankel(rows_ref, hankel_ref, first, count):
    q, v = row_lane()
    keep = q + v < LANES
    here = turned_left(rows_ref[pl.ds(first, 1), :])
    for i in range(count):
        after = turned_left(rows_ref[pl.ds(first + i + 1, 1), :])
        hankel_ref[first + i] = jnp.where(keep, here, after).astype(BF16)
        here = after


def windows_of(hankel_ref, slab, width):
    per = width // LANES
    rows = [
        jnp.concatenate([hankel_ref[slab * per + p + i] for i in range(per)], axis=1)
        for p in range(per)
    ]
    return jnp.concatenate(rows, axis=0)


def soft(value, cutoff):
    return value - jnp.minimum(jnp.maximum(value, -cutoff), cutoff)


def normalised(updated):
    return updated / jnp.sqrt(jnp.mean(updated * updated, axis=1, keepdims=True) + EPSILON)


def stacked_taps(atoms):
    return jnp.concatenate([atoms[:, i : i + LANES] for i in range(0, atoms.shape[1], LANES)], axis=0)


def rebuild(taps, slab_of, slabs, width, turned_ref, sums_ref):
    per = width // LANES
    q, v = row_lane()
    keep = v >= q
    turned_ref[...] = jnp.zeros_like(turned_ref)

    def body(n):
        now, before = slab_of(n), slab_of(n - 1)
        shifted = [now] + [
            jnp.concatenate([before[:, width - LANES * p :], now[:, : width - LANES * p]], axis=1) for p in range(1, per)
        ]
        products = dot(taps, jnp.concatenate(shifted, axis=0), ((0,), (0,)))
        last = turned_ref[...]
        for i in range(per):
            turned = pltpu.roll(products[:, LANES * i : LANES * (i + 1)], 0, 1, stride=1, stride_axis=0)
            placed = jnp.where(keep, turned, last)
            sums_ref[n * per + i] = placed.reshape(LANES // 8, 8, LANES).sum(axis=0)
            last = turned
        turned_ref[...] = last

    repeat(slabs, body)


def partial_residual(me, factor, signal_ref, sums_ref, out_ref):
    rows = signal_ref.shape[0]
    out_ref[...] = -factor * jnp.sum(sums_ref[...], axis=1)
    own = pl.ds(me * rows, rows)
    out_ref[own, :] = out_ref[own, :] + signal_ref[...]


def first_kernel(factor, me_ref, atoms_ref, codes_ref, signal_ref, out_ref, turned_ref, sums_ref):
    slabs, owned, width = codes_ref.shape
    taps = stacked_taps(atoms_ref[...].astype(BF16))
    zero = jnp.zeros((owned, width), BF16)

    def slab_of(n):
        if isinstance(n, int):
            return codes_ref[n] if n >= 0 else zero
        return jnp.where(n >= 0, codes_ref[jnp.maximum(n, 0)], zero)

    rebuild(taps, slab_of, slabs, width, turned_ref, sums_ref)
    partial_residual(me_ref[0], factor, signal_ref, sums_ref, out_ref)


def round_rows(residual_ref, rows_ref):
    count = residual_ref.shape[0]
    rows_ref[:count, :] = residual_ref[...].astype(BF16).astype(F32)
    rows_ref[count:, :] = jnp.zeros((rows_ref.shape[0] - count, LANES), F32)


def second_kernel(
    factor, me_ref, residual_ref, atoms_ref, codes_ref, thresholds_ref, signal_ref,
    atoms_out, rounded_out, codes_out, part_out,
    rows_ref, hankel_ref, gradient_ref, turned_ref, sums_ref,
):
    slabs, owned, width = codes_ref.shape
    per = width // LANES
    round_rows(residual_ref, rows_ref)
    atoms = atoms_ref[...]
    atoms_b = atoms.astype(BF16)
    cutoff = CODE_STEP * thresholds_ref[...]
    gradient_ref[...] = jnp.zeros_like(gradient_ref)
    codes_out[0] = jnp.zeros((owned, width), BF16)
    fill_hankel(rows_ref, hankel_ref, 0, per - 1)

    def body(n):
        fill_hankel(rows_ref, hankel_ref, n * per + per - 1, per)
        frames = windows_of(hankel_ref, n, width)
        code = codes_ref[n]
        both = dot(jnp.concatenate([atoms_b, code], axis=0), frames, ((1,), (0,)))
        gradient_ref[...] += both[owned:]
        value = code.astype(F32) + (CODE_STEP * factor) * both[:owned]
        codes_out[n + 1] = soft(value, cutoff).astype(BF16)

    repeat(slabs, body)
    after = normalised(atoms + factor * gradient_ref[...])
    atoms_out[...] = after
    after_b = after.astype(BF16)
    rounded_out[...] = after_b
    rebuild(stacked_taps(after_b), lambda n: codes_out[n + 1], slabs, width, turned_ref, sums_ref)
    partial_residual(me_ref[0], factor, signal_ref, sums_ref, part_out)


def third_kernel(
    factor, me_ref, first_ref, second_ref, atoms_ref, owned_codes_ref, before_ref, after_ref, codes_ref, thresholds_ref,
    atoms_out, residual_out, codes_out,
    rows_ref, hankel_ref, gradient_ref, part_rows_ref, part_hankel_ref,
):
    slabs, owned, width = owned_codes_ref.shape
    slabs -= 1
    per = width // LANES
    me = me_ref[0]
    cutoff = CODE_STEP * thresholds_ref[...]
    frames = []
    for i, residual in enumerate((first_ref, second_ref)):
        round_rows(residual, rows_ref)
        part_rows_ref[: 2 * per, :] = rows_ref[pl.ds(me * per, 2 * per), :]
        fill_hankel(part_rows_ref, part_hankel_ref, 0, 2 * per - 1)
        frames.append(windows_of(part_hankel_ref, 0, width))
    step = 256 if codes_ref.shape[0] % 256 == 0 else codes_ref.shape[0]
    for start in range(0, codes_ref.shape[0], step):
        own = slice(start, start + step)
        value = codes_ref[own, :].astype(F32)
        for atoms_b, frame in ((before_ref, frames[0]), (after_ref, frames[1])):
            value = soft(value + (CODE_STEP * factor) * dot(atoms_b[own, :], frame, ((1,), (0,))), cutoff[own, :])
        codes_out[own, :] = value.astype(BF16)
    gradient_ref[...] = jnp.zeros_like(gradient_ref)
    fill_hankel(rows_ref, hankel_ref, 0, per - 1)

    def body(n):
        fill_hankel(rows_ref, hankel_ref, n * per + per - 1, per)
        gradient_ref[...] += dot(owned_codes_ref[n + 1], windows_of(hankel_ref, n, width), ((1,), (0,)))

    repeat(slabs, body)
    atoms_out[...] = normalised(atoms_ref[...] + factor * gradient_ref[...])
    residual_out[...] = second_ref[pl.ds(me * per, per), :]


def call(kernel, outs, scratch, *args):
    vmem = pl.BlockSpec(memory_space=pltpu.VMEM)
    return pl.pallas_call(
        kernel,
        out_shape=outs,
        in_specs=[pl.BlockSpec(memory_space=pltpu.SMEM)] + [vmem] * (len(args) - 1),
        out_specs=jax.tree.map(lambda _: vmem, outs),
        scratch_shapes=scratch,
        compiler_params=pltpu.CompilerParams(vmem_limit_bytes=VMEM_BYTES),
    )(*args)


def swapped(block, distance):
    count = lax.axis_size("tm")
    return lax.ppermute(block, "tm", [(i, i ^ distance) for i in range(count)])


def gathered(block):
    me = lax.axis_index("tm")
    rows, width = block.shape
    block = block[None]
    distance = lax.axis_size("tm") // 2
    while distance:
        other = swapped(block, distance)
        upper = (me & distance) != 0
        low, high = jnp.where(upper, other, block), jnp.where(upper, block, other)
        block = jnp.stack([low, high], axis=1).reshape(-1, rows, width)
        distance //= 2
    return block.reshape(-1, width)


def summed(part):
    distance = 1
    while distance < lax.axis_size("tm"):
        part = part + swapped(part, distance)
        distance *= 2
    return part


def on_device(signal, codes, dictionary, thresholds):
    _, atom_count, width = codes.shape
    owned, lag_count = dictionary.shape
    slabs = lax.axis_size("tm")
    per = width // LANES
    blocks = slabs * per
    factor = (atom_count * lag_count) ** (-0.5)
    me = lax.axis_index("tm")
    at = me.astype(jnp.int32).reshape(1)
    signal_rows = signal.reshape(per, LANES)
    own_thresholds = lax.dynamic_slice(thresholds, (me * owned,), (owned,)).reshape(owned, 1)
    codes = codes[0]

    by_atom = lax.all_to_all(codes.reshape(slabs, owned, width), "tm", 0, 0, tiled=True)
    before = gathered(dictionary.astype(BF16))

    sums = [pltpu.VMEM((LANES, LANES), F32), pltpu.VMEM((blocks, 8, LANES), F32)]
    rows = [
        pltpu.VMEM((blocks + 8, LANES), F32),
        pltpu.VMEM((blocks + per - 1, LANES, LANES), BF16),
        pltpu.VMEM((owned, lag_count), F32),
    ]
    residual_shape = jax.ShapeDtypeStruct((blocks, LANES), F32)
    part = call(functools.partial(first_kernel, factor), residual_shape, sums, at, dictionary, by_atom, signal_rows)
    first = summed(part)
    atoms, after, next_codes, part = call(
        functools.partial(second_kernel, factor),
        (
            jax.ShapeDtypeStruct((owned, lag_count), F32),
            jax.ShapeDtypeStruct((owned, lag_count), BF16),
            jax.ShapeDtypeStruct((slabs + 1, owned, width), BF16),
            residual_shape,
        ),
        rows + sums,
        at, first, dictionary, by_atom, own_thresholds, signal_rows,
    )
    second = summed(part)
    after = gathered(after)
    atoms, residual, codes = call(
        functools.partial(third_kernel, factor),
        (
            jax.ShapeDtypeStruct((owned, lag_count), F32),
            jax.ShapeDtypeStruct((per, LANES), F32),
            jax.ShapeDtypeStruct((atom_count, width), BF16),
        ),
        rows + [pltpu.VMEM((2 * per, LANES), F32), pltpu.VMEM((2 * per - 1, LANES, LANES), BF16)],
        at, first, second, atoms, next_codes, before, after, codes, thresholds.reshape(atom_count, 1),
    )
    return codes[None], atoms, residual.reshape(1, width)


def solution(mesh):
    return jax.shard_map(
        on_device,
        mesh=mesh,
        in_specs=(P("groups", "tm"), P("groups", None, "tm"), P("tm", None), P()),
        out_specs=(P("groups", None, "tm"), P(("groups", "tm"), None), P("groups", "tm")),
        check_vma=False,
    )
```

profile of v0, /device:TPU:0, one launch (start us, length us, event | category | flops | bytes accessed | tf_op | source)
XLA Modules:
  0.0 105.1 jit_solution(8889412195781746100)
XLA Ops:
  0.6 7.5 %all-to-all-start = ((bf16[16,64,512]{2,1,0:T(8,128)(2,1)}), bf16[16,64,512]{2,1,0:T(8,128)(2,1)S(1)}, u32[]{:S(2)}, u32[]{:S(2)}) async-start(bf16[16,64,512]{2,1,0:T(8,128)(2,1)} %bitcast.74), calls=%async_computation | async-start | bytes 2097152 | tf_op jit(solution)/shard_map/all_to_all | solution.py:246
  8.2 0.0 copy-start.3
  8.2 22.9 %all-to-all-done.codes_ref = bf16[16,64,512]{2,1,0:T(8,128)(2,1)S(1)} async-done(((bf16[16,64,512]{2,1,0:T(8,128)(2,1)}), bf16[16,64,512]{2,1,0:T(8,128)(2,1)S(1)}, u32[]{:S(2)}, u32[]{:S(2)}) %all-to-all-start) | async-done | bytes 1048608 | tf_op jit(solution)/shard_map/all_to_all | solution.py:246
  31.1 1.4 %shard_map.67 = f32[64,128]{1,0:T(8,128)S(1)} custom-call(s32[1]{0:T(128)} %bitcast.me_ref, f32[64,512]{1,0:T(8,128)S(1)} %copy-done.1, bf16[16,64,512]{2,1,0:T(8,128)(2,1)S(1)} %all-to-all-done.codes_ref, f32[4,128]{1,0:T(4,128)S(1)} %bitcast.79), custom_call_target="tpu_custom_call" | custom-call | tf_op jit(solution)/shard_map/pallas_call | solution.py:196
  32.6 0.7 collective-permute-start
  33.2 0.9 collective-permute-done
  34.1 2.0 %collective-permute-start.1 = (f32[64,128]{1,0:T(8,128)S(1)}, f32[64,128]{1,0:T(8,128)S(1)}, u32[]{:S(2)}, u32[]{:S(2)}) collective-permute-start(f32[64,128]{1,0:T(8,128)S(1)} %add.27), channel_id=1, source_target_pairs={{0,2},{1,3},{2,0},{3,1},{4,6},{5,7},{6,4},{7,5},{8,10},{9,11},{10,... | collective-permute-start | bytes 98312 | tf_op jit(solution)/shard_map/ppermute | solution.py:208
  36.1 2.9 %collective-permute-start.8 = (bf16[1,64,512]{2,1,0:T(8,128)(2,1)S(1)}, bf16[1,64,512]{2,1,0:T(8,128)(2,1)S(1)}, u32[]{:S(2)}, u32[]{:S(2)}) collective-permute-start(bf16[1,64,512]{2,1,0:T(8,128)(2,1)S(1)} %convert_bitcast_fusion), channel_id=1, source_target_pairs={{0,8},{1,9},{2,10},{3,11},{4,12},{5,13},{6,14},{7,15},{8,0},{9,1},... | collective-permute-start | bytes 196616 | tf_op jit(solution)/shard_map/ppermute | solution.py:208
  39.0 2.4 %collective-permute-start.2 = (f32[64,128]{1,0:T(8,128)S(1)}, f32[64,128]{1,0:T(8,128)S(1)}, u32[]{:S(2)}, u32[]{:S(2)}) collective-permute-start(f32[64,128]{1,0:T(8,128)S(1)} %add.28), channel_id=1, source_target_pairs={{0,4},{1,5},{2,6},{3,7},{4,0},{5,1},{6,2},{7,3},{8,12},{9,13},{10,... | collective-permute-start | bytes 98312 | tf_op jit(solution)/shard_map/ppermute | solution.py:208
  41.4 0.1 dynamic-slice_bitcast_fusion
  41.5 0.1 copy.18.thresholds_ref
  41.6 1.7 %collective-permute-done.2 = f32[64,128]{1,0:T(8,128)S(1)} collective-permute-done((f32[64,128]{1,0:T(8,128)S(1)}, f32[64,128]{1,0:T(8,128)S(1)}, u32[]{:S(2)}, u32[]{:S(2)}) %collective-permute-start.2) | collective-permute-done | bytes 32800 | tf_op jit(solution)/shard_map/ppermute | solution.py:208
  43.3 3.5 %collective-permute-start.3 = (f32[64,128]{1,0:T(8,128)S(1)}, f32[64,128]{1,0:T(8,128)S(1)}, u32[]{:S(2)}, u32[]{:S(2)}) collective-permute-start(f32[64,128]{1,0:T(8,128)S(1)} %add.29), channel_id=1, source_target_pairs={{0,8},{1,9},{2,10},{3,11},{4,12},{5,13},{6,14},{7,15},{8,0},{9,1},... | collective-permute-start | bytes 98312 | tf_op jit(solution)/shard_map/ppermute | solution.py:208
  46.8 1.9 %collective-permute-done.3 = f32[64,128]{1,0:T(8,128)S(1)} collective-permute-done((f32[64,128]{1,0:T(8,128)S(1)}, f32[64,128]{1,0:T(8,128)S(1)}, u32[]{:S(2)}, u32[]{:S(2)}) %collective-permute-start.3) | collective-permute-done | bytes 32800 | tf_op jit(solution)/shard_map/ppermute | solution.py:208
  48.6 10.2 %shard_map.68 = (f32[64,512]{1,0:T(8,128)S(1)}, bf16[64,512]{1,0:T(8,128)(2,1)S(1)}, bf16[17,64,512]{2,1,0:T(8,128)(2,1)S(1)}, f32[64,128]{1,0:T(8,128)S(1)}) custom-call(s32[1]{0:T(128)} %bitcast.me_ref, f32[64,128]{1,0:T(8,128)S(1)} %add.30.residual_ref.first_ref, f32[64,512]{1,0:T(8,128)S(1)} %copy-done.1, ...), custom_call_target="tpu_custom_call" | custom-call | tf_op jit(solution)/shard_map/pallas_call | solution.py:196
  58.8 3.0 %collective-permute-start.12 = (bf16[1,64,512]{2,1,0:T(8,128)(2,1)S(1)}, bf16[1,64,512]{2,1,0:T(8,128)(2,1)S(1)}, u32[]{:S(2)}, u32[]{:S(2)}) collective-permute-start(bf16[1,64,512]{2,1,0:T(8,128)(2,1)S(1)} %bitcast.78), channel_id=1, source_target_pairs={{0,8},{1,9},{2,10},{3,11},{4,12},{5,13},{6,14},{7,15},{8,0},{9,1},... | collective-permute-start | bytes 196616 | tf_op jit(solution)/shard_map/ppermute | solution.py:208
  61.8 0.5 collective-permute-start.9
  62.4 1.8 %collective-permute-done.12 = bf16[1,64,512]{2,1,0:T(8,128)(2,1)S(1)} collective-permute-done((bf16[1,64,512]{2,1,0:T(8,128)(2,1)S(1)}, bf16[1,64,512]{2,1,0:T(8,128)(2,1)S(1)}, u32[]{:S(2)}, u32[]{:S(2)}) %collective-permute-start.12) | collective-permute-done | bytes 65568 | tf_op jit(solution)/shard_map/ppermute | solution.py:208
  64.2 1.8 %collective-permute-start.13 = (bf16[2,64,512]{2,1,0:T(8,128)(2,1)S(1)}, bf16[2,64,512]{2,1,0:T(8,128)(2,1)S(1)}, u32[]{:S(2)}, u32[]{:S(2)}) collective-permute-start(bf16[2,64,512]{2,1,0:T(8,128)(2,1)S(1)} %maximum_bitcast_fusion.1), channel_id=1, source_target_pairs={{0,4},{1,5},{2,6},{3,7},{4,0},{5,1},{6,2},{7,3},{8,12},{9,13},{10,... | collective-permute-start | bytes 393224 | tf_op jit(solution)/shard_map/ppermute | solution.py:208
  66.0 0.8 collective-permute-done.9
  66.9 2.4 %collective-permute-done.13 = bf16[2,64,512]{2,1,0:T(8,128)(2,1)S(1)} collective-permute-done((bf16[2,64,512]{2,1,0:T(8,128)(2,1)S(1)}, bf16[2,64,512]{2,1,0:T(8,128)(2,1)S(1)}, u32[]{:S(2)}, u32[]{:S(2)}) %collective-permute-start.13) | collective-permute-done | bytes 131104 | tf_op jit(solution)/shard_map/ppermute | solution.py:208
  69.4 1.7 %collective-permute-start.14 = (bf16[4,64,512]{2,1,0:T(8,128)(2,1)S(1)}, bf16[4,64,512]{2,1,0:T(8,128)(2,1)S(1)}, u32[]{:S(2)}, u32[]{:S(2)}) collective-permute-start(bf16[4,64,512]{2,1,0:T(8,128)(2,1)S(1)} %bitcast.84), channel_id=1, source_target_pairs={{0,2},{1,3},{2,0},{3,1},{4,6},{5,7},{6,4},{7,5},{8,10},{9,11},{10,... | collective-permute-start | bytes 786440 | tf_op jit(solution)/shard_map/ppermute | solution.py:208
  71.1 0.5 collective-permute-start.10
  71.6 5.8 %collective-permute-done.14 = bf16[4,64,512]{2,1,0:T(8,128)(2,1)S(1)} collective-permute-done((bf16[4,64,512]{2,1,0:T(8,128)(2,1)S(1)}, bf16[4,64,512]{2,1,0:T(8,128)(2,1)S(1)}, u32[]{:S(2)}, u32[]{:S(2)}) %collective-permute-start.14) | collective-permute-done | bytes 262176 | tf_op jit(solution)/shard_map/ppermute | solution.py:208
  77.4 0.1 select_bitcast_fusion.5
  77.4 0.1 pad_maximum_fusion.3
  77.5 0.1 collective-permute-start.15
  77.6 0.5 collective-permute-start.4
  78.1 2.1 %collective-permute-done.10 = bf16[4,64,512]{2,1,0:T(8,128)(2,1)S(1)} collective-permute-done((bf16[4,64,512]{2,1,0:T(8,128)(2,1)S(1)}, bf16[4,64,512]{2,1,0:T(8,128)(2,1)S(1)}, u32[]{:S(2)}, u32[]{:S(2)}) %collective-permute-start.10) | collective-permute-done | bytes 262176 | tf_op jit(solution)/shard_map/ppermute | solution.py:208
  80.2 0.1 select_bitcast_fusion.7
  80.3 0.1 pad_maximum_fusion.2
  80.4 0.1 collective-permute-start.11
  80.5 1.8 %collective-permute-start.5 = (f32[64,128]{1,0:T(8,128)S(1)}, f32[64,128]{1,0:T(8,128)S(1)}, u32[]{:S(2)}, u32[]{:S(2)}) collective-permute-start(f32[64,128]{1,0:T(8,128)S(1)} %add.32), channel_id=1, source_target_pairs={{0,2},{1,3},{2,0},{3,1},{4,6},{5,7},{6,4},{7,5},{8,10},{9,11},{10,... | collective-permute-start | bytes 98312 | tf_op jit(solution)/shard_map/ppermute | solution.py:208
  82.3 2.2 %collective-permute-done.5 = f32[64,128]{1,0:T(8,128)S(1)} collective-permute-done((f32[64,128]{1,0:T(8,128)S(1)}, f32[64,128]{1,0:T(8,128)S(1)}, u32[]{:S(2)}, u32[]{:S(2)}) %collective-permute-start.5) | collective-permute-done | bytes 32800 | tf_op jit(solution)/shard_map/ppermute | solution.py:208
  84.5 0.2 collective-permute-start.6
  84.6 3.7 %collective-permute-done.6 = f32[64,128]{1,0:T(8,128)S(1)} collective-permute-done((f32[64,128]{1,0:T(8,128)S(1)}, f32[64,128]{1,0:T(8,128)S(1)}, u32[]{:S(2)}, u32[]{:S(2)}) %collective-permute-start.6) | collective-permute-done | bytes 32800 | tf_op jit(solution)/shard_map/ppermute | solution.py:208
  88.4 1.9 %collective-permute-start.7 = (f32[64,128]{1,0:T(8,128)S(1)}, f32[64,128]{1,0:T(8,128)S(1)}, u32[]{:S(2)}, u32[]{:S(2)}) collective-permute-start(f32[64,128]{1,0:T(8,128)S(1)} %add.34), channel_id=1, source_target_pairs={{0,8},{1,9},{2,10},{3,11},{4,12},{5,13},{6,14},{7,15},{8,0},{9,1},... | collective-permute-start | bytes 98312 | tf_op jit(solution)/shard_map/ppermute | solution.py:208
  90.3 0.2 copy.25.thresholds_ref
  90.5 2.8 %collective-permute-done.7 = f32[64,128]{1,0:T(8,128)S(1)} collective-permute-done((f32[64,128]{1,0:T(8,128)S(1)}, f32[64,128]{1,0:T(8,128)S(1)}, u32[]{:S(2)}, u32[]{:S(2)}) %collective-permute-start.7) | collective-permute-done | bytes 32800 | tf_op jit(solution)/shard_map/ppermute | solution.py:208
  93.3 1.1 %select_bitcast_fusion.1 = (bf16[8,1,64,512]{3,2,0,1:T(8,128)(2,1)S(1)}, bf16[8,1,64,512]{3,2,0,1:T(8,128)(2,1)S(1)}) fusion(bf16[8,64,512]{2,1,0:T(8,128)(2,1)} %collective-permute-done.15, pred[]{:T(512)S(6)} %ne.16, bf16[4,2,64,512]{3,2,1,0:T(8,128)(2,1)S(1)} %copy.23), kind=kLoop, calls=%fused_computation.5 | loop fusion | flops 524288 | bytes 2097153 | tf_op jit(solution)/shard_map/stack | solution.py:220
  94.5 0.1 pad_maximum_fusion.1
  94.6 0.1 copy.24
  94.7 1.1 %select_bitcast_fusion.3 = (bf16[8,1,64,512]{3,2,0,1:T(8,128)(2,1)S(1)}, bf16[8,1,64,512]{3,2,0,1:T(8,128)(2,1)S(1)}) fusion(bf16[8,64,512]{2,1,0:T(8,128)(2,1)} %collective-permute-done.11, pred[]{:T(512)S(6)} %ne.16, bf16[4,2,64,512]{3,2,1,0:T(8,128)(2,1)S(1)} %copy.20), kind=kLoop, calls=%fused_computation.7 | loop fusion | flops 524288 | bytes 2097153 | tf_op jit(solution)/shard_map/stack | solution.py:220
  95.8 0.1 pad_maximum_fusion
  95.9 0.0 copy-start
  95.9 0.1 copy.21
  96.0 1.1 %copy-done = bf16[1,1024,512]{2,1,0:T(8,128)(2,1)S(1)} copy-done((bf16[1,1024,512]{2,1,0:T(8,128)(2,1)S(1)}, bf16[1,1024,512]{2,1,0:T(8,128)(2,1)}, u32[]{:S(2)}) %copy-start) | copy-done | bytes 1048600
  97.1 8.0 %shard_map.69 = (f32[64,512]{1,0:T(8,128)}, f32[4,128]{1,0:T(4,128)}, bf16[1024,512]{1,0:T(8,128)(2,1)}) custom-call(s32[1]{0:T(128)} %bitcast.me_ref, f32[64,128]{1,0:T(8,128)S(1)} %add.30.residual_ref.first_ref, f32[64,128]{1,0:T(8,128)S(1)} %add.35.second_ref, f32[64,512]{1,0:T(8,128)S(1)} %get-tuple-element.11.atoms_ref, ...), custom_call_target="tpu_custom_call" | custom-call | tf_op jit(solution)/shard_map/pallas_call | solution.py:196
  (30 shorter events, 0.3 us)
Async XLA Ops:
  0.6 30.5 %copy-start.1 = (f32[64,512]{1,0:T(8,128)S(1)}, f32[64,512]{1,0:T(8,128)}, u32[]{:S(2)}) copy-start(f32[64,512]{1,0:T(8,128)} %atoms_ref.3) | copy-start | bytes 393220
  0.6 30.5 %copy-start.2 = (f32[1,512]{1,0:T(1,128)S(1)}, f32[1,512]{1,0:T(1,128)}, u32[]{:S(2)}) copy-start(f32[1,512]{1,0:T(1,128)} %param.4) | copy-start | bytes 6148
  0.6 30.5 %all-to-all-start = ((bf16[16,64,512]{2,1,0:T(8,128)(2,1)}), bf16[16,64,512]{2,1,0:T(8,128)(2,1)S(1)}, u32[]{:S(2)}, u32[]{:S(2)}) async-start(bf16[16,64,512]{2,1,0:T(8,128)(2,1)} %bitcast.74), calls=%async_computation | async-start | bytes 2097152 | tf_op jit(solution)/shard_map/all_to_all | solution.py:246
  8.2 33.2 %copy-start.3 = (f32[1024]{0:T(1024)S(1)}, f32[1024]{0:T(1024)}, u32[]{:S(2)}) copy-start(f32[1024]{0:T(1024)} %param.7) | copy-start | bytes 12292
  32.6 1.5 %collective-permute-start = (f32[64,128]{1,0:T(8,128)S(1)}, f32[64,128]{1,0:T(8,128)S(1)}, u32[]{:S(2)}, u32[]{:S(2)}) collective-permute-start(f32[64,128]{1,0:T(8,128)S(1)} %shard_map.67), channel_id=1, source_target_pairs={{0,1},{1,0},{2,3},{3,2},{4,5},{5,4},{6,7},{7,6},{8,9},{9,8},{10,11... | collective-permute-start | bytes 98312 | tf_op jit(solution)/shard_map/ppermute | solution.py:208
  34.1 4.9 %collective-permute-start.1 = (f32[64,128]{1,0:T(8,128)S(1)}, f32[64,128]{1,0:T(8,128)S(1)}, u32[]{:S(2)}, u32[]{:S(2)}) collective-permute-start(f32[64,128]{1,0:T(8,128)S(1)} %add.27), channel_id=1, source_target_pairs={{0,2},{1,3},{2,0},{3,1},{4,6},{5,7},{6,4},{7,5},{8,10},{9,11},{10,... | collective-permute-start | bytes 98312 | tf_op jit(solution)/shard_map/ppermute | solution.py:208
  36.1 10.7 %collective-permute-start.8 = (bf16[1,64,512]{2,1,0:T(8,128)(2,1)S(1)}, bf16[1,64,512]{2,1,0:T(8,128)(2,1)S(1)}, u32[]{:S(2)}, u32[]{:S(2)}) collective-permute-start(bf16[1,64,512]{2,1,0:T(8,128)(2,1)S(1)} %convert_bitcast_fusion), channel_id=1, source_target_pairs={{0,8},{1,9},{2,10},{3,11},{4,12},{5,13},{6,14},{7,15},{8,0},{9,1},... | collective-permute-start | bytes 196616 | tf_op jit(solution)/shard_map/ppermute | solution.py:208
  39.0 4.3 %collective-permute-start.2 = (f32[64,128]{1,0:T(8,128)S(1)}, f32[64,128]{1,0:T(8,128)S(1)}, u32[]{:S(2)}, u32[]{:S(2)}) collective-permute-start(f32[64,128]{1,0:T(8,128)S(1)} %add.28), channel_id=1, source_target_pairs={{0,4},{1,5},{2,6},{3,7},{4,0},{5,1},{6,2},{7,3},{8,12},{9,13},{10,... | collective-permute-start | bytes 98312 | tf_op jit(solution)/shard_map/ppermute | solution.py:208
  43.3 5.3 %collective-permute-start.3 = (f32[64,128]{1,0:T(8,128)S(1)}, f32[64,128]{1,0:T(8,128)S(1)}, u32[]{:S(2)}, u32[]{:S(2)}) collective-permute-start(f32[64,128]{1,0:T(8,128)S(1)} %add.29), channel_id=1, source_target_pairs={{0,8},{1,9},{2,10},{3,11},{4,12},{5,13},{6,14},{7,15},{8,0},{9,1},... | collective-permute-start | bytes 98312 | tf_op jit(solution)/shard_map/ppermute | solution.py:208
  58.8 5.3 %collective-permute-start.12 = (bf16[1,64,512]{2,1,0:T(8,128)(2,1)S(1)}, bf16[1,64,512]{2,1,0:T(8,128)(2,1)S(1)}, u32[]{:S(2)}, u32[]{:S(2)}) collective-permute-start(bf16[1,64,512]{2,1,0:T(8,128)(2,1)S(1)} %bitcast.78), channel_id=1, source_target_pairs={{0,8},{1,9},{2,10},{3,11},{4,12},{5,13},{6,14},{7,15},{8,0},{9,1},... | collective-permute-start | bytes 196616 | tf_op jit(solution)/shard_map/ppermute | solution.py:208
  61.8 5.0 %collective-permute-start.9 = (bf16[2,64,512]{2,1,0:T(8,128)(2,1)S(1)}, bf16[2,64,512]{2,1,0:T(8,128)(2,1)S(1)}, u32[]{:S(2)}, u32[]{:S(2)}) collective-permute-start(bf16[2,64,512]{2,1,0:T(8,128)(2,1)S(1)} %maximum_bitcast_fusion), channel_id=1, source_target_pairs={{0,4},{1,5},{2,6},{3,7},{4,0},{5,1},{6,2},{7,3},{8,12},{9,13},{10,... | collective-permute-start | bytes 393224 | tf_op jit(solution)/shard_map/ppermute | solution.py:208
  64.2 5.0 %collective-permute-start.13 = (bf16[2,64,512]{2,1,0:T(8,128)(2,1)S(1)}, bf16[2,64,512]{2,1,0:T(8,128)(2,1)S(1)}, u32[]{:S(2)}, u32[]{:S(2)}) collective-permute-start(bf16[2,64,512]{2,1,0:T(8,128)(2,1)S(1)} %maximum_bitcast_fusion.1), channel_id=1, source_target_pairs={{0,4},{1,5},{2,6},{3,7},{4,0},{5,1},{6,2},{7,3},{8,12},{9,13},{10,... | collective-permute-start | bytes 393224 | tf_op jit(solution)/shard_map/ppermute | solution.py:208
  69.4 8.0 %collective-permute-start.14 = (bf16[4,64,512]{2,1,0:T(8,128)(2,1)S(1)}, bf16[4,64,512]{2,1,0:T(8,128)(2,1)S(1)}, u32[]{:S(2)}, u32[]{:S(2)}) collective-permute-start(bf16[4,64,512]{2,1,0:T(8,128)(2,1)S(1)} %bitcast.84), channel_id=1, source_target_pairs={{0,2},{1,3},{2,0},{3,1},{4,6},{5,7},{6,4},{7,5},{8,10},{9,11},{10,... | collective-permute-start | bytes 786440 | tf_op jit(solution)/shard_map/ppermute | solution.py:208
  71.1 9.1 %collective-permute-start.10 = (bf16[4,64,512]{2,1,0:T(8,128)(2,1)S(1)}, bf16[4,64,512]{2,1,0:T(8,128)(2,1)S(1)}, u32[]{:S(2)}, u32[]{:S(2)}) collective-permute-start(bf16[4,64,512]{2,1,0:T(8,128)(2,1)S(1)} %bitcast.83), channel_id=1, source_target_pairs={{0,2},{1,3},{2,0},{3,1},{4,6},{5,7},{6,4},{7,5},{8,10},{9,11},{10,... | collective-permute-start | bytes 786440 | tf_op jit(solution)/shard_map/ppermute | solution.py:208
  77.5 15.8 %collective-permute-start.15 = (bf16[8,64,512]{2,1,0:T(8,128)(2,1)S(1)}, bf16[8,64,512]{2,1,0:T(8,128)(2,1)}, u32[]{:S(2)}, u32[]{:S(2)}) collective-permute-start(bf16[8,64,512]{2,1,0:T(8,128)(2,1)S(1)} %bitcast.81), channel_id=1, source_target_pairs={{0,1},{1,0},{2,3},{3,2},{4,5},{5,4},{6,7},{7,6},{8,9},{9,8},{10,11... | collective-permute-start | bytes 1572872 | tf_op jit(solution)/shard_map/ppermute | solution.py:208
  77.6 2.8 %collective-permute-start.4 = (f32[64,128]{1,0:T(8,128)S(1)}, f32[64,128]{1,0:T(8,128)S(1)}, u32[]{:S(2)}, u32[]{:S(2)}) collective-permute-start(f32[64,128]{1,0:T(8,128)S(1)} %get-tuple-element.10), channel_id=1, source_target_pairs={{0,1},{1,0},{2,3},{3,2},{4,5},{5,4},{6,7},{7,6},{8,9},{9,8},{10,11... | collective-permute-start | bytes 98312 | tf_op jit(solution)/shard_map/ppermute | solution.py:208
  80.4 14.3 %collective-permute-start.11 = (bf16[8,64,512]{2,1,0:T(8,128)(2,1)S(1)}, bf16[8,64,512]{2,1,0:T(8,128)(2,1)}, u32[]{:S(2)}, u32[]{:S(2)}) collective-permute-start(bf16[8,64,512]{2,1,0:T(8,128)(2,1)S(1)} %bitcast.82), channel_id=1, source_target_pairs={{0,1},{1,0},{2,3},{3,2},{4,5},{5,4},{6,7},{7,6},{8,9},{9,8},{10,11... | collective-permute-start | bytes 1572872 | tf_op jit(solution)/shard_map/ppermute | solution.py:208
  80.5 4.0 %collective-permute-start.5 = (f32[64,128]{1,0:T(8,128)S(1)}, f32[64,128]{1,0:T(8,128)S(1)}, u32[]{:S(2)}, u32[]{:S(2)}) collective-permute-start(f32[64,128]{1,0:T(8,128)S(1)} %add.32), channel_id=1, source_target_pairs={{0,2},{1,3},{2,0},{3,1},{4,6},{5,7},{6,4},{7,5},{8,10},{9,11},{10,... | collective-permute-start | bytes 98312 | tf_op jit(solution)/shard_map/ppermute | solution.py:208
  84.5 3.9 %collective-permute-start.6 = (f32[64,128]{1,0:T(8,128)S(1)}, f32[64,128]{1,0:T(8,128)S(1)}, u32[]{:S(2)}, u32[]{:S(2)}) collective-permute-start(f32[64,128]{1,0:T(8,128)S(1)} %add.33), channel_id=1, source_target_pairs={{0,4},{1,5},{2,6},{3,7},{4,0},{5,1},{6,2},{7,3},{8,12},{9,13},{10,... | collective-permute-start | bytes 98312 | tf_op jit(solution)/shard_map/ppermute | solution.py:208
  88.4 5.0 %collective-permute-start.7 = (f32[64,128]{1,0:T(8,128)S(1)}, f32[64,128]{1,0:T(8,128)S(1)}, u32[]{:S(2)}, u32[]{:S(2)}) collective-permute-start(f32[64,128]{1,0:T(8,128)S(1)} %add.34), channel_id=1, source_target_pairs={{0,8},{1,9},{2,10},{3,11},{4,12},{5,13},{6,14},{7,15},{8,0},{9,1},... | collective-permute-start | bytes 98312 | tf_op jit(solution)/shard_map/ppermute | solution.py:208
  95.9 1.2 %copy-start = (bf16[1,1024,512]{2,1,0:T(8,128)(2,1)S(1)}, bf16[1,1024,512]{2,1,0:T(8,128)(2,1)}, u32[]{:S(2)}) copy-start(bf16[1,1024,512]{2,1,0:T(8,128)(2,1)} %param.5) | copy-start | bytes 3145732
where the time goes:
time: 105 us
  waiting for transfers between devices  49.1 us (47%)
  starting transfers between devices  30.9 us (29%)
  Pallas kernels  19.6 us (19%)
  other arithmetic  2.86 us (3%)
  local copies, waits for them, and re-layouts  1.82 us (2%)
    ppermute x16, waiting for transfers between devices, swapped(): return lax.ppermute(block, 'tm', [(i, i ^ distance) for i in range(count)])  26.1 us
    ppermute x16, starting transfers between devices, swapped(): return lax.ppermute(block, 'tm', [(i, i ^ distance) for i in range(count)])  23.4 us
    all_to_all x1, waiting for transfers between devices, on_device(): lax.all_to_all(codes.reshape(slabs, owned, width), 'tm', 0, 0, tiled=True)  22.9 us
    pallas_call x3, Pallas kernels, call(): pl.pallas_call(kernel, out_shape=outs, in_specs=[pl.BlockSpec(memory_spac...  19.6 us
    all_to_all x1, starting transfers between devices, on_device(): lax.all_to_all(codes.reshape(slabs, owned, width), 'tm', 0, 0, tiled=True)  7.53 us
    another operation x13, other arithmetic, gathered(): block = jnp.stack([low, high], axis=1).reshape(-1, rows, width)  2.78 us
  transfers between devices with their start and end apart: 17, of which 12 were waited for; matrix products, arithmetic and copies ran while one was open for 2% of the time, Pallas kernels for 0%

commit v1 on v0

--- a/solution.py
+++ b/solution.py
@@ -103,34 +103,62 @@
     out_ref[own, :] = out_ref[own, :] + signal_ref[...]
 
 
-def first_kernel(factor, me_ref, atoms_ref, codes_ref, signal_ref, out_ref, turned_ref, sums_ref):
-    slabs, owned, width = codes_ref.shape
-    taps = stacked_taps(atoms_ref[...].astype(BF16))
-    zero = jnp.zeros((owned, width), BF16)
-
-    def slab_of(n):
-        if isinstance(n, int):
-            return codes_ref[n] if n >= 0 else zero
-        return jnp.where(n >= 0, codes_ref[jnp.maximum(n, 0)], zero)
-
-    rebuild(taps, slab_of, slabs, width, turned_ref, sums_ref)
-    partial_residual(me_ref[0], factor, signal_ref, sums_ref, out_ref)
-
-
-def round_rows(residual_ref, rows_ref):
-    count = residual_ref.shape[0]
-    rows_ref[:count, :] = residual_ref[...].astype(BF16).astype(F32)
+def owner_of(me, place, count):
+    distance, bit = count // 2, 0
+    while distance:
+        if place >> bit & 1:
+            me = me ^ distance
+        distance, bit = distance // 2, bit + 1
+    return me
+
+
+def first_kernel(factor, me_ref, near_ref, far_ref, codes_ref, signal_ref, out_ref):
+    half, owned, lag_count = near_ref.shape
+    width = codes_ref.shape[1]
+    per, reach = width // LANES, lag_count // LANES
+    me = me_ref[0]
+    together = max(1, min(half, 256 // owned))
+    lagged = jnp.zeros((lag_count, width), F32)
+    for side, ref in enumerate((near_ref, far_ref)):
+        for start in range(0, half, together):
+            places = range(start, start + together)
+            code = [codes_ref[pl.ds(pl.multiple_of(owner_of(me, side * half + b, 2 * half) * owned, owned), owned), :] for b in places]
+            atoms = [ref[b] for b in places]
+            lagged = lagged + dot(jnp.concatenate(atoms, axis=0), jnp.concatenate(code, axis=0), ((0,), (0,)))
+    q, v = row_lane()
+    keep = v >= q
+    last = jnp.zeros((LANES, LANES), F32)
+    for m in range(per + reach):
+        pieces = [
+            lagged[LANES * p : LANES * (p + 1), LANES * (m - p) : LANES * (m - p + 1)] for p in range(reach) if 0 <= m - p < per
+        ]
+        turned = jnp.zeros((LANES, LANES), F32)
+        if pieces:
+            turned = pltpu.roll(sum(pieces[1:], pieces[0]), 0, 1, stride=1, stride_axis=0)
+        row = -factor * jnp.sum(jnp.where(keep, turned, last), axis=0, keepdims=True)
+        out_ref[m : m + 1, :] = row + signal_ref[m : m + 1, :] if m < per else row
+        last = turned
+
+
+def round_rows(residual_ref, count, rows_ref):
+    rows_ref[:count, :] = residual_ref[:count, :].astype(BF16).astype(F32)
     rows_ref[count:, :] = jnp.zeros((rows_ref.shape[0] - count, LANES), F32)
 
 
 def second_kernel(
-    factor, me_ref, residual_ref, atoms_ref, codes_ref, thresholds_ref, signal_ref,
-    atoms_out, rounded_out, codes_out, part_out,
-    rows_ref, hankel_ref, gradient_ref, turned_ref, sums_ref,
+    factor, me_ref, near_ref, far_ref, atoms_ref, codes_ref, thresholds_ref, signal_ref,
+    atoms_out, taps_out, codes_out, part_out, rows_ref,
+    hankel_ref, gradient_ref, turned_ref, sums_ref,
 ):
     slabs, owned, width = codes_ref.shape
     per = width // LANES
-    round_rows(residual_ref, rows_ref)
+    half, span, _ = near_ref.shape
+    rows_ref[...] = jnp.zeros_like(rows_ref)
+    for side, ref in enumerate((near_ref, far_ref)):
+        for b in range(half):
+            there = pl.ds(owner_of(me_ref[0], side * half + b, slabs) * per, span)
+            rows_ref[there, :] = rows_ref[there, :] + ref[b]
+    round_rows(rows_ref, slabs * per, rows_ref)
     atoms = atoms_ref[...]
     atoms_b = atoms.astype(BF16)
     cutoff = CODE_STEP * thresholds_ref[...]
@@ -151,34 +179,49 @@
     after = normalised(atoms + factor * gradient_ref[...])
     atoms_out[...] = after
     after_b = after.astype(BF16)
-    rounded_out[...] = after_b
-    rebuild(stacked_taps(after_b), lambda n: codes_out[n + 1], slabs, width, turned_ref, sums_ref)
+    taps = stacked_taps(after_b)
+    taps_out[...] = taps
+    rebuild(taps, lambda n: codes_out[n + 1], slabs, width, turned_ref, sums_ref)
     partial_residual(me_ref[0], factor, signal_ref, sums_ref, part_out)
 
 
 def third_kernel(
-    factor, me_ref, first_ref, second_ref, atoms_ref, owned_codes_ref, before_ref, after_ref, codes_ref, thresholds_ref,
+    factor, me_ref, first_ref, second_ref, atoms_ref, owned_codes_ref,
+    near_before_ref, far_before_ref, near_after_ref, far_after_ref, codes_ref, thresholds_ref,
     atoms_out, residual_out, codes_out,
     rows_ref, hankel_ref, gradient_ref, part_rows_ref, part_hankel_ref,
 ):
     slabs, owned, width = owned_codes_ref.shape
     slabs -= 1
-    per = width // LANES
+    per, half = width // LANES, slabs // 2
+    reach = near_before_ref.shape[2] // LANES
     me = me_ref[0]
-    cutoff = CODE_STEP * thresholds_ref[...]
+    round_rows(second_ref, slabs * per, rows_ref)
     frames = []
-    for i, residual in enumerate((first_ref, second_ref)):
-        round_rows(residual, rows_ref)
-        part_rows_ref[: 2 * per, :] = rows_ref[pl.ds(me * per, 2 * per), :]
+    for residual in (first_ref, rows_ref):
+        part_rows_ref[: 2 * per, :] = residual[pl.ds(me * per, 2 * per), :]
         fill_hankel(part_rows_ref, part_hankel_ref, 0, 2 * per - 1)
         frames.append(windows_of(part_hankel_ref, 0, width))
-    step = 256 if codes_ref.shape[0] % 256 == 0 else codes_ref.shape[0]
-    for start in range(0, codes_ref.shape[0], step):
-        own = slice(start, start + step)
-        value = codes_ref[own, :].astype(F32)
-        for atoms_b, frame in ((before_ref, frames[0]), (after_ref, frames[1])):
-            value = soft(value + (CODE_STEP * factor) * dot(atoms_b[own, :], frame, ((1,), (0,))), cutoff[own, :])
-        codes_out[own, :] = value.astype(BF16)
+    together = max(1, min(half, 256 // owned))
+    for side, before, after in ((0, near_before_ref, near_after_ref), (1, far_before_ref, far_after_ref)):
+        for start in range(0, half, together):
+            places = range(start, start + together)
+            there = [pl.ds(pl.multiple_of(owner_of(me, side * half + b, slabs) * owned, owned), owned) for b in places]
+            value = jnp.concatenate([codes_ref[own, :] for own in there], axis=0).astype(F32)
+            cutoff = jnp.concatenate([CODE_STEP * thresholds_ref[own, :] for own in there], axis=0)
+            old = jnp.concatenate([before[b] for b in places], axis=0)
+            new = jnp.concatenate(
+                [
+                    jnp.concatenate([after[(b * reach + p) * owned : (b * reach + p + 1) * owned, :] for p in range(reach)], axis=1)
+                    for b in places
+                ],
+                axis=0,
+            )
+            for atoms_b, frame in ((old, frames[0]), (new, frames[1])):
+                value = soft(value + (CODE_STEP * factor) * dot(atoms_b, frame, ((1,), (0,))), cutoff)
+            value = value.astype(BF16)
+            for i, own in enumerate(there):
+                codes_out[own, :] = value[i * owned : (i + 1) * owned]
     gradient_ref[...] = jnp.zeros_like(gradient_ref)
     fill_hankel(rows_ref, hankel_ref, 0, per - 1)
 
@@ -209,25 +252,30 @@
 
 
 def gathered(block):
-    me = lax.axis_index("tm")
-    rows, width = block.shape
     block = block[None]
     distance = lax.axis_size("tm") // 2
-    while distance:
+    while True:
         other = swapped(block, distance)
-        upper = (me & distance) != 0
-        low, high = jnp.where(upper, other, block), jnp.where(upper, block, other)
-        block = jnp.stack([low, high], axis=1).reshape(-1, rows, width)
+        if distance == 1:
+            return block, other
+        block = jnp.concatenate([block, other])
         distance //= 2
-    return block.reshape(-1, width)
-
-
-def summed(part):
-    distance = 1
-    while distance < lax.axis_size("tm"):
-        part = part + swapped(part, distance)
-        distance *= 2
-    return part
+
+
+def gathered_and_summed(block, part):
+    distance = lax.axis_size("tm") // 2
+    rows = part.shape[0]
+    while True:
+        high = lax.reduce_precision(part, 8, 7)
+        low = lax.reduce_precision(part - high, 8, 7)
+        mine = jnp.concatenate([block, high.astype(BF16), low.astype(BF16)])
+        other = swapped(mine, distance)
+        end = block.shape[0]
+        part = (high + low) + (other[end : end + rows].astype(F32) + other[end + rows :].astype(F32))
+        if distance == 1:
+            return mine, other, part
+        block = jnp.concatenate([block, other[:end]])
+        distance //= 2
 
 
 def on_device(signal, codes, dictionary, thresholds):
@@ -243,31 +291,30 @@
     own_thresholds = lax.dynamic_slice(thresholds, (me * owned,), (owned,)).reshape(owned, 1)
     codes = codes[0]
 
+    near_before, far_before = gathered(dictionary.astype(BF16))
     by_atom = lax.all_to_all(codes.reshape(slabs, owned, width), "tm", 0, 0, tiled=True)
-    before = gathered(dictionary.astype(BF16))
-
-    sums = [pltpu.VMEM((LANES, LANES), F32), pltpu.VMEM((blocks, 8, LANES), F32)]
-    rows = [
-        pltpu.VMEM((blocks + 8, LANES), F32),
-        pltpu.VMEM((blocks + per - 1, LANES, LANES), BF16),
-        pltpu.VMEM((owned, lag_count), F32),
-    ]
-    residual_shape = jax.ShapeDtypeStruct((blocks, LANES), F32)
-    part = call(functools.partial(first_kernel, factor), residual_shape, sums, at, dictionary, by_atom, signal_rows)
-    first = summed(part)
-    atoms, after, next_codes, part = call(
+
+    part = call(
+        functools.partial(first_kernel, factor),
+        jax.ShapeDtypeStruct((per + lag_count // LANES, LANES), F32),
+        [],
+        at, near_before, far_before, codes, signal_rows,
+    )
+    near, far = gathered(part)
+    hankel = [pltpu.VMEM((blocks + per - 1, LANES, LANES), BF16), pltpu.VMEM((owned, lag_count), F32)]
+    atoms, taps, next_codes, part, first = call(
         functools.partial(second_kernel, factor),
         (
             jax.ShapeDtypeStruct((owned, lag_count), F32),
-            jax.ShapeDtypeStruct((owned, lag_count), BF16),
+            jax.ShapeDtypeStruct((owned * lag_count // LANES, LANES), BF16),
             jax.ShapeDtypeStruct((slabs + 1, owned, width), BF16),
-            residual_shape,
+            jax.ShapeDtypeStruct((blocks, LANES), F32),
+            jax.ShapeDtypeStruct((blocks + 8, LANES), F32),
         ),
-        rows + sums,
-        at, first, dictionary, by_atom, own_thresholds, signal_rows,
+        hankel + [pltpu.VMEM((LANES, LANES), F32), pltpu.VMEM((blocks, 8, LANES), F32)],
+        at, near, far, dictionary, by_atom, own_thresholds, signal_rows,
     )
-    second = summed(part)
-    after = gathered(after)
+    near_after, far_after, second = gathered_and_summed(taps, part)
     atoms, residual, codes = call(
         functools.partial(third_kernel, factor),
         (
@@ -275,8 +322,11 @@
             jax.ShapeDtypeStruct((per, LANES), F32),
             jax.ShapeDtypeStruct((atom_count, width), BF16),
         ),
-        rows + [pltpu.VMEM((2 * per, LANES), F32), pltpu.VMEM((2 * per - 1, LANES, LANES), BF16)],
-        at, first, second, atoms, next_codes, before, after, codes, thresholds.reshape(atom_count, 1),
+        [pltpu.VMEM((blocks + 8, LANES), F32)]
+        + hankel
+        + [pltpu.VMEM((2 * per, LANES), F32), pltpu.VMEM((2 * per - 1, LANES, LANES), BF16)],
+        at, first, second, atoms, next_codes,
+        near_before, far_before, near_after, far_after, codes, thresholds.reshape(atom_count, 1),
     )
     return codes[None], atoms, residual.reshape(1, width)
 

time: 105 us -> 115 us (1.095)
  waiting for transfers between devices: 49.1 us -> 70.4 us
  starting transfers between devices: 30.9 us -> 17.1 us
  local copies, waits for them, and re-layouts: 1.82 us -> 4.34 us
    ppermute x16 -> x12, waiting for transfers between devices: 26.1 us -> 70.4 us  [swapped(): return lax.ppermute(block, 'tm', [(i, i ^ distance) for i in range(count)])]
    all_to_all x1, waiting for transfers between devices: 22.9 us -> 0.01 us  [on_device(): lax.all_to_all(codes.reshape(slabs, owned, width), 'tm', 0, 0, tiled=True)]
    ppermute x16 -> x12, starting transfers between devices: 23.4 us -> 9.55 us  [swapped(): return lax.ppermute(block, 'tm', [(i, i ^ distance) for i in range(count)])]
    unnamed x8 -> x16, local copies, waits for them, and re-layouts: 1.14 us -> 3.94 us
    another operation x13 -> x0, other arithmetic: 2.78 us -> none  [gathered(): block = jnp.stack([low, high], axis=1).reshape(-1, rows, width)]
  transfers between devices with their start and end apart: 17 -> 13, of which waited for: 12 -> 12; matrix products, arithmetic and copies ran while one was open for 2% -> 1% of each run, Pallas kernels for 0% -> 1%
where the time goes in v1:
time: 115 us
  waiting for transfers between devices  70.4 us (61%)
  Pallas kernels  20 us (17%)
  starting transfers between devices  17.1 us (15%)
  local copies, waits for them, and re-layouts  4.34 us (4%)
  other arithmetic  2.21 us (2%)
    ppermute x12, waiting for transfers between devices, swapped(): return lax.ppermute(block, 'tm', [(i, i ^ distance) for i in range(count)])  70.4 us
    pallas_call x3, Pallas kernels, call(): pl.pallas_call(kernel, out_shape=outs, in_specs=[pl.BlockSpec(memory_spac...  20 us
    ppermute x12, starting transfers between devices, swapped(): return lax.ppermute(block, 'tm', [(i, i ^ distance) for i in range(count)])  9.55 us
    all_to_all x1, starting transfers between devices, on_device(): lax.all_to_all(codes.reshape(slabs, owned, width), 'tm', 0, 0, tiled=True)  7.53 us
    unnamed x16, local copies, waits for them, and re-layouts  3.94 us
  transfers between devices with their start and end apart: 13, of which 12 were waited for; matrix products, arithmetic and copies ran while one was open for 1% of the time, Pallas kernels for 1%

profile of v1, /device:TPU:0, one launch (start us, length us, event | category | flops | bytes accessed | tf_op | source)
XLA Modules:
  0.0 114.9 jit_solution(16846098250776910099)
XLA Ops:
  0.6 0.0 copy-start.3
  0.6 7.5 %all-to-all-start = ((bf16[16,64,512]{2,1,0:T(8,128)(2,1)}), bf16[16,64,512]{2,1,0:T(8,128)(2,1)S(1)}, u32[]{:S(2)}, u32[]{:S(2)}) async-start(bf16[16,64,512]{2,1,0:T(8,128)(2,1)} %bitcast.12), calls=%async_computation | async-start | bytes 2097152 | tf_op jit(solution)/shard_map/all_to_all | solution.py:295
  8.2 0.0 copy-done.3
  8.2 0.0 copy-start
  8.2 0.0 copy-start.4
  8.2 2.9 %collective-permute-start = (bf16[1,64,512]{2,1,0:T(8,128)(2,1)S(1)}, bf16[1,64,512]{2,1,0:T(8,128)(2,1)S(1)}, u32[]{:S(2)}, u32[]{:S(2)}) collective-permute-start(bf16[1,64,512]{2,1,0:T(8,128)(2,1)S(1)} %convert_bitcast_fusion), channel_id=1, source_target_pairs={{0,8},{1,9},{2,10},{3,11},{4,12},{5,13},{6,14},{7,15},{8,0},{9,1},... | collective-permute-start | bytes 196616 | tf_op jit(solution)/shard_map/ppermute | solution.py:251
  11.1 26.4 %collective-permute-done = bf16[1,64,512]{2,1,0:T(8,128)(2,1)S(1)} collective-permute-done((bf16[1,64,512]{2,1,0:T(8,128)(2,1)S(1)}, bf16[1,64,512]{2,1,0:T(8,128)(2,1)S(1)}, u32[]{:S(2)}, u32[]{:S(2)}) %collective-permute-start) | collective-permute-done | bytes 65568 | tf_op jit(solution)/shard_map/ppermute | solution.py:251
  37.6 0.1 collective-permute-start.1
  37.6 5.0 %collective-permute-done.1 = bf16[2,64,512]{2,1,0:T(8,128)(2,1)S(1)} collective-permute-done((bf16[2,64,512]{2,1,0:T(8,128)(2,1)S(1)}, bf16[2,64,512]{2,1,0:T(8,128)(2,1)S(1)}, u32[]{:S(2)}, u32[]{:S(2)}) %collective-permute-start.1) | collective-permute-done | bytes 131104 | tf_op jit(solution)/shard_map/ppermute | solution.py:251
  42.7 1.5 %collective-permute-start.2 = (bf16[4,64,512]{2,1,0:T(8,128)(2,1)S(1)}, bf16[4,64,512]{2,1,0:T(8,128)(2,1)S(1)}, u32[]{:S(2)}, u32[]{:S(2)}) collective-permute-start(bf16[4,64,512]{2,1,0:T(8,128)(2,1)S(1)} %pad_maximum_fusion.1), channel_id=1, source_target_pairs={{0,2},{1,3},{2,0},{3,1},{4,6},{5,7},{6,4},{7,5},{8,10},{9,11},{10,... | collective-permute-start | bytes 786440 | tf_op jit(solution)/shard_map/ppermute | solution.py:251
  44.2 5.5 %collective-permute-done.2 = bf16[4,64,512]{2,1,0:T(8,128)(2,1)S(1)} collective-permute-done((bf16[4,64,512]{2,1,0:T(8,128)(2,1)S(1)}, bf16[4,64,512]{2,1,0:T(8,128)(2,1)S(1)}, u32[]{:S(2)}, u32[]{:S(2)}) %collective-permute-start.2) | collective-permute-done | bytes 262176 | tf_op jit(solution)/shard_map/ppermute | solution.py:251
  49.7 0.1 pad_maximum_fusion.near_ref.near_before_ref
  49.8 0.1 collective-permute-start.3
  49.8 1.9 %collective-permute-done.3.far_ref.far_before_ref = bf16[8,64,512]{2,1,0:T(8,128)(2,1)S(1)} collective-permute-done((bf16[8,64,512]{2,1,0:T(8,128)(2,1)S(1)}, bf16[8,64,512]{2,1,0:T(8,128)(2,1)S(1)}, u32[]{:S(2)}, u32[]{:S(2)}) %collective-permute-start.3) | collective-permute-done | bytes 524320 | tf_op jit(solution)/shard_map/ppermute | solution.py:251
  51.7 0.0 copy-done
  51.7 0.0 copy-done.4
  51.7 0.9 shard_map.67
  52.6 0.7 collective-permute-start.4
  53.3 3.9 %collective-permute-done.4 = f32[1,8,128]{2,1,0:T(8,128)S(1)} collective-permute-done((f32[1,8,128]{2,1,0:T(8,128)S(1)}, f32[1,8,128]{2,1,0:T(8,128)S(1)}, u32[]{:S(2)}, u32[]{:S(2)}) %collective-permute-start.4) | collective-permute-done | bytes 4128 | tf_op jit(solution)/shard_map/ppermute | solution.py:251
  57.2 0.6 collective-permute-start.5
  57.8 3.1 %collective-permute-done.5 = f32[2,8,128]{2,1,0:T(8,128)S(1)} collective-permute-done((f32[2,8,128]{2,1,0:T(8,128)S(1)}, f32[2,8,128]{2,1,0:T(8,128)S(1)}, u32[]{:S(2)}, u32[]{:S(2)}) %collective-permute-start.5) | collective-permute-done | bytes 8224 | tf_op jit(solution)/shard_map/ppermute | solution.py:251
  60.8 1.5 %collective-permute-start.6 = (f32[4,8,128]{2,1,0:T(8,128)S(1)}, f32[4,8,128]{2,1,0:T(8,128)S(1)}, u32[]{:S(2)}, u32[]{:S(2)}) collective-permute-start(f32[4,8,128]{2,1,0:T(8,128)S(1)} %pad_maximum_fusion.6), channel_id=1, source_target_pairs={{0,2},{1,3},{2,0},{3,1},{4,6},{5,7},{6,4},{7,5},{8,10},{9,11},{10,... | collective-permute-start | bytes 49160 | tf_op jit(solution)/shard_map/ppermute | solution.py:251
  62.3 2.3 %collective-permute-done.6 = f32[4,8,128]{2,1,0:T(8,128)S(1)} collective-permute-done((f32[4,8,128]{2,1,0:T(8,128)S(1)}, f32[4,8,128]{2,1,0:T(8,128)S(1)}, u32[]{:S(2)}, u32[]{:S(2)}) %collective-permute-start.6) | collective-permute-done | bytes 16416 | tf_op jit(solution)/shard_map/ppermute | solution.py:251
  64.6 0.0 collective-permute-start.7
  64.6 0.0 copy-done.5
  64.6 0.1 dynamic-slice_bitcast_fusion
  64.7 0.1 copy.8.thresholds_ref
  64.8 1.0 collective-permute-done.7.far_ref
  65.8 0.0 all-to-all-done.codes_ref
  65.8 9.9 %shard_map.68 = (f32[64,512]{1,0:T(8,128)S(1)}, bf16[256,128]{1,0:T(8,128)(2,1)S(1)}, bf16[17,64,512]{2,1,0:T(8,128)(2,1)S(1)}, f32[64,128]{1,0:T(8,128)S(1)}, f32[72,128]{1,0:T(8,128)S(1)}) custom-call(s32[1]{0:T(128)} %bitcast.me_ref, f32[8,8,128]{2,1,0:T(8,128)S(1)} %pad_maximum_fusion.5.near_ref, f32[8,8,128]{2,1,0:T(8,128)S(1)} %collective-permute-done.7.far_ref, ...), custom_call_target="tpu_custom_call" | custom-call | tf_op jit(solution)/shard_map/pallas_call | solution.py:239
  75.8 0.7 collective-permute-start.8
  76.4 0.6 constant_dynamic-update-slice_fusion.3
  77.1 6.6 %collective-permute-done.8 = bf16[384,128]{1,0:T(8,128)(2,1)S(1)} collective-permute-done((bf16[384,128]{1,0:T(8,128)(2,1)S(1)}, bf16[384,128]{1,0:T(8,128)(2,1)S(1)}, u32[]{:S(2)}, u32[]{:S(2)}) %collective-permute-start.8) | collective-permute-done | bytes 98336 | tf_op jit(solution)/shard_map/ppermute | solution.py:251
  83.7 0.6 constant_dynamic-update-slice_fusion.2
  84.4 0.1 collective-permute-start.9
  84.5 6.1 %collective-permute-done.9 = bf16[640,128]{1,0:T(8,128)(2,1)S(1)} collective-permute-done((bf16[640,128]{1,0:T(8,128)(2,1)S(1)}, bf16[640,128]{1,0:T(8,128)(2,1)S(1)}, u32[]{:S(2)}, u32[]{:S(2)}) %collective-permute-start.9) | collective-permute-done | bytes 163872 | tf_op jit(solution)/shard_map/ppermute | solution.py:251
  90.5 0.7 slice_dynamic-update-slice_fusion.2
  91.3 1.5 %collective-permute-start.10 = (bf16[1152,128]{1,0:T(8,128)(2,1)S(1)}, bf16[1152,128]{1,0:T(8,128)(2,1)S(1)}, u32[]{:S(2)}, u32[]{:S(2)}) collective-permute-start(bf16[1152,128]{1,0:T(8,128)(2,1)S(1)} %constant_dynamic-update-slice_fusion), channel_id=1, source_target_pairs={{0,2},{1,3},{2,0},{3,1},{4,6},{5,7},{6,4},{7,5},{8,10},{9,11},{10,... | collective-permute-start | bytes 884744 | tf_op jit(solution)/shard_map/ppermute | solution.py:251
  92.8 6.6 %collective-permute-done.10 = bf16[1152,128]{1,0:T(8,128)(2,1)S(1)} collective-permute-done((bf16[1152,128]{1,0:T(8,128)(2,1)S(1)}, bf16[1152,128]{1,0:T(8,128)(2,1)S(1)}, u32[]{:S(2)}, u32[]{:S(2)}) %collective-permute-start.10) | collective-permute-done | bytes 294944 | tf_op jit(solution)/shard_map/ppermute | solution.py:251
  99.4 0.7 slice_dynamic-update-slice_fusion
  100.1 0.6 constant_dynamic-update-slice_fusion.5
  100.7 0.6 constant_dynamic-update-slice_fusion.4.near_after_ref
  101.4 0.0 collective-permute-start.11
  101.4 0.2 copy.9.thresholds_ref
  101.6 2.1 %collective-permute-done.11.far_after_ref = bf16[2176,128]{1,0:T(8,128)(2,1)} collective-permute-done((bf16[2176,128]{1,0:T(8,128)(2,1)}, bf16[2176,128]{1,0:T(8,128)(2,1)}, u32[]{:S(2)}, u32[]{:S(2)}) %collective-permute-start.11) | collective-permute-done | bytes 557088 | tf_op jit(solution)/shard_map/ppermute | solution.py:251
  103.7 0.8 fusion.11.second_ref
  104.4 1.2 %copy-done.2 = bf16[17,64,512]{2,1,0:T(8,128)(2,1)S(1)} copy-done((bf16[17,64,512]{2,1,0:T(8,128)(2,1)S(1)}, bf16[17,64,512]{2,1,0:T(8,128)(2,1)}, u32[]{:S(2)}) %copy-start.2) | copy-done | bytes 1114136
  105.7 9.3 %shard_map.69 = (f32[64,512]{1,0:T(8,128)}, f32[4,128]{1,0:T(4,128)}, bf16[1024,512]{1,0:T(8,128)(2,1)}) custom-call(s32[1]{0:T(128)} %bitcast.me_ref, f32[72,128]{1,0:T(8,128)S(1)} %get-tuple-element.11.first_ref, f32[64,128]{1,0:T(8,128)S(1)} %fusion.11.second_ref, f32[64,512]{1,0:T(8,128)S(1)} %get-tuple-element.14.atoms_ref, ...), custom_call_target="tpu_custom_call" | custom-call | tf_op jit(solution)/shard_map/pallas_call | solution.py:239
  (16 shorter events, 0.2 us)
Async XLA Ops:
  0.6 7.5 %copy-start.3 = (f32[64,512]{1,0:T(8,128)S(1)}, f32[64,512]{1,0:T(8,128)}, u32[]{:S(2)}) copy-start(f32[64,512]{1,0:T(8,128)} %atoms_ref.1) | copy-start | bytes 393220
  0.6 65.2 %all-to-all-start = ((bf16[16,64,512]{2,1,0:T(8,128)(2,1)}), bf16[16,64,512]{2,1,0:T(8,128)(2,1)S(1)}, u32[]{:S(2)}, u32[]{:S(2)}) async-start(bf16[16,64,512]{2,1,0:T(8,128)(2,1)} %bitcast.12), calls=%async_computation | async-start | bytes 2097152 | tf_op jit(solution)/shard_map/all_to_all | solution.py:295
  8.2 43.6 %copy-start = (bf16[1,1024,512]{2,1,0:T(8,128)(2,1)S(1)}, bf16[1,1024,512]{2,1,0:T(8,128)(2,1)}, u32[]{:S(2)}) copy-start(bf16[1,1024,512]{2,1,0:T(8,128)(2,1)} %param.5) | copy-start | bytes 3145732
  8.2 43.5 %copy-start.4 = (f32[1,512]{1,0:T(1,128)S(1)}, f32[1,512]{1,0:T(1,128)}, u32[]{:S(2)}) copy-start(f32[1,512]{1,0:T(1,128)} %param.4) | copy-start | bytes 6148
  8.2 29.3 %collective-permute-start = (bf16[1,64,512]{2,1,0:T(8,128)(2,1)S(1)}, bf16[1,64,512]{2,1,0:T(8,128)(2,1)S(1)}, u32[]{:S(2)}, u32[]{:S(2)}) collective-permute-start(bf16[1,64,512]{2,1,0:T(8,128)(2,1)S(1)} %convert_bitcast_fusion), channel_id=1, source_target_pairs={{0,8},{1,9},{2,10},{3,11},{4,12},{5,13},{6,14},{7,15},{8,0},{9,1},... | collective-permute-start | bytes 196616 | tf_op jit(solution)/shard_map/ppermute | solution.py:251
  37.6 5.1 %collective-permute-start.1 = (bf16[2,64,512]{2,1,0:T(8,128)(2,1)S(1)}, bf16[2,64,512]{2,1,0:T(8,128)(2,1)S(1)}, u32[]{:S(2)}, u32[]{:S(2)}) collective-permute-start(bf16[2,64,512]{2,1,0:T(8,128)(2,1)S(1)} %pad_maximum_fusion.3), channel_id=1, source_target_pairs={{0,4},{1,5},{2,6},{3,7},{4,0},{5,1},{6,2},{7,3},{8,12},{9,13},{10,... | collective-permute-start | bytes 393224 | tf_op jit(solution)/shard_map/ppermute | solution.py:251
  42.7 7.0 %collective-permute-start.2 = (bf16[4,64,512]{2,1,0:T(8,128)(2,1)S(1)}, bf16[4,64,512]{2,1,0:T(8,128)(2,1)S(1)}, u32[]{:S(2)}, u32[]{:S(2)}) collective-permute-start(bf16[4,64,512]{2,1,0:T(8,128)(2,1)S(1)} %pad_maximum_fusion.1), channel_id=1, source_target_pairs={{0,2},{1,3},{2,0},{3,1},{4,6},{5,7},{6,4},{7,5},{8,10},{9,11},{10,... | collective-permute-start | bytes 786440 | tf_op jit(solution)/shard_map/ppermute | solution.py:251
  49.8 2.0 %collective-permute-start.3 = (bf16[8,64,512]{2,1,0:T(8,128)(2,1)S(1)}, bf16[8,64,512]{2,1,0:T(8,128)(2,1)S(1)}, u32[]{:S(2)}, u32[]{:S(2)}) collective-permute-start(bf16[8,64,512]{2,1,0:T(8,128)(2,1)S(1)} %pad_maximum_fusion.near_ref.near_before_ref), channel_id=1, source_target_pairs={{0,1},{1,0},{2,3},{3,2},{4,5},{5,4},{6,7},{7,6},{8,9},{9,8},{10,11... | collective-permute-start | bytes 1572872 | tf_op jit(solution)/shard_map/ppermute | solution.py:251
  51.7 12.8 %copy-start.5 = (f32[1024]{0:T(1024)S(1)}, f32[1024]{0:T(1024)}, u32[]{:S(2)}) copy-start(f32[1024]{0:T(1024)} %param.7) | copy-start | bytes 12292
  52.6 4.6 %collective-permute-start.4 = (f32[1,8,128]{2,1,0:T(8,128)S(1)}, f32[1,8,128]{2,1,0:T(8,128)S(1)}, u32[]{:S(2)}, u32[]{:S(2)}) collective-permute-start(f32[1,8,128]{2,1,0:T(8,128)S(1)} %bitcast.15), channel_id=1, source_target_pairs={{0,8},{1,9},{2,10},{3,11},{4,12},{5,13},{6,14},{7,15},{8,0},{9,1},... | collective-permute-start | bytes 12296 | tf_op jit(solution)/shard_map/ppermute | solution.py:251
  57.2 3.7 %collective-permute-start.5 = (f32[2,8,128]{2,1,0:T(8,128)S(1)}, f32[2,8,128]{2,1,0:T(8,128)S(1)}, u32[]{:S(2)}, u32[]{:S(2)}) collective-permute-start(f32[2,8,128]{2,1,0:T(8,128)S(1)} %pad_maximum_fusion.7), channel_id=1, source_target_pairs={{0,4},{1,5},{2,6},{3,7},{4,0},{5,1},{6,2},{7,3},{8,12},{9,13},{10,... | collective-permute-start | bytes 24584 | tf_op jit(solution)/shard_map/ppermute | solution.py:251
  60.8 3.7 %collective-permute-start.6 = (f32[4,8,128]{2,1,0:T(8,128)S(1)}, f32[4,8,128]{2,1,0:T(8,128)S(1)}, u32[]{:S(2)}, u32[]{:S(2)}) collective-permute-start(f32[4,8,128]{2,1,0:T(8,128)S(1)} %pad_maximum_fusion.6), channel_id=1, source_target_pairs={{0,2},{1,3},{2,0},{3,1},{4,6},{5,7},{6,4},{7,5},{8,10},{9,11},{10,... | collective-permute-start | bytes 49160 | tf_op jit(solution)/shard_map/ppermute | solution.py:251
  64.6 1.2 %collective-permute-start.7 = (f32[8,8,128]{2,1,0:T(8,128)S(1)}, f32[8,8,128]{2,1,0:T(8,128)S(1)}, u32[]{:S(2)}, u32[]{:S(2)}) collective-permute-start(f32[8,8,128]{2,1,0:T(8,128)S(1)} %pad_maximum_fusion.5.near_ref), channel_id=1, source_target_pairs={{0,1},{1,0},{2,3},{3,2},{4,5},{5,4},{6,7},{7,6},{8,9},{9,8},{10,11... | collective-permute-start | bytes 98312 | tf_op jit(solution)/shard_map/ppermute | solution.py:251
  75.7 24.4 %copy-start.1 = (bf16[17,64,512]{2,1,0:T(8,128)(2,1)}, bf16[17,64,512]{2,1,0:T(8,128)(2,1)S(1)}, u32[]{:S(2)}) copy-start(bf16[17,64,512]{2,1,0:T(8,128)(2,1)S(1)} %get-tuple-element.15.owned_codes_ref) | copy-start | bytes 3342340
  75.8 7.9 %collective-permute-start.8 = (bf16[384,128]{1,0:T(8,128)(2,1)S(1)}, bf16[384,128]{1,0:T(8,128)(2,1)S(1)}, u32[]{:S(2)}, u32[]{:S(2)}) collective-permute-start(bf16[384,128]{1,0:T(8,128)(2,1)S(1)} %pad_maximum_fusion.4), channel_id=1, source_target_pairs={{0,8},{1,9},{2,10},{3,11},{4,12},{5,13},{6,14},{7,15},{8,0},{9,1},... | collective-permute-start | bytes 294920 | tf_op jit(solution)/shard_map/ppermute | solution.py:251
  84.4 6.2 %collective-permute-start.9 = (bf16[640,128]{1,0:T(8,128)(2,1)S(1)}, bf16[640,128]{1,0:T(8,128)(2,1)S(1)}, u32[]{:S(2)}, u32[]{:S(2)}) collective-permute-start(bf16[640,128]{1,0:T(8,128)(2,1)S(1)} %pad_maximum_fusion.2), channel_id=1, source_target_pairs={{0,4},{1,5},{2,6},{3,7},{4,0},{5,1},{6,2},{7,3},{8,12},{9,13},{10,... | collective-permute-start | bytes 491528 | tf_op jit(solution)/shard_map/ppermute | solution.py:251
  91.3 8.1 %collective-permute-start.10 = (bf16[1152,128]{1,0:T(8,128)(2,1)S(1)}, bf16[1152,128]{1,0:T(8,128)(2,1)S(1)}, u32[]{:S(2)}, u32[]{:S(2)}) collective-permute-start(bf16[1152,128]{1,0:T(8,128)(2,1)S(1)} %constant_dynamic-update-slice_fusion), channel_id=1, source_target_pairs={{0,2},{1,3},{2,0},{3,1},{4,6},{5,7},{6,4},{7,5},{8,10},{9,11},{10,... | collective-permute-start | bytes 884744 | tf_op jit(solution)/shard_map/ppermute | solution.py:251
  101.4 2.3 %collective-permute-start.11 = (bf16[2176,128]{1,0:T(8,128)(2,1)}, bf16[2176,128]{1,0:T(8,128)(2,1)}, u32[]{:S(2)}, u32[]{:S(2)}) collective-permute-start(bf16[2176,128]{1,0:T(8,128)(2,1)} %constant_dynamic-update-slice_fusion.4.near_after_ref), channel_id=1, source_target_pairs={{0,1},{1,0},{2,3},{3,2},{4,5},{5,4},{6,7},{7,6},{8,9},{9,8},{10,11... | collective-permute-start | bytes 1671176 | tf_op jit(solution)/shard_map/ppermute | solution.py:251
  104.4 1.2 %copy-start.2 = (bf16[17,64,512]{2,1,0:T(8,128)(2,1)S(1)}, bf16[17,64,512]{2,1,0:T(8,128)(2,1)}, u32[]{:S(2)}) copy-start(bf16[17,64,512]{2,1,0:T(8,128)(2,1)} %copy-done.1) | copy-start | bytes 3342340

commit v2 on v0

v2 whole, which is shorter than its diff:
```python
import functools

import jax
import jax.numpy as jnp
from jax import lax
from jax.experimental import pallas as pl
from jax.experimental.pallas import tpu as pltpu
from jax.sharding import PartitionSpec as P

CODE_STEP = 6.0
EPSILON = 1e-06
LANES = 128
F32, BF16 = jnp.float32, jnp.bfloat16
VMEM_BYTES = 48 * 1024 * 1024


def dot(a, b, dims):
    return lax.dot_general(a, b, (dims, ((), ())), preferred_element_type=F32)


def repeat(count, body, carry=None):
    def step(i, carry):
        return body(i) if carry is None else body(i, carry)

    if count > 80:
        return lax.fori_loop(0, count, step, carry)
    for i in range(count):
        carry = step(i, carry)
    return carry


def row_lane():
    shape = (LANES, LANES)
    return lax.broadcasted_iota(jnp.int32, shape, 0), lax.broadcasted_iota(jnp.int32, shape, 1)


def fill_hankel(rows_ref, turned_ref, hankel_ref):
    count = hankel_ref.shape[0]
    q = lax.broadcasted_iota(jnp.int32, (8, LANES), 0)
    v = lax.broadcasted_iota(jnp.int32, (8, LANES), 1)

    def turn(m):
        group = jnp.broadcast_to(rows_ref[pl.ds(m, 1), :], (8, LANES))
        for bit in (1, 2, 4):
            group = jnp.where((q & bit) != 0, pltpu.roll(group, LANES - bit, 1), group)
        turned_ref[m] = group

    repeat(count + 1, turn)
    for a in range(0, LANES, 16):
        keeps = [q + v + (a + b) < LANES for b in (0, 8)]

        def groups(m):
            group = turned_ref[m]
            return tuple(pltpu.roll(group, LANES - a - b, 1) if a + b else group for b in (0, 8))

        def place(m, here):
            after = groups(m + 1)
            pair = [jnp.where(keep, old, new) for keep, old, new in zip(keeps, here, after)]
            hankel_ref[m, a : a + 16, :] = jnp.concatenate(pair, axis=0).astype(BF16)
            return after

        repeat(count, place, groups(0))


def windows_of(hankel_ref, slab, width):
    per = width // LANES
    rows = [
        jnp.concatenate([hankel_ref[slab * per + p + i] for i in range(per)], axis=1)
        for p in range(per)
    ]
    return jnp.concatenate(rows, axis=0)


def soft(value, cutoff):
    return value - jnp.minimum(jnp.maximum(value, -cutoff), cutoff)


def normalised(updated):
    return updated / jnp.sqrt(jnp.mean(updated * updated, axis=1, keepdims=True) + EPSILON)


def stacked_taps(atoms):
    return jnp.concatenate([atoms[:, i : i + LANES] for i in range(0, atoms.shape[1], LANES)], axis=0)


def rebuild(taps, slab_of, slabs, width, turned_ref, sums_ref):
    per = width // LANES
    q, v = row_lane()
    keep = v >= q
    turned_ref[...] = jnp.zeros_like(turned_ref)

    def body(n):
        now, before = slab_of(n), slab_of(n - 1)
        shifted = [now] + [
            jnp.concatenate([before[:, width - LANES * p :], now[:, : width - LANES * p]], axis=1) for p in range(1, per)
        ]
        products = dot(taps, jnp.concatenate(shifted, axis=0), ((0,), (0,)))
        last = turned_ref[...]
        for i in range(per):
            turned = pltpu.roll(products[:, LANES * i : LANES * (i + 1)], 0, 1, stride=1, stride_axis=0)
            placed = jnp.where(keep, turned, last)
            sums_ref[n * per + i] = placed.reshape(LANES // 8, 8, LANES).sum(axis=0)
            last = turned
        turned_ref[...] = last

    repeat(slabs, body)


def partial_residual(me, factor, signal_ref, sums_ref, out_ref):
    rows = signal_ref.shape[0]
    out_ref[...] = -factor * jnp.sum(sums_ref[...], axis=1)
    own = pl.ds(me * rows, rows)
    out_ref[own, :] = out_ref[own, :] + signal_ref[...]


def owner_of(me, place, count):
    distance, bit = count // 2, 0
    while distance:
        if place >> bit & 1:
            me = me ^ distance
        distance, bit = distance // 2, bit + 1
    return me


def first_kernel(factor, me_ref, atoms_ref, codes_ref, signal_ref, taps_out, part_out, turned_ref, sums_ref):
    slabs, owned, width = codes_ref.shape
    taps = stacked_taps(atoms_ref[...].astype(BF16))
    taps_out[...] = taps
    zero = jnp.zeros((owned, width), BF16)

    def slab_of(n):
        if isinstance(n, int):
            return codes_ref[n] if n >= 0 else zero
        return jnp.where(n >= 0, codes_ref[jnp.maximum(n, 0)], zero)

    rebuild(taps, slab_of, slabs, width, turned_ref, sums_ref)
    partial_residual(me_ref[0], factor, signal_ref, sums_ref, part_out)


def round_rows(residual_ref, rows_ref):
    count = residual_ref.shape[0]
    rows_ref[:count, :] = residual_ref[...].astype(BF16).astype(F32)
    rows_ref[count:, :] = jnp.zeros((rows_ref.shape[0] - count, LANES), F32)


def second_kernel(
    factor, me_ref, residual_ref, atoms_ref, codes_ref, thresholds_ref, signal_ref,
    atoms_out, taps_out, codes_out, part_out, frames_out,
    rows_ref, turned_rows_ref, hankel_ref, gradient_ref, turned_ref, sums_ref,
):
    slabs, owned, width = codes_ref.shape
    per = width // LANES
    round_rows(residual_ref, rows_ref)
    fill_hankel(rows_ref, turned_rows_ref, hankel_ref)
    frames_out[...] = hankel_ref[pl.ds(me_ref[0] * per, 2 * per - 1)]
    atoms = atoms_ref[...]
    atoms_b = atoms.astype(BF16)
    cutoff = CODE_STEP * thresholds_ref[...]
    gradient_ref[...] = jnp.zeros_like(gradient_ref)
    codes_out[0] = jnp.zeros((owned, width), BF16)

    def body(n):
        frames = windows_of(hankel_ref, n, width)
        code = codes_ref[n]
        both = dot(jnp.concatenate([atoms_b, code], axis=0), frames, ((1,), (0,)))
        gradient_ref[...] += both[owned:]
        value = code.astype(F32) + (CODE_STEP * factor) * both[:owned]
        codes_out[n + 1] = soft(value, cutoff).astype(BF16)

    repeat(slabs, body)
    after = normalised(atoms + factor * gradient_ref[...])
    atoms_out[...] = after
    after_b = after.astype(BF16)
    taps = stacked_taps(after_b)
    taps_out[...] = taps
    rebuild(taps, lambda n: codes_out[n + 1], slabs, width, turned_ref, sums_ref)
    partial_residual(me_ref[0], factor, signal_ref, sums_ref, part_out)


def third_kernel(
    factor, buffers, me_ref, frames_ref, residual_ref, atoms_ref, owned_codes_ref, codes_ref, thresholds_ref, *refs
):
    before_refs, after_refs = refs[:buffers], refs[buffers : 2 * buffers]
    atoms_out, residual_out, codes_out, rows_ref, turned_rows_ref, hankel_ref, gradient_ref = refs[2 * buffers :]
    slabs, owned, width = owned_codes_ref.shape
    slabs -= 1
    per, reach = width // LANES, atoms_ref.shape[1] // LANES
    me = me_ref[0]
    round_rows(residual_ref, rows_ref)
    fill_hankel(rows_ref, turned_rows_ref, hankel_ref)
    frames = windows_of(frames_ref, 0, width), windows_of(hankel_ref, me, width)
    each = slabs // buffers
    together = max(1, min(each, 256 // owned))

    def atoms_at(ref, b):
        taps = [ref[(b * reach + p) * owned : (b * reach + p + 1) * owned, :] for p in range(reach)]
        return jnp.concatenate(taps, axis=1)

    for i in range(buffers):
        for start in range(0, each, together):
            places = range(start, start + together)
            there = [pl.ds(pl.multiple_of(owner_of(me, i * each + b, slabs) * owned, owned), owned) for b in places]
            value = jnp.concatenate([codes_ref[own, :] for own in there], axis=0).astype(F32)
            cutoff = CODE_STEP * jnp.concatenate([thresholds_ref[own, :] for own in there], axis=0)
            for ref, frame in ((before_refs[i], frames[0]), (after_refs[i], frames[1])):
                atoms_b = jnp.concatenate([atoms_at(ref, b) for b in places], axis=0)
                value = soft(value + (CODE_STEP * factor) * dot(atoms_b, frame, ((1,), (0,))), cutoff)
            value = value.astype(BF16)
            for b, own in enumerate(there):
                codes_out[own, :] = value[b * owned : (b + 1) * owned]
    gradient_ref[...] = jnp.zeros_like(gradient_ref)

    def body(n):
        gradient_ref[...] += dot(owned_codes_ref[n + 1], windows_of(hankel_ref, n, width), ((1,), (0,)))

    repeat(slabs, body)
    atoms_out[...] = normalised(atoms_ref[...] + factor * gradient_ref[...])
    residual_out[...] = residual_ref[pl.ds(me * per, per), :]


def call(kernel, outs, scratch, *args):
    vmem = pl.BlockSpec(memory_space=pltpu.VMEM)
    return pl.pallas_call(
        kernel,
        out_shape=outs,
        in_specs=[pl.BlockSpec(memory_space=pltpu.SMEM)] + [vmem] * (len(args) - 1),
        out_specs=jax.tree.map(lambda _: vmem, outs),
        scratch_shapes=scratch,
        compiler_params=pltpu.CompilerParams(vmem_limit_bytes=VMEM_BYTES),
    )(*args)


def swapped(block, distance):
    count = lax.axis_size("tm")
    return lax.ppermute(block, "tm", [(i, i ^ distance) for i in range(count)])


def gathered_and_summed(block, part):
    distance = lax.axis_size("tm") // 2
    rows = part.shape[0]
    buffers = [block]
    while distance:
        high = lax.reduce_precision(part, 8, 7)
        low = lax.reduce_precision(part - high, 8, 7)
        terms = [high.astype(BF16), low.astype(BF16)]
        if distance > 1:
            mine = jnp.concatenate(buffers + terms)
            other = swapped(mine, distance)
            end = mine.shape[0] - 2 * rows
            terms = other[end:]
            buffers = [mine[:end], other[:end]]
        else:
            terms = swapped(jnp.concatenate(terms), distance)
            buffers = buffers + [swapped(buffer, distance) for buffer in buffers]
        part = (high + low) + (terms[:rows].astype(F32) + terms[rows:].astype(F32))
        distance //= 2
    return buffers, part


def on_device(signal, codes, dictionary, thresholds):
    _, atom_count, width = codes.shape
    owned, lag_count = dictionary.shape
    slabs = lax.axis_size("tm")
    per = width // LANES
    blocks = slabs * per
    factor = (atom_count * lag_count) ** (-0.5)
    me = lax.axis_index("tm")
    at = me.astype(jnp.int32).reshape(1)
    signal_rows = signal.reshape(per, LANES)
    own_thresholds = lax.dynamic_slice(thresholds, (me * owned,), (owned,)).reshape(owned, 1)
    codes = codes[0]

    by_atom = lax.all_to_all(codes.reshape(slabs, owned, width), "tm", 0, 0, tiled=True)

    sums = [pltpu.VMEM((LANES, LANES), F32), pltpu.VMEM((blocks, 8, LANES), F32)]
    windows = [
        pltpu.VMEM((blocks + 8, LANES), F32),
        pltpu.VMEM((blocks + 8, 8, LANES), F32),
        pltpu.VMEM((blocks + per - 1, LANES, LANES), BF16),
        pltpu.VMEM((owned, lag_count), F32),
    ]
    atoms_shape = jax.ShapeDtypeStruct((owned, lag_count), F32)
    taps_shape = jax.ShapeDtypeStruct((owned * lag_count // LANES, LANES), BF16)
    part_shape = jax.ShapeDtypeStruct((blocks, LANES), F32)
    taps, part = call(
        functools.partial(first_kernel, factor), (taps_shape, part_shape), sums, at, dictionary, by_atom, signal_rows
    )
    before, first = gathered_and_summed(taps, part)
    atoms, taps, next_codes, part, frames = call(
        functools.partial(second_kernel, factor),
        (
            atoms_shape,
            taps_shape,
            jax.ShapeDtypeStruct((slabs + 1, owned, width), BF16),
            part_shape,
            jax.ShapeDtypeStruct((2 * per - 1, LANES, LANES), BF16),
        ),
        windows + sums,
        at, first, dictionary, by_atom, own_thresholds, signal_rows,
    )
    after, second = gathered_and_summed(taps, part)
    atoms, residual, codes = call(
        functools.partial(third_kernel, factor, len(after)),
        (
            atoms_shape,
            jax.ShapeDtypeStruct((per, LANES), F32),
            jax.ShapeDtypeStruct((atom_count, width), BF16),
        ),
        windows,
        at, frames, second, atoms, next_codes, codes, thresholds.reshape(atom_count, 1), *before, *after,
    )
    return codes[None], atoms, residual.reshape(1, width)


def solution(mesh):
    return jax.shard_map(
        on_device,
        mesh=mesh,
        in_specs=(P("groups", "tm"), P("groups", None, "tm"), P("tm", None), P()),
        out_specs=(P("groups", None, "tm"), P(("groups", "tm"), None), P("groups", "tm")),
        check_vma=False,
    )
```

time: 105 us -> 92.5 us (0.88)
  starting transfers between devices: 30.9 us -> 18.8 us
  Pallas kernels: 19.6 us -> 10.8 us
  waiting for transfers between devices: 49.1 us -> 57.3 us
  other arithmetic: 2.86 us -> 1.11 us
  local copies, waits for them, and re-layouts: 1.82 us -> 3.18 us
    ppermute x16 -> x12, starting transfers between devices: 23.4 us -> 11.3 us  [swapped(): return lax.ppermute(block, 'tm', [(i, i ^ distance) for i in range(count)])]
    pallas_call x3, Pallas kernels: 19.6 us -> 10.8 us  [call(): pl.pallas_call(kernel, out_shape=outs, in_specs=[pl.BlockSpec(memory_spac...]
    ppermute x16 -> x12, waiting for transfers between devices: 26.1 us -> 34.3 us  [swapped(): return lax.ppermute(block, 'tm', [(i, i ^ distance) for i in range(count)])]
    another operation x13 -> x0, other arithmetic: 2.78 us -> none  [gathered(): block = jnp.stack([low, high], axis=1).reshape(-1, rows, width)]
  transfers between devices with their start and end apart: 17 -> 13, of which waited for: 12 -> 9; matrix products, arithmetic and copies ran while one was open for 2% -> 2% of each run, Pallas kernels for 0% -> 0%
where the time goes in v2:
time: 92.5 us; the launch traced here: 92.1 us
  waiting for transfers between devices  57.3 us (62%)
  starting transfers between devices  18.8 us (20%)
  Pallas kernels  10.8 us (12%)
  local copies, waits for them, and re-layouts  3.18 us (3%)
  other arithmetic  1.11 us (1%)
  between operations  0.95 us (1%)
    ppermute x12, waiting for transfers between devices, swapped(): return lax.ppermute(block, 'tm', [(i, i ^ distance) for i in range(count)])  34.3 us
    all_to_all x1, waiting for transfers between devices, on_device(): lax.all_to_all(codes.reshape(slabs, owned, width), 'tm', 0, 0, tiled=True)  22.9 us
    ppermute x12, starting transfers between devices, swapped(): return lax.ppermute(block, 'tm', [(i, i ^ distance) for i in range(count)])  11.3 us
    pallas_call x3, Pallas kernels, call(): pl.pallas_call(kernel, out_shape=outs, in_specs=[pl.BlockSpec(memory_spac...  10.8 us
    all_to_all x1, starting transfers between devices, on_device(): lax.all_to_all(codes.reshape(slabs, owned, width), 'tm', 0, 0, tiled=True)  7.53 us
    unnamed x24, local copies, waits for them, and re-layouts  1.89 us
  transfers between devices with their start and end apart: 13, of which 9 were waited for; matrix products, arithmetic and copies ran while one was open for 2% of the time, Pallas kernels for 0%

profile of v2, /device:TPU:0, one launch (start us, length us, event | category | flops | bytes accessed | tf_op | source)
XLA Modules:
  0.0 92.1 jit_solution(6216499627979250015)
XLA Ops:
  0.6 0.0 copy-start.1
  0.6 0.0 copy-start.6
  0.6 7.5 %all-to-all-start = ((bf16[16,64,512]{2,1,0:T(8,128)(2,1)}), bf16[16,64,512]{2,1,0:T(8,128)(2,1)S(1)}, u32[]{:S(2)}, u32[]{:S(2)}) async-start(bf16[16,64,512]{2,1,0:T(8,128)(2,1)} %bitcast.9), calls=%async_computation | async-start | bytes 2097152 | tf_op jit(solution)/shard_map/all_to_all | solution.py:273
  8.2 22.9 %all-to-all-done.codes_ref = bf16[16,64,512]{2,1,0:T(8,128)(2,1)S(1)} async-done(((bf16[16,64,512]{2,1,0:T(8,128)(2,1)}), bf16[16,64,512]{2,1,0:T(8,128)(2,1)S(1)}, u32[]{:S(2)}, u32[]{:S(2)}) %all-to-all-start) | async-done | bytes 1048608 | tf_op jit(solution)/shard_map/all_to_all | solution.py:273
  31.1 0.0 copy-done.1
  31.1 0.0 copy-done.6
  31.1 1.4 %shard_map.67 = (bf16[256,128]{1,0:T(8,128)(2,1)S(1)}, f32[64,128]{1,0:T(8,128)S(1)}) custom-call(s32[1]{0:T(128)} %bitcast.me_ref, f32[64,512]{1,0:T(8,128)S(1)} %copy-done.1, bf16[16,64,512]{2,1,0:T(8,128)(2,1)S(1)} %all-to-all-done.codes_ref, f32[4,128]{1,0:T(4,128)S(1)} %bitcast.11), custom_call_target="tpu_custom_call" | custom-call | tf_op jit(solution)/shard_map/pallas_call | solution.py:223
  32.6 0.0 copy-start.10
  32.6 5.1 %collective-permute-start = (bf16[384,128]{1,0:T(8,128)(2,1)S(1)}, bf16[384,128]{1,0:T(8,128)(2,1)S(1)}, u32[]{:S(2)}, u32[]{:S(2)}) collective-permute-start(bf16[384,128]{1,0:T(8,128)(2,1)S(1)} %pad_maximum_fusion.4), channel_id=1, source_target_pairs={{0,8},{1,9},{2,10},{3,11},{4,12},{5,13},{6,14},{7,15},{8,0},{9,1},... | collective-permute-start | bytes 294920 | tf_op jit(solution)/shard_map/ppermute | solution.py:235
  37.7 4.7 %collective-permute-done = bf16[384,128]{1,0:T(8,128)(2,1)S(1)} collective-permute-done((bf16[384,128]{1,0:T(8,128)(2,1)S(1)}, bf16[384,128]{1,0:T(8,128)(2,1)S(1)}, u32[]{:S(2)}, u32[]{:S(2)}) %collective-permute-start) | collective-permute-done | bytes 98336 | tf_op jit(solution)/shard_map/ppermute | solution.py:235
  42.5 0.1 collective-permute-start.1
  42.6 5.3 %collective-permute-done.1 = bf16[640,128]{1,0:T(8,128)(2,1)S(1)} collective-permute-done((bf16[640,128]{1,0:T(8,128)(2,1)S(1)}, bf16[640,128]{1,0:T(8,128)(2,1)S(1)}, u32[]{:S(2)}, u32[]{:S(2)}) %collective-permute-start.1) | collective-permute-done | bytes 163872 | tf_op jit(solution)/shard_map/ppermute | solution.py:235
  48.0 0.1 collective-permute-start.2
  48.1 6.7 %collective-permute-done.2 = bf16[1152,128]{1,0:T(8,128)(2,1)S(1)} collective-permute-done((bf16[1152,128]{1,0:T(8,128)(2,1)S(1)}, bf16[1152,128]{1,0:T(8,128)(2,1)S(1)}, u32[]{:S(2)}, u32[]{:S(2)}) %collective-permute-start.2) | collective-permute-done | bytes 294944 | tf_op jit(solution)/shard_map/ppermute | solution.py:235
  54.8 0.1 collective-permute-start.3
  54.9 0.0 copy-done.10
  54.9 0.1 dynamic-slice_bitcast_fusion
  55.0 0.1 copy.8.thresholds_ref
  55.1 1.0 %collective-permute-done.3 = bf16[128,128]{1,0:T(8,128)(2,1)S(1)} collective-permute-done((bf16[128,128]{1,0:T(8,128)(2,1)S(1)}, bf16[128,128]{1,0:T(8,128)(2,1)S(1)}, u32[]{:S(2)}, u32[]{:S(2)}) %collective-permute-start.3) | collective-permute-done | bytes 32800 | tf_op jit(solution)/shard_map/ppermute | solution.py:235
  56.1 3.3 %shard_map.68 = (f32[64,512]{1,0:T(8,128)S(1)}, bf16[256,128]{1,0:T(8,128)(2,1)S(1)}, bf16[17,64,512]{2,1,0:T(8,128)(2,1)S(1)}, f32[64,128]{1,0:T(8,128)S(1)}, bf16[7,128,128]{2,1,0:T(8,128)(2,1)S(1)}) custom-call(s32[1]{0:T(128)} %bitcast.me_ref, f32[64,128]{1,0:T(8,128)S(1)} %fusion.11.residual_ref, f32[64,512]{1,0:T(8,128)S(1)} %copy-done.1, ...), custom_call_target="tpu_custom_call" | custom-call | tf_op jit(solution)/shard_map/pallas_call | solution.py:223
  59.4 0.0 copy-start.4
  59.5 0.0 copy-start.8
  59.5 2.4 %collective-permute-start.4 = (bf16[384,128]{1,0:T(8,128)(2,1)S(1)}, bf16[384,128]{1,0:T(8,128)(2,1)S(1)}, u32[]{:S(2)}, u32[]{:S(2)}) collective-permute-start(bf16[384,128]{1,0:T(8,128)(2,1)S(1)} %pad_maximum_fusion.5), channel_id=1, source_target_pairs={{0,8},{1,9},{2,10},{3,11},{4,12},{5,13},{6,14},{7,15},{8,0},{9,1},... | collective-permute-start | bytes 294920 | tf_op jit(solution)/shard_map/ppermute | solution.py:235
  61.9 5.5 %collective-permute-done.4 = bf16[384,128]{1,0:T(8,128)(2,1)S(1)} collective-permute-done((bf16[384,128]{1,0:T(8,128)(2,1)S(1)}, bf16[384,128]{1,0:T(8,128)(2,1)S(1)}, u32[]{:S(2)}, u32[]{:S(2)}) %collective-permute-start.4) | collective-permute-done | bytes 98336 | tf_op jit(solution)/shard_map/ppermute | solution.py:235
  67.5 0.4 collective-permute-start.5
  67.9 5.1 %collective-permute-done.5 = bf16[640,128]{1,0:T(8,128)(2,1)S(1)} collective-permute-done((bf16[640,128]{1,0:T(8,128)(2,1)S(1)}, bf16[640,128]{1,0:T(8,128)(2,1)S(1)}, u32[]{:S(2)}, u32[]{:S(2)}) %collective-permute-start.5) | collective-permute-done | bytes 163872 | tf_op jit(solution)/shard_map/ppermute | solution.py:235
  73.1 1.8 %collective-permute-start.6 = (bf16[1152,128]{1,0:T(8,128)(2,1)S(1)}, bf16[1152,128]{1,0:T(8,128)(2,1)S(1)}, u32[]{:S(2)}, u32[]{:S(2)}) collective-permute-start(bf16[1152,128]{1,0:T(8,128)(2,1)S(1)} %constant_dynamic-update-slice_fusion.5), channel_id=1, source_target_pairs={{0,2},{1,3},{2,0},{3,1},{4,6},{5,7},{6,4},{7,5},{8,10},{9,11},{10,... | collective-permute-start | bytes 884744 | tf_op jit(solution)/shard_map/ppermute | solution.py:235
  74.9 0.0 copy-start
  75.0 0.1 collective-permute-start.8
  75.1 0.5 collective-permute-start.9
  75.7 0.1 collective-permute-start.10
  75.8 5.1 %collective-permute-done.6 = bf16[1152,128]{1,0:T(8,128)(2,1)S(1)} collective-permute-done((bf16[1152,128]{1,0:T(8,128)(2,1)S(1)}, bf16[1152,128]{1,0:T(8,128)(2,1)S(1)}, u32[]{:S(2)}, u32[]{:S(2)}) %collective-permute-start.6) | collective-permute-done | bytes 294944 | tf_op jit(solution)/shard_map/ppermute | solution.py:235
  80.9 0.8 slice.135.refs_5_
  81.6 0.0 collective-permute-start.11
  81.7 0.6 collective-permute-start.7
  82.2 0.0 copy-done.9
  82.2 0.2 copy.9.thresholds_ref
  82.5 0.9 collective-permute-done.7
  83.3 0.8 fusion.23.residual_ref
  84.1 0.0 collective-permute-done.8.refs_2_
  84.1 0.0 collective-permute-done.9.refs_3_
  84.2 0.0 collective-permute-done.10.refs_6_
  84.2 0.0 collective-permute-done.11.refs_7_
  84.2 0.0 copy-done
  84.2 0.0 copy-start.3
  84.2 0.9 %copy-done.3 = bf16[7,128,128]{2,1,0:T(8,128)(2,1)S(1)} copy-done((bf16[7,128,128]{2,1,0:T(8,128)(2,1)S(1)}, bf16[7,128,128]{2,1,0:T(8,128)(2,1)}, u32[]{:S(2)}) %copy-start.3) | copy-done | bytes 229400
  85.1 0.9 copy-done.5
  86.0 6.1 %shard_map.69 = (f32[64,512]{1,0:T(8,128)}, f32[4,128]{1,0:T(4,128)}, bf16[1024,512]{1,0:T(8,128)(2,1)}) custom-call(s32[1]{0:T(128)} %bitcast.me_ref, bf16[7,128,128]{2,1,0:T(8,128)(2,1)S(1)} %copy-done.3, f32[64,128]{1,0:T(8,128)S(1)} %fusion.23.residual_ref, f32[64,512]{1,0:T(8,128)S(1)} %copy-done.5, ...), custom_call_target="tpu_custom_call" | custom-call | tf_op jit(solution)/shard_map/pallas_call | solution.py:223
  (34 shorter events, 0.5 us)
Async XLA Ops:
  0.6 30.5 %copy-start.1 = (f32[64,512]{1,0:T(8,128)S(1)}, f32[64,512]{1,0:T(8,128)}, u32[]{:S(2)}) copy-start(f32[64,512]{1,0:T(8,128)} %atoms_ref.3) | copy-start | bytes 393220
  0.6 30.5 %copy-start.6 = (f32[1,512]{1,0:T(1,128)S(1)}, f32[1,512]{1,0:T(1,128)}, u32[]{:S(2)}) copy-start(f32[1,512]{1,0:T(1,128)} %param.4) | copy-start | bytes 6148
  0.6 30.5 %all-to-all-start = ((bf16[16,64,512]{2,1,0:T(8,128)(2,1)}), bf16[16,64,512]{2,1,0:T(8,128)(2,1)S(1)}, u32[]{:S(2)}, u32[]{:S(2)}) async-start(bf16[16,64,512]{2,1,0:T(8,128)(2,1)} %bitcast.9), calls=%async_computation | async-start | bytes 2097152 | tf_op jit(solution)/shard_map/all_to_all | solution.py:273
  32.6 22.3 %copy-start.10 = (f32[1024]{0:T(1024)S(1)}, f32[1024]{0:T(1024)}, u32[]{:S(2)}) copy-start(f32[1024]{0:T(1024)} %param.7) | copy-start | bytes 12292
  32.6 9.8 %collective-permute-start = (bf16[384,128]{1,0:T(8,128)(2,1)S(1)}, bf16[384,128]{1,0:T(8,128)(2,1)S(1)}, u32[]{:S(2)}, u32[]{:S(2)}) collective-permute-start(bf16[384,128]{1,0:T(8,128)(2,1)S(1)} %pad_maximum_fusion.4), channel_id=1, source_target_pairs={{0,8},{1,9},{2,10},{3,11},{4,12},{5,13},{6,14},{7,15},{8,0},{9,1},... | collective-permute-start | bytes 294920 | tf_op jit(solution)/shard_map/ppermute | solution.py:235
  42.5 5.4 %collective-permute-start.1 = (bf16[640,128]{1,0:T(8,128)(2,1)S(1)}, bf16[640,128]{1,0:T(8,128)(2,1)S(1)}, u32[]{:S(2)}, u32[]{:S(2)}) collective-permute-start(bf16[640,128]{1,0:T(8,128)(2,1)S(1)} %pad_maximum_fusion.2), channel_id=1, source_target_pairs={{0,4},{1,5},{2,6},{3,7},{4,0},{5,1},{6,2},{7,3},{8,12},{9,13},{10,... | collective-permute-start | bytes 491528 | tf_op jit(solution)/shard_map/ppermute | solution.py:235
  48.0 6.8 %collective-permute-start.2 = (bf16[1152,128]{1,0:T(8,128)(2,1)S(1)}, bf16[1152,128]{1,0:T(8,128)(2,1)S(1)}, u32[]{:S(2)}, u32[]{:S(2)}) collective-permute-start(bf16[1152,128]{1,0:T(8,128)(2,1)S(1)} %constant_dynamic-update-slice_fusion), channel_id=1, source_target_pairs={{0,2},{1,3},{2,0},{3,1},{4,6},{5,7},{6,4},{7,5},{8,10},{9,11},{10,... | collective-permute-start | bytes 884744 | tf_op jit(solution)/shard_map/ppermute | solution.py:235
  54.8 1.3 %copy-start.7 = (bf16[1152,128]{1,0:T(8,128)(2,1)}, bf16[1152,128]{1,0:T(8,128)(2,1)S(1)}, u32[]{:S(2)}) copy-start(bf16[1152,128]{1,0:T(8,128)(2,1)S(1)} %collective-permute-done.2) | copy-start | bytes 884740
  54.8 1.3 %collective-permute-start.3 = (bf16[128,128]{1,0:T(8,128)(2,1)S(1)}, bf16[128,128]{1,0:T(8,128)(2,1)S(1)}, u32[]{:S(2)}, u32[]{:S(2)}) collective-permute-start(bf16[128,128]{1,0:T(8,128)(2,1)S(1)} %pad_maximum_fusion.6), channel_id=1, source_target_pairs={{0,1},{1,0},{2,3},{3,2},{4,5},{5,4},{6,7},{7,6},{8,9},{9,8},{10,11... | collective-permute-start | bytes 98312 | tf_op jit(solution)/shard_map/ppermute | solution.py:235
  59.4 15.6 %copy-start.2 = (bf16[7,128,128]{2,1,0:T(8,128)(2,1)}, bf16[7,128,128]{2,1,0:T(8,128)(2,1)S(1)}, u32[]{:S(2)}) copy-start(bf16[7,128,128]{2,1,0:T(8,128)(2,1)S(1)} %get-tuple-element.15.frames_ref) | copy-start | bytes 688132
  59.4 15.6 %copy-start.4 = (f32[64,512]{1,0:T(8,128)}, f32[64,512]{1,0:T(8,128)S(1)}, u32[]{:S(2)}) copy-start(f32[64,512]{1,0:T(8,128)S(1)} %get-tuple-element.18.atoms_ref) | copy-start | bytes 393220
  59.5 15.6 %copy-start.8 = (bf16[1152,128]{1,0:T(8,128)(2,1)S(1)}, bf16[1152,128]{1,0:T(8,128)(2,1)}, u32[]{:S(2)}) copy-start(bf16[1152,128]{1,0:T(8,128)(2,1)} %copy-done.7) | copy-start | bytes 884740
  59.5 7.9 %collective-permute-start.4 = (bf16[384,128]{1,0:T(8,128)(2,1)S(1)}, bf16[384,128]{1,0:T(8,128)(2,1)S(1)}, u32[]{:S(2)}, u32[]{:S(2)}) collective-permute-start(bf16[384,128]{1,0:T(8,128)(2,1)S(1)} %pad_maximum_fusion.5), channel_id=1, source_target_pairs={{0,8},{1,9},{2,10},{3,11},{4,12},{5,13},{6,14},{7,15},{8,0},{9,1},... | collective-permute-start | bytes 294920 | tf_op jit(solution)/shard_map/ppermute | solution.py:235
  67.5 5.5 %collective-permute-start.5 = (bf16[640,128]{1,0:T(8,128)(2,1)S(1)}, bf16[640,128]{1,0:T(8,128)(2,1)S(1)}, u32[]{:S(2)}, u32[]{:S(2)}) collective-permute-start(bf16[640,128]{1,0:T(8,128)(2,1)S(1)} %pad_maximum_fusion.3), channel_id=1, source_target_pairs={{0,4},{1,5},{2,6},{3,7},{4,0},{5,1},{6,2},{7,3},{8,12},{9,13},{10,... | collective-permute-start | bytes 491528 | tf_op jit(solution)/shard_map/ppermute | solution.py:235
  73.1 7.8 %collective-permute-start.6 = (bf16[1152,128]{1,0:T(8,128)(2,1)S(1)}, bf16[1152,128]{1,0:T(8,128)(2,1)S(1)}, u32[]{:S(2)}, u32[]{:S(2)}) collective-permute-start(bf16[1152,128]{1,0:T(8,128)(2,1)S(1)} %constant_dynamic-update-slice_fusion.5), channel_id=1, source_target_pairs={{0,2},{1,3},{2,0},{3,1},{4,6},{5,7},{6,4},{7,5},{8,10},{9,11},{10,... | collective-permute-start | bytes 884744 | tf_op jit(solution)/shard_map/ppermute | solution.py:235
  74.9 9.2 %copy-start = (bf16[1,1024,512]{2,1,0:T(8,128)(2,1)S(1)}, bf16[1,1024,512]{2,1,0:T(8,128)(2,1)}, u32[]{:S(2)}) copy-start(bf16[1,1024,512]{2,1,0:T(8,128)(2,1)} %param.5) | copy-start | bytes 3145732
  75.0 9.2 %collective-permute-start.8 = (bf16[1024,128]{1,0:T(8,128)(2,1)S(1)}, bf16[1024,128]{1,0:T(8,128)(2,1)}, u32[]{:S(2)}, u32[]{:S(2)}) collective-permute-start(bf16[1024,128]{1,0:T(8,128)(2,1)S(1)} %pad_maximum_fusion.refs_0_), channel_id=1, source_target_pairs={{0,1},{1,0},{2,3},{3,2},{4,5},{5,4},{6,7},{7,6},{8,9},{9,8},{10,11... | collective-permute-start | bytes 786440 | tf_op jit(solution)/shard_map/ppermute | solution.py:235
  75.1 9.1 %collective-permute-start.9 = (bf16[1024,128]{1,0:T(8,128)(2,1)S(1)}, bf16[1024,128]{1,0:T(8,128)(2,1)}, u32[]{:S(2)}, u32[]{:S(2)}) collective-permute-start(bf16[1024,128]{1,0:T(8,128)(2,1)S(1)} %slice.134.refs_1_), channel_id=1, source_target_pairs={{0,1},{1,0},{2,3},{3,2},{4,5},{5,4},{6,7},{7,6},{8,9},{9,8},{10,11... | collective-permute-start | bytes 786440 | tf_op jit(solution)/shard_map/ppermute | solution.py:235
  75.7 8.5 %collective-permute-start.10 = (bf16[1024,128]{1,0:T(8,128)(2,1)S(1)}, bf16[1024,128]{1,0:T(8,128)(2,1)}, u32[]{:S(2)}, u32[]{:S(2)}) collective-permute-start(bf16[1024,128]{1,0:T(8,128)(2,1)S(1)} %pad_maximum_fusion.1.refs_4_), channel_id=1, source_target_pairs={{0,1},{1,0},{2,3},{3,2},{4,5},{5,4},{6,7},{7,6},{8,9},{9,8},{10,11... | collective-permute-start | bytes 786440 | tf_op jit(solution)/shard_map/ppermute | solution.py:235
  80.9 1.4 %copy-start.9 = (bf16[1152,128]{1,0:T(8,128)(2,1)}, bf16[1152,128]{1,0:T(8,128)(2,1)S(1)}, u32[]{:S(2)}) copy-start(bf16[1152,128]{1,0:T(8,128)(2,1)S(1)} %collective-permute-done.6) | copy-start | bytes 884740
  81.6 2.5 %collective-permute-start.11 = (bf16[1024,128]{1,0:T(8,128)(2,1)}, bf16[1024,128]{1,0:T(8,128)(2,1)}, u32[]{:S(2)}, u32[]{:S(2)}) collective-permute-start(bf16[1024,128]{1,0:T(8,128)(2,1)} %slice.135.refs_5_), channel_id=1, source_target_pairs={{0,1},{1,0},{2,3},{3,2},{4,5},{5,4},{6,7},{7,6},{8,9},{9,8},{10,11... | collective-permute-start | bytes 786440 | tf_op jit(solution)/shard_map/ppermute | solution.py:235
  81.7 1.7 %collective-permute-start.7 = (bf16[128,128]{1,0:T(8,128)(2,1)S(1)}, bf16[128,128]{1,0:T(8,128)(2,1)}, u32[]{:S(2)}, u32[]{:S(2)}) collective-permute-start(bf16[128,128]{1,0:T(8,128)(2,1)S(1)} %pad_maximum_fusion.7), channel_id=1, source_target_pairs={{0,1},{1,0},{2,3},{3,2},{4,5},{5,4},{6,7},{7,6},{8,9},{9,8},{10,11... | collective-permute-start | bytes 98312 | tf_op jit(solution)/shard_map/ppermute | solution.py:235
  84.2 0.9 %copy-start.3 = (bf16[7,128,128]{2,1,0:T(8,128)(2,1)S(1)}, bf16[7,128,128]{2,1,0:T(8,128)(2,1)}, u32[]{:S(2)}) copy-start(bf16[7,128,128]{2,1,0:T(8,128)(2,1)} %copy-done.2) | copy-start | bytes 688132
  85.1 0.9 copy-start.5

commit v3 on v2

--- a/solution.py
+++ b/solution.py
@@ -1,4 +1,5 @@
 import functools
+import math
 
 import jax
 import jax.numpy as jnp
@@ -11,7 +12,6 @@
 EPSILON = 1e-06
 LANES = 128
 F32, BF16 = jnp.float32, jnp.bfloat16
-VMEM_BYTES = 48 * 1024 * 1024
 
 
 def dot(a, b, dims):
@@ -177,35 +177,56 @@
     partial_residual(me_ref[0], factor, signal_ref, sums_ref, part_out)
 
 
+def atoms_at(ref, places, owned, reach):
+    taps = [[ref[(b * reach + p) * owned : (b * reach + p + 1) * owned, :] for p in range(reach)] for b in places]
+    return jnp.concatenate([jnp.concatenate(row, axis=1) for row in taps], axis=0)
+
+
+def rows_at(me, first, places, owned, count):
+    return [pl.ds(pl.multiple_of(owner_of(me, first + b, count) * owned, owned), owned) for b in places]
+
+
+def batches(each, owned):
+    together = max(1, min(each, 256 // owned))
+    return [range(start, start + together) for start in range(0, each, together)]
+
+
+def shrink_kernel(factor, count, owned, me_ref, frames_ref, codes_ref, thresholds_ref, *refs):
+    buffers, values_out = refs[:-1], refs[-1]
+    width = codes_ref.shape[1]
+    reach = width // LANES
+    frames = windows_of(frames_ref, 0, width)
+    each = count // len(buffers)
+    for i, ref in enumerate(buffers):
+        for places in batches(each, owned):
+            there = rows_at(me_ref[0], i * each, places, owned, count)
+            value = jnp.concatenate([codes_ref[own, :] for own in there], axis=0).astype(F32)
+            cutoff = CODE_STEP * jnp.concatenate([thresholds_ref[own, :] for own in there], axis=0)
+            value += (CODE_STEP * factor) * dot(atoms_at(ref, places, owned, reach), frames, ((1,), (0,)))
+            first = (i * each + places[0]) * owned
+            values_out[first : first + value.shape[0], :] = soft(value, cutoff)
+
+
 def third_kernel(
-    factor, buffers, me_ref, frames_ref, residual_ref, atoms_ref, owned_codes_ref, codes_ref, thresholds_ref, *refs
+    factor, me_ref, residual_ref, atoms_ref, owned_codes_ref, values_ref, thresholds_ref, *refs
 ):
-    before_refs, after_refs = refs[:buffers], refs[buffers : 2 * buffers]
-    atoms_out, residual_out, codes_out, rows_ref, turned_rows_ref, hankel_ref, gradient_ref = refs[2 * buffers :]
+    buffers = refs[:-7]
+    atoms_out, residual_out, codes_out, rows_ref, turned_rows_ref, hankel_ref, gradient_ref = refs[-7:]
     slabs, owned, width = owned_codes_ref.shape
     slabs -= 1
     per, reach = width // LANES, atoms_ref.shape[1] // LANES
     me = me_ref[0]
     round_rows(residual_ref, rows_ref)
     fill_hankel(rows_ref, turned_rows_ref, hankel_ref)
-    frames = windows_of(frames_ref, 0, width), windows_of(hankel_ref, me, width)
-    each = slabs // buffers
-    together = max(1, min(each, 256 // owned))
-
-    def atoms_at(ref, b):
-        taps = [ref[(b * reach + p) * owned : (b * reach + p + 1) * owned, :] for p in range(reach)]
-        return jnp.concatenate(taps, axis=1)
-
-    for i in range(buffers):
-        for start in range(0, each, together):
-            places = range(start, start + together)
-            there = [pl.ds(pl.multiple_of(owner_of(me, i * each + b, slabs) * owned, owned), owned) for b in places]
-            value = jnp.concatenate([codes_ref[own, :] for own in there], axis=0).astype(F32)
+    frames = windows_of(hankel_ref, me, width)
+    each = slabs // len(buffers)
+    for i, ref in enumerate(buffers):
+        for places in batches(each, owned):
+            there = rows_at(me, i * each, places, owned, slabs)
             cutoff = CODE_STEP * jnp.concatenate([thresholds_ref[own, :] for own in there], axis=0)
-            for ref, frame in ((before_refs[i], frames[0]), (after_refs[i], frames[1])):
-                atoms_b = jnp.concatenate([atoms_at(ref, b) for b in places], axis=0)
-                value = soft(value + (CODE_STEP * factor) * dot(atoms_b, frame, ((1,), (0,))), cutoff)
-            value = value.astype(BF16)
+            first = (i * each + places[0]) * owned
+            change = (CODE_STEP * factor) * dot(atoms_at(ref, places, owned, reach), frames, ((1,), (0,)))
+            value = soft(values_ref[first : first + change.shape[0], :] + change, cutoff).astype(BF16)
             for b, own in enumerate(there):
                 codes_out[own, :] = value[b * owned : (b + 1) * owned]
     gradient_ref[...] = jnp.zeros_like(gradient_ref)
@@ -219,6 +240,8 @@
 
 
 def call(kernel, outs, scratch, *args):
+    held = [(a.shape, a.dtype) for a in [*args[1:], *jax.tree.leaves(outs)]] + [(a.shape, a.dtype) for a in scratch]
+    room = sum(math.prod(shape) * jnp.dtype(kind).itemsize for shape, kind in held)
     vmem = pl.BlockSpec(memory_space=pltpu.VMEM)
     return pl.pallas_call(
         kernel,
@@ -226,7 +249,7 @@
         in_specs=[pl.BlockSpec(memory_space=pltpu.SMEM)] + [vmem] * (len(args) - 1),
         out_specs=jax.tree.map(lambda _: vmem, outs),
         scratch_shapes=scratch,
-        compiler_params=pltpu.CompilerParams(vmem_limit_bytes=VMEM_BYTES),
+        compiler_params=pltpu.CompilerParams(vmem_limit_bytes=room + 6 * 1024 * 1024),
     )(*args)
 
 
@@ -235,24 +258,28 @@
     return lax.ppermute(block, "tm", [(i, i ^ distance) for i in range(count)])
 
 
-def gathered_and_summed(block, part):
+def tied(value, *others):
+    return lax.optimization_barrier((value, others))[0]
+
+
+def exchanged(block, part, alone, late=None):
     distance = lax.axis_size("tm") // 2
     rows = part.shape[0]
     buffers = [block]
     while distance:
         high = lax.reduce_precision(part, 8, 7)
         low = lax.reduce_precision(part - high, 8, 7)
-        terms = [high.astype(BF16), low.astype(BF16)]
-        if distance > 1:
-            mine = jnp.concatenate(buffers + terms)
-            other = swapped(mine, distance)
-            end = mine.shape[0] - 2 * rows
-            terms = other[end:]
-            buffers = [mine[:end], other[:end]]
-        else:
-            terms = swapped(jnp.concatenate(terms), distance)
-            buffers = buffers + [swapped(buffer, distance) for buffer in buffers]
-        part = (high + low) + (terms[:rows].astype(F32) + terms[rows:].astype(F32))
+        sent = [high.astype(BF16), low.astype(BF16)]
+        if distance > alone:
+            sent = buffers + sent
+        sent = jnp.concatenate(sent)
+        if distance == 2 and late is not None:
+            sent = tied(sent, late)
+        other = swapped(sent, distance)
+        end = sent.shape[0] - 2 * rows
+        if distance > alone:
+            buffers = [sent[:end], other[:end]]
+        part = (high + low) + (other[end : end + rows].astype(F32) + other[end + rows :].astype(F32))
         distance //= 2
     return buffers, part
 
@@ -285,7 +312,7 @@
     taps, part = call(
         functools.partial(first_kernel, factor), (taps_shape, part_shape), sums, at, dictionary, by_atom, signal_rows
     )
-    before, first = gathered_and_summed(taps, part)
+    before, first = exchanged(taps, part, 2)
     atoms, taps, next_codes, part, frames = call(
         functools.partial(second_kernel, factor),
         (
@@ -298,16 +325,27 @@
         windows + sums,
         at, first, dictionary, by_atom, own_thresholds, signal_rows,
     )
-    after, second = gathered_and_summed(taps, part)
+    all_thresholds = thresholds.reshape(atom_count, 1)
+    mine = jnp.concatenate(before)
+    other = swapped(tied(mine, part), 2)
+    before = [mine, other, swapped(mine, 1), swapped(other, 1)]
+    after, second = exchanged(taps, part, 1, other)
+    after = after + [swapped(buffer, 1) for buffer in after]
+    values = call(
+        functools.partial(shrink_kernel, factor, slabs, owned),
+        jax.ShapeDtypeStruct((atom_count, width), F32),
+        [],
+        at, frames, codes, all_thresholds, *before,
+    )
     atoms, residual, codes = call(
-        functools.partial(third_kernel, factor, len(after)),
+        functools.partial(third_kernel, factor),
         (
             atoms_shape,
             jax.ShapeDtypeStruct((per, LANES), F32),
             jax.ShapeDtypeStruct((atom_count, width), BF16),
         ),
         windows,
-        at, frames, second, atoms, next_codes, codes, thresholds.reshape(atom_count, 1), *before, *after,
+        at, second, atoms, next_codes, values, all_thresholds, *after,
     )
     return codes[None], atoms, residual.reshape(1, width)
 

time: 92.5 us -> 92.3 us (level)
  starting transfers between devices: 18.8 us -> 16.2 us
  waiting for transfers between devices: 57.3 us -> 59.5 us
  Pallas kernels: 10.8 us -> 12 us
  local copies, waits for them, and re-layouts: 3.18 us -> 2.15 us
    ppermute x12 -> x13, starting transfers between devices: 11.3 us -> 8.71 us  [swapped(): return lax.ppermute(block, 'tm', [(i, i ^ distance) for i in range(count)])]
    ppermute x12 -> x13, waiting for transfers between devices: 34.3 us -> 36.6 us  [swapped(): return lax.ppermute(block, 'tm', [(i, i ^ distance) for i in range(count)])]
    pallas_call x3 -> x4, Pallas kernels: 10.8 us -> 12 us  [call(): pl.pallas_call(kernel, out_shape=outs, in_specs=[pl.BlockSpec(memory_spac...]
    unnamed x24 -> x20, local copies, waits for them, and re-layouts: 1.89 us -> 1.68 us
  transfers between devices with their start and end apart: 13 -> 14, of which waited for: 9 -> 9; matrix products, arithmetic and copies ran while one was open for 2% -> 1% of each run, Pallas kernels for 0% -> 2%
where the time goes in v3:
time: 92.3 us; the launch traced here: 91.9 us
  waiting for transfers between devices  59.5 us (64%)
  starting transfers between devices  16.2 us (18%)
  Pallas kernels  12 us (13%)
  local copies, waits for them, and re-layouts  2.15 us (2%)
  other arithmetic  1.09 us (1%)
  between operations  0.97 us (1%)
    ppermute x13, waiting for transfers between devices, swapped(): return lax.ppermute(block, 'tm', [(i, i ^ distance) for i in range(count)])  36.6 us
    all_to_all x1, waiting for transfers between devices, on_device(): lax.all_to_all(codes.reshape(slabs, owned, width), 'tm', 0, 0, tiled=True)  22.9 us
    pallas_call x4, Pallas kernels, call(): pl.pallas_call(kernel, out_shape=outs, in_specs=[pl.BlockSpec(memory_spac...  12 us
    ppermute x13, starting transfers between devices, swapped(): return lax.ppermute(block, 'tm', [(i, i ^ distance) for i in range(count)])  8.71 us
    all_to_all x1, starting transfers between devices, on_device(): lax.all_to_all(codes.reshape(slabs, owned, width), 'tm', 0, 0, tiled=True)  7.53 us
  transfers between devices with their start and end apart: 14, of which 9 were waited for; matrix products, arithmetic and copies ran while one was open for 1% of the time, Pallas kernels for 2%

profile of v3, /device:TPU:0, one launch (start us, length us, event | category | flops | bytes accessed | tf_op | source)
XLA Modules:
  0.0 91.9 jit_solution(4450151091540971105)
XLA Ops:
  0.6 0.0 copy-start.6
  0.6 0.0 copy-start.1
  0.7 0.0 copy-start.8
  0.7 7.5 %all-to-all-start = ((bf16[16,64,512]{2,1,0:T(8,128)(2,1)}), bf16[16,64,512]{2,1,0:T(8,128)(2,1)S(1)}, u32[]{:S(2)}, u32[]{:S(2)}) async-start(bf16[16,64,512]{2,1,0:T(8,128)(2,1)} %bitcast.9), calls=%async_computation | async-start | bytes 2097152 | tf_op jit(solution)/shard_map/all_to_all | solution.py:300
  8.2 22.9 %all-to-all-done.codes_ref = bf16[16,64,512]{2,1,0:T(8,128)(2,1)S(1)} async-done(((bf16[16,64,512]{2,1,0:T(8,128)(2,1)}), bf16[16,64,512]{2,1,0:T(8,128)(2,1)S(1)}, u32[]{:S(2)}, u32[]{:S(2)}) %all-to-all-start) | async-done | bytes 1048608 | tf_op jit(solution)/shard_map/all_to_all | solution.py:300
  31.1 0.0 copy-done.6
  31.1 0.0 copy-done.1
  31.1 1.4 %shard_map.67 = (bf16[256,128]{1,0:T(8,128)(2,1)S(1)}, f32[64,128]{1,0:T(8,128)S(1)}) custom-call(s32[1]{0:T(128)} %bitcast.me_ref, f32[64,512]{1,0:T(8,128)S(1)} %copy-done.1, bf16[16,64,512]{2,1,0:T(8,128)(2,1)S(1)} %all-to-all-done.codes_ref, f32[4,128]{1,0:T(4,128)S(1)} %bitcast.11), custom_call_target="tpu_custom_call" | custom-call | tf_op jit(solution)/shard_map/pallas_call | solution.py:246
  32.6 5.1 %collective-permute-start = (bf16[384,128]{1,0:T(8,128)(2,1)S(1)}, bf16[384,128]{1,0:T(8,128)(2,1)S(1)}, u32[]{:S(2)}, u32[]{:S(2)}) collective-permute-start(bf16[384,128]{1,0:T(8,128)(2,1)S(1)} %pad_maximum_fusion.3), channel_id=1, source_target_pairs={{0,8},{1,9},{2,10},{3,11},{4,12},{5,13},{6,14},{7,15},{8,0},{9,1},... | collective-permute-start | bytes 294920 | tf_op jit(solution)/shard_map/ppermute | solution.py:258
  37.7 4.7 %collective-permute-done = bf16[384,128]{1,0:T(8,128)(2,1)S(1)} collective-permute-done((bf16[384,128]{1,0:T(8,128)(2,1)S(1)}, bf16[384,128]{1,0:T(8,128)(2,1)S(1)}, u32[]{:S(2)}, u32[]{:S(2)}) %collective-permute-start) | collective-permute-done | bytes 98336 | tf_op jit(solution)/shard_map/ppermute | solution.py:258
  42.5 0.1 collective-permute-start.1
  42.6 5.3 %collective-permute-done.1 = bf16[640,128]{1,0:T(8,128)(2,1)S(1)} collective-permute-done((bf16[640,128]{1,0:T(8,128)(2,1)S(1)}, bf16[640,128]{1,0:T(8,128)(2,1)S(1)}, u32[]{:S(2)}, u32[]{:S(2)}) %collective-permute-start.1) | collective-permute-done | bytes 163872 | tf_op jit(solution)/shard_map/ppermute | solution.py:258
  47.9 0.1 collective-permute-start.2
  48.0 3.9 %collective-permute-done.2 = bf16[128,128]{1,0:T(8,128)(2,1)S(1)} collective-permute-done((bf16[128,128]{1,0:T(8,128)(2,1)S(1)}, bf16[128,128]{1,0:T(8,128)(2,1)S(1)}, u32[]{:S(2)}, u32[]{:S(2)}) %collective-permute-start.2) | collective-permute-done | bytes 32800 | tf_op jit(solution)/shard_map/ppermute | solution.py:258
  51.9 0.1 collective-permute-start.3
  52.0 0.0 copy-done.8
  52.0 0.1 dynamic-slice_bitcast_fusion
  52.1 0.1 copy.8.thresholds_ref
  52.2 1.0 %collective-permute-done.3 = bf16[128,128]{1,0:T(8,128)(2,1)S(1)} collective-permute-done((bf16[128,128]{1,0:T(8,128)(2,1)S(1)}, bf16[128,128]{1,0:T(8,128)(2,1)S(1)}, u32[]{:S(2)}, u32[]{:S(2)}) %collective-permute-start.3) | collective-permute-done | bytes 32800 | tf_op jit(solution)/shard_map/ppermute | solution.py:258
  53.2 3.3 %shard_map.68 = (f32[64,512]{1,0:T(8,128)S(1)}, bf16[256,128]{1,0:T(8,128)(2,1)S(1)}, bf16[17,64,512]{2,1,0:T(8,128)(2,1)S(1)}, f32[64,128]{1,0:T(8,128)S(1)}, bf16[7,128,128]{2,1,0:T(8,128)(2,1)S(1)}) custom-call(s32[1]{0:T(128)} %bitcast.me_ref, f32[64,128]{1,0:T(8,128)S(1)} %fusion.11.residual_ref, f32[64,512]{1,0:T(8,128)S(1)} %copy-done.1, ...), custom_call_target="tpu_custom_call" | custom-call | tf_op jit(solution)/shard_map/pallas_call | solution.py:246
  56.6 0.0 copy-start.2
  56.6 0.7 copy-done.2
  57.3 0.9 collective-permute-start.4
  58.2 7.0 %collective-permute-done.4 = bf16[384,128]{1,0:T(8,128)(2,1)S(1)} collective-permute-done((bf16[384,128]{1,0:T(8,128)(2,1)S(1)}, bf16[384,128]{1,0:T(8,128)(2,1)S(1)}, u32[]{:S(2)}, u32[]{:S(2)}) %collective-permute-start.4) | collective-permute-done | bytes 98336 | tf_op jit(solution)/shard_map/ppermute | solution.py:258
  65.3 0.1 collective-permute-start.5
  65.4 0.8 collective-permute-start.6
  66.2 5.3 %collective-permute-done.5 = bf16[640,128]{1,0:T(8,128)(2,1)S(1)} collective-permute-done((bf16[640,128]{1,0:T(8,128)(2,1)S(1)}, bf16[640,128]{1,0:T(8,128)(2,1)S(1)}, u32[]{:S(2)}, u32[]{:S(2)}) %collective-permute-start.5) | collective-permute-done | bytes 163872 | tf_op jit(solution)/shard_map/ppermute | solution.py:258
  71.6 2.3 %collective-permute-done.6.refs_1_ = bf16[1024,128]{1,0:T(8,128)(2,1)} collective-permute-done((bf16[1024,128]{1,0:T(8,128)(2,1)S(1)}, bf16[1024,128]{1,0:T(8,128)(2,1)}, u32[]{:S(2)}, u32[]{:S(2)}) %collective-permute-start.6) | collective-permute-done | bytes 262176 | tf_op jit(solution)/shard_map/ppermute | solution.py:258
  73.9 0.4 collective-permute-start.7
  74.3 0.0 collective-permute-start.9
  74.3 0.5 collective-permute-start.10
  74.8 0.1 collective-permute-start.11
  74.9 7.1 %collective-permute-done.7 = bf16[1152,128]{1,0:T(8,128)(2,1)S(1)} collective-permute-done((bf16[1152,128]{1,0:T(8,128)(2,1)S(1)}, bf16[1152,128]{1,0:T(8,128)(2,1)S(1)}, u32[]{:S(2)}, u32[]{:S(2)}) %collective-permute-start.7) | collective-permute-done | bytes 294944 | tf_op jit(solution)/shard_map/ppermute | solution.py:258
  82.0 0.1 collective-permute-start.12
  82.1 0.6 collective-permute-start.8
  82.7 0.0 copy-done.7
  82.7 0.2 copy.9.thresholds_ref
  82.9 0.0 collective-permute-done.9.refs_2_
  82.9 0.0 collective-permute-done.10.refs_3_
  82.9 0.0 copy-done
  82.9 0.0 copy-start.3
  82.9 0.9 %copy-done.3 = bf16[7,128,128]{2,1,0:T(8,128)(2,1)S(1)} copy-done((bf16[7,128,128]{2,1,0:T(8,128)(2,1)S(1)}, bf16[7,128,128]{2,1,0:T(8,128)(2,1)}, u32[]{:S(2)}) %copy-start.3) | copy-done | bytes 229400
  83.9 2.0 %shard_map.69.values_ref = f32[1024,512]{1,0:T(8,128)S(1)} custom-call(s32[1]{0:T(128)} %bitcast.me_ref, bf16[7,128,128]{2,1,0:T(8,128)(2,1)S(1)} %copy-done.3, bf16[1024,512]{1,0:T(8,128)(2,1)S(1)} %bitcast.10, f32[1024,1]{1,0:T(8,128)S(1)} %copy.9.thresholds_ref, bf16[1024,128]{1,0:T(8,128)(2,1)S(1)} %pad_maximum_fusion.refs_0_, ...), custom_call_target="tpu_custom_call" | custom-call | tf_op jit(solution)/shard_map/pallas_call | solution.py:246
  85.8 0.0 collective-permute-done.8
  85.8 0.8 fusion.23.residual_ref
  86.6 0.0 collective-permute-done.11.refs_2_
  86.7 0.0 collective-permute-done.12.refs_3_
  86.7 5.3 %shard_map.70 = (f32[64,512]{1,0:T(8,128)}, f32[4,128]{1,0:T(4,128)}, bf16[1024,512]{1,0:T(8,128)(2,1)}) custom-call(s32[1]{0:T(128)} %bitcast.me_ref, f32[64,128]{1,0:T(8,128)S(1)} %fusion.23.residual_ref, f32[64,512]{1,0:T(8,128)S(1)} %copy-done.5, bf16[17,64,512]{2,1,0:T(8,128)(2,1)S(1)} %get-tuple-element.22.owned_codes_ref, ...), custom_call_target="tpu_custom_call" | custom-call | tf_op jit(solution)/shard_map/pallas_call | solution.py:246
  (32 shorter events, 0.4 us)
Async XLA Ops:
  0.6 30.5 %copy-start.6 = (f32[1,512]{1,0:T(1,128)S(1)}, f32[1,512]{1,0:T(1,128)}, u32[]{:S(2)}) copy-start(f32[1,512]{1,0:T(1,128)} %param.4) | copy-start | bytes 6148
  0.6 30.5 %copy-start.1 = (f32[64,512]{1,0:T(8,128)S(1)}, f32[64,512]{1,0:T(8,128)}, u32[]{:S(2)}) copy-start(f32[64,512]{1,0:T(8,128)} %atoms_ref.3) | copy-start | bytes 393220
  0.7 51.4 %copy-start.8 = (f32[1024]{0:T(1024)S(1)}, f32[1024]{0:T(1024)}, u32[]{:S(2)}) copy-start(f32[1024]{0:T(1024)} %param.7) | copy-start | bytes 12292
  0.7 30.5 %all-to-all-start = ((bf16[16,64,512]{2,1,0:T(8,128)(2,1)}), bf16[16,64,512]{2,1,0:T(8,128)(2,1)S(1)}, u32[]{:S(2)}, u32[]{:S(2)}) async-start(bf16[16,64,512]{2,1,0:T(8,128)(2,1)} %bitcast.9), calls=%async_computation | async-start | bytes 2097152 | tf_op jit(solution)/shard_map/all_to_all | solution.py:300
  32.6 9.8 %collective-permute-start = (bf16[384,128]{1,0:T(8,128)(2,1)S(1)}, bf16[384,128]{1,0:T(8,128)(2,1)S(1)}, u32[]{:S(2)}, u32[]{:S(2)}) collective-permute-start(bf16[384,128]{1,0:T(8,128)(2,1)S(1)} %pad_maximum_fusion.3), channel_id=1, source_target_pairs={{0,8},{1,9},{2,10},{3,11},{4,12},{5,13},{6,14},{7,15},{8,0},{9,1},... | collective-permute-start | bytes 294920 | tf_op jit(solution)/shard_map/ppermute | solution.py:258
  42.5 5.4 %collective-permute-start.1 = (bf16[640,128]{1,0:T(8,128)(2,1)S(1)}, bf16[640,128]{1,0:T(8,128)(2,1)S(1)}, u32[]{:S(2)}, u32[]{:S(2)}) collective-permute-start(bf16[640,128]{1,0:T(8,128)(2,1)S(1)} %pad_maximum_fusion.1), channel_id=1, source_target_pairs={{0,4},{1,5},{2,6},{3,7},{4,0},{5,1},{6,2},{7,3},{8,12},{9,13},{10,... | collective-permute-start | bytes 491528 | tf_op jit(solution)/shard_map/ppermute | solution.py:258
  47.9 4.0 %collective-permute-start.2 = (bf16[128,128]{1,0:T(8,128)(2,1)S(1)}, bf16[128,128]{1,0:T(8,128)(2,1)S(1)}, u32[]{:S(2)}, u32[]{:S(2)}) collective-permute-start(bf16[128,128]{1,0:T(8,128)(2,1)S(1)} %pad_maximum_fusion.5), channel_id=1, source_target_pairs={{0,2},{1,3},{2,0},{3,1},{4,6},{5,7},{6,4},{7,5},{8,10},{9,11},{10,... | collective-permute-start | bytes 98312 | tf_op jit(solution)/shard_map/ppermute | solution.py:258
  51.9 1.3 %collective-permute-start.3 = (bf16[128,128]{1,0:T(8,128)(2,1)S(1)}, bf16[128,128]{1,0:T(8,128)(2,1)S(1)}, u32[]{:S(2)}, u32[]{:S(2)}) collective-permute-start(bf16[128,128]{1,0:T(8,128)(2,1)S(1)} %pad_maximum_fusion.6), channel_id=1, source_target_pairs={{0,1},{1,0},{2,3},{3,2},{4,5},{5,4},{6,7},{7,6},{8,9},{9,8},{10,11... | collective-permute-start | bytes 98312 | tf_op jit(solution)/shard_map/ppermute | solution.py:258
  56.6 0.7 copy-start.2
  57.3 8.1 %copy-start.4 = (f32[64,512]{1,0:T(8,128)}, f32[64,512]{1,0:T(8,128)S(1)}, u32[]{:S(2)}) copy-start(f32[64,512]{1,0:T(8,128)S(1)} %get-tuple-element.21.atoms_ref) | copy-start | bytes 393220
  57.3 25.6 %copy-start = (bf16[1,1024,512]{2,1,0:T(8,128)(2,1)S(1)}, bf16[1,1024,512]{2,1,0:T(8,128)(2,1)}, u32[]{:S(2)}) copy-start(bf16[1,1024,512]{2,1,0:T(8,128)(2,1)} %param.5) | copy-start | bytes 3145732
  57.3 7.9 %collective-permute-start.4 = (bf16[384,128]{1,0:T(8,128)(2,1)S(1)}, bf16[384,128]{1,0:T(8,128)(2,1)S(1)}, u32[]{:S(2)}, u32[]{:S(2)}) collective-permute-start(bf16[384,128]{1,0:T(8,128)(2,1)S(1)} %pad_maximum_fusion.4), channel_id=1, source_target_pairs={{0,8},{1,9},{2,10},{3,11},{4,12},{5,13},{6,14},{7,15},{8,0},{9,1},... | collective-permute-start | bytes 294920 | tf_op jit(solution)/shard_map/ppermute | solution.py:258
  65.3 6.2 %collective-permute-start.5 = (bf16[640,128]{1,0:T(8,128)(2,1)S(1)}, bf16[640,128]{1,0:T(8,128)(2,1)S(1)}, u32[]{:S(2)}, u32[]{:S(2)}) collective-permute-start(bf16[640,128]{1,0:T(8,128)(2,1)S(1)} %pad_maximum_fusion.2), channel_id=1, source_target_pairs={{0,4},{1,5},{2,6},{3,7},{4,0},{5,1},{6,2},{7,3},{8,12},{9,13},{10,... | collective-permute-start | bytes 491528 | tf_op jit(solution)/shard_map/ppermute | solution.py:258
  65.4 8.4 %collective-permute-start.6 = (bf16[1024,128]{1,0:T(8,128)(2,1)S(1)}, bf16[1024,128]{1,0:T(8,128)(2,1)}, u32[]{:S(2)}, u32[]{:S(2)}) collective-permute-start(bf16[1024,128]{1,0:T(8,128)(2,1)S(1)} %pad_maximum_fusion.refs_0_), channel_id=1, source_target_pairs={{0,2},{1,3},{2,0},{3,1},{4,6},{5,7},{6,4},{7,5},{8,10},{9,11},{10,... | collective-permute-start | bytes 786440 | tf_op jit(solution)/shard_map/ppermute | solution.py:258
  73.9 8.1 %collective-permute-start.7 = (bf16[1152,128]{1,0:T(8,128)(2,1)S(1)}, bf16[1152,128]{1,0:T(8,128)(2,1)S(1)}, u32[]{:S(2)}, u32[]{:S(2)}) collective-permute-start(bf16[1152,128]{1,0:T(8,128)(2,1)S(1)} %fusion.24), channel_id=1, source_target_pairs={{0,2},{1,3},{2,0},{3,1},{4,6},{5,7},{6,4},{7,5},{8,10},{9,11},{10,... | collective-permute-start | bytes 884744 | tf_op jit(solution)/shard_map/ppermute | solution.py:258
  74.3 8.6 %collective-permute-start.9 = (bf16[1024,128]{1,0:T(8,128)(2,1)S(1)}, bf16[1024,128]{1,0:T(8,128)(2,1)}, u32[]{:S(2)}, u32[]{:S(2)}) collective-permute-start(bf16[1024,128]{1,0:T(8,128)(2,1)S(1)} %pad_maximum_fusion.refs_0_), channel_id=1, source_target_pairs={{0,1},{1,0},{2,3},{3,2},{4,5},{5,4},{6,7},{7,6},{8,9},{9,8},{10,11... | collective-permute-start | bytes 786440 | tf_op jit(solution)/shard_map/ppermute | solution.py:258
  74.3 8.6 %collective-permute-start.10 = (bf16[1024,128]{1,0:T(8,128)(2,1)}, bf16[1024,128]{1,0:T(8,128)(2,1)}, u32[]{:S(2)}, u32[]{:S(2)}) collective-permute-start(bf16[1024,128]{1,0:T(8,128)(2,1)} %collective-permute-done.6.refs_1_), channel_id=1, source_target_pairs={{0,1},{1,0},{2,3},{3,2},{4,5},{5,4},{6,7},{7,6},{8,9},{9,8},{10,11... | collective-permute-start | bytes 786440 | tf_op jit(solution)/shard_map/ppermute | solution.py:258
  74.8 11.8 %collective-permute-start.11 = (bf16[1024,128]{1,0:T(8,128)(2,1)S(1)}, bf16[1024,128]{1,0:T(8,128)(2,1)}, u32[]{:S(2)}, u32[]{:S(2)}) collective-permute-start(bf16[1024,128]{1,0:T(8,128)(2,1)S(1)} %slice.90.refs_0_), channel_id=1, source_target_pairs={{0,1},{1,0},{2,3},{3,2},{4,5},{5,4},{6,7},{7,6},{8,9},{9,8},{10,11... | collective-permute-start | bytes 786440 | tf_op jit(solution)/shard_map/ppermute | solution.py:258
  82.0 0.7 copy-start.7
  82.0 4.7 %collective-permute-start.12 = (bf16[1024,128]{1,0:T(8,128)(2,1)S(1)}, bf16[1024,128]{1,0:T(8,128)(2,1)}, u32[]{:S(2)}, u32[]{:S(2)}) collective-permute-start(bf16[1024,128]{1,0:T(8,128)(2,1)S(1)} %slice.112.refs_1_), channel_id=1, source_target_pairs={{0,1},{1,0},{2,3},{3,2},{4,5},{5,4},{6,7},{7,6},{8,9},{9,8},{10,11... | collective-permute-start | bytes 786440 | tf_op jit(solution)/shard_map/ppermute | solution.py:258
  82.1 3.7 %collective-permute-start.8 = (bf16[128,128]{1,0:T(8,128)(2,1)S(1)}, bf16[128,128]{1,0:T(8,128)(2,1)}, u32[]{:S(2)}, u32[]{:S(2)}) collective-permute-start(bf16[128,128]{1,0:T(8,128)(2,1)S(1)} %pad_maximum_fusion.7), channel_id=1, source_target_pairs={{0,1},{1,0},{2,3},{3,2},{4,5},{5,4},{6,7},{7,6},{8,9},{9,8},{10,11... | collective-permute-start | bytes 98312 | tf_op jit(solution)/shard_map/ppermute | solution.py:258
  82.9 0.9 %copy-start.3 = (bf16[7,128,128]{2,1,0:T(8,128)(2,1)S(1)}, bf16[7,128,128]{2,1,0:T(8,128)(2,1)}, u32[]{:S(2)}) copy-start(bf16[7,128,128]{2,1,0:T(8,128)(2,1)} %copy-done.2) | copy-start | bytes 688132
  83.9 2.8 %copy-start.5 = (f32[64,512]{1,0:T(8,128)S(1)}, f32[64,512]{1,0:T(8,128)}, u32[]{:S(2)}) copy-start(f32[64,512]{1,0:T(8,128)} %copy-done.4) | copy-start | bytes 393220

commit v4 on v3

--- a/solution.py
+++ b/solution.py
@@ -137,22 +137,37 @@
     partial_residual(me_ref[0], factor, signal_ref, sums_ref, part_out)
 
 
-def round_rows(residual_ref, rows_ref):
-    count = residual_ref.shape[0]
-    rows_ref[:count, :] = residual_ref[...].astype(BF16).astype(F32)
+def whole_residual(terms):
+    rows = terms[0].shape[0] // 2
+    mine, other = (ref[:rows, :].astype(F32) + ref[rows:, :].astype(F32) for ref in terms)
+    return mine + other
+
+
+def round_rows(residual, rows_ref):
+    count = residual.shape[0]
+    rows_ref[:count, :] = residual.astype(BF16).astype(F32)
     rows_ref[count:, :] = jnp.zeros((rows_ref.shape[0] - count, LANES), F32)
 
 
+def kept_at(piece, slabs, per):
+    lane = piece % per * LANES
+    return slabs + 3 + piece // per, slice(lane, lane + LANES)
+
+
 def second_kernel(
-    factor, me_ref, residual_ref, atoms_ref, codes_ref, thresholds_ref, signal_ref,
-    atoms_out, taps_out, codes_out, part_out, frames_out,
+    factor, me_ref, sent_ref, other_ref, atoms_ref, codes_ref, thresholds_ref, signal_ref,
+    taps_out, codes_out, part_out,
     rows_ref, turned_rows_ref, hankel_ref, gradient_ref, turned_ref, sums_ref,
 ):
     slabs, owned, width = codes_ref.shape
     per = width // LANES
-    round_rows(residual_ref, rows_ref)
+    round_rows(whole_residual((sent_ref, other_ref)), rows_ref)
     fill_hankel(rows_ref, turned_rows_ref, hankel_ref)
-    frames_out[...] = hankel_ref[pl.ds(me_ref[0] * per, 2 * per - 1)]
+    for m in range(2 * per - 1):
+        block = hankel_ref[me_ref[0] * per + m]
+        for h in range(LANES // owned):
+            slab, lane = kept_at(m * (LANES // owned) + h, slabs, per)
+            codes_out[slab, :, lane] = block[h * owned : (h + 1) * owned, :]
     atoms = atoms_ref[...]
     atoms_b = atoms.astype(BF16)
     cutoff = CODE_STEP * thresholds_ref[...]
@@ -169,8 +184,9 @@
 
     repeat(slabs, body)
     after = normalised(atoms + factor * gradient_ref[...])
-    atoms_out[...] = after
     after_b = after.astype(BF16)
+    codes_out[slabs + 1] = after_b
+    codes_out[slabs + 2] = (after - after_b.astype(F32)).astype(BF16)
     taps = stacked_taps(after_b)
     taps_out[...] = taps
     rebuild(taps, lambda n: codes_out[n + 1], slabs, width, turned_ref, sums_ref)
@@ -191,63 +207,55 @@
     return [range(start, start + together) for start in range(0, each, together)]
 
 
-def shrink_kernel(factor, count, owned, me_ref, frames_ref, codes_ref, thresholds_ref, *refs):
-    buffers, values_out = refs[:-1], refs[-1]
-    width = codes_ref.shape[1]
-    reach = width // LANES
-    frames = windows_of(frames_ref, 0, width)
-    each = count // len(buffers)
-    for i, ref in enumerate(buffers):
-        for places in batches(each, owned):
-            there = rows_at(me_ref[0], i * each, places, owned, count)
-            value = jnp.concatenate([codes_ref[own, :] for own in there], axis=0).astype(F32)
-            cutoff = CODE_STEP * jnp.concatenate([thresholds_ref[own, :] for own in there], axis=0)
-            value += (CODE_STEP * factor) * dot(atoms_at(ref, places, owned, reach), frames, ((1,), (0,)))
-            first = (i * each + places[0]) * owned
-            values_out[first : first + value.shape[0], :] = soft(value, cutoff)
-
-
 def third_kernel(
-    factor, me_ref, residual_ref, atoms_ref, owned_codes_ref, values_ref, thresholds_ref, *refs
+    factor, buffers, me_ref, sent_ref, other_ref, kept_ref, codes_ref, thresholds_ref, *refs
 ):
-    buffers = refs[:-7]
-    atoms_out, residual_out, codes_out, rows_ref, turned_rows_ref, hankel_ref, gradient_ref = refs[-7:]
-    slabs, owned, width = owned_codes_ref.shape
-    slabs -= 1
-    per, reach = width // LANES, atoms_ref.shape[1] // LANES
+    before_refs, after_refs = refs[:buffers], refs[buffers : 2 * buffers]
+    atoms_out, residual_out, codes_out = refs[2 * buffers : 2 * buffers + 3]
+    rows_ref, turned_rows_ref, hankel_ref, gradient_ref = refs[2 * buffers + 3 :]
+    owned, lag_count = atoms_out.shape
+    atom_count, width = codes_ref.shape
+    slabs, per, reach = atom_count // owned, width // LANES, lag_count // LANES
     me = me_ref[0]
-    round_rows(residual_ref, rows_ref)
+    residual = whole_residual((sent_ref, other_ref))
+    round_rows(residual, rows_ref)
     fill_hankel(rows_ref, turned_rows_ref, hankel_ref)
-    frames = windows_of(hankel_ref, me, width)
-    each = slabs // len(buffers)
-    for i, ref in enumerate(buffers):
+    pieces = [kept_at(piece, slabs, per) for piece in range((2 * per - 1) * (LANES // owned))]
+    pieces = [kept_ref[slab, :, lane] for slab, lane in pieces]
+    blocks = [jnp.concatenate(pieces[i : i + LANES // owned], axis=0) for i in range(0, len(pieces), LANES // owned)]
+    frames = windows_of(blocks, 0, width), windows_of(hankel_ref, me, width)
+    each = slabs // buffers
+    for i in range(buffers):
         for places in batches(each, owned):
             there = rows_at(me, i * each, places, owned, slabs)
             cutoff = CODE_STEP * jnp.concatenate([thresholds_ref[own, :] for own in there], axis=0)
-            first = (i * each + places[0]) * owned
-            change = (CODE_STEP * factor) * dot(atoms_at(ref, places, owned, reach), frames, ((1,), (0,)))
-            value = soft(values_ref[first : first + change.shape[0], :] + change, cutoff).astype(BF16)
+            value = jnp.concatenate([codes_ref[own, :] for own in there], axis=0).astype(F32)
+            for ref, frame in ((before_refs[i], frames[0]), (after_refs[i], frames[1])):
+                change = dot(atoms_at(ref, places, owned, reach), frame, ((1,), (0,)))
+                value = soft(value + (CODE_STEP * factor) * change, cutoff)
+            value = value.astype(BF16)
             for b, own in enumerate(there):
                 codes_out[own, :] = value[b * owned : (b + 1) * owned]
     gradient_ref[...] = jnp.zeros_like(gradient_ref)
 
     def body(n):
-        gradient_ref[...] += dot(owned_codes_ref[n + 1], windows_of(hankel_ref, n, width), ((1,), (0,)))
+        gradient_ref[...] += dot(kept_ref[n + 1], windows_of(hankel_ref, n, width), ((1,), (0,)))
 
     repeat(slabs, body)
-    atoms_out[...] = normalised(atoms_ref[...] + factor * gradient_ref[...])
-    residual_out[...] = residual_ref[pl.ds(me * per, per), :]
+    atoms = kept_ref[slabs + 1].astype(F32) + kept_ref[slabs + 2].astype(F32)
+    atoms_out[...] = normalised(atoms + factor * gradient_ref[...])
+    rows_ref[: slabs * per, :] = residual
+    residual_out[...] = rows_ref[pl.ds(me * per, per), :]
 
 
 def call(kernel, outs, scratch, *args):
-    held = [(a.shape, a.dtype) for a in [*args[1:], *jax.tree.leaves(outs)]] + [(a.shape, a.dtype) for a in scratch]
-    room = sum(math.prod(shape) * jnp.dtype(kind).itemsize for shape, kind in held)
     vmem = pl.BlockSpec(memory_space=pltpu.VMEM)
+    room = sum(math.prod(a.shape) * jnp.dtype(a.dtype).itemsize for a in [*args, *outs, *scratch])
     return pl.pallas_call(
         kernel,
-        out_shape=outs,
+        out_shape=tuple(outs),
         in_specs=[pl.BlockSpec(memory_space=pltpu.SMEM)] + [vmem] * (len(args) - 1),
-        out_specs=jax.tree.map(lambda _: vmem, outs),
+        out_specs=(vmem,) * len(outs),
         scratch_shapes=scratch,
         compiler_params=pltpu.CompilerParams(vmem_limit_bytes=room + 6 * 1024 * 1024),
     )(*args)
@@ -262,26 +270,28 @@
     return lax.optimization_barrier((value, others))[0]
 
 
-def exchanged(block, part, alone, late=None):
+def exchanged(block, part, alone, late={}):
     distance = lax.axis_size("tm") // 2
     rows = part.shape[0]
     buffers = [block]
-    while distance:
+    while True:
         high = lax.reduce_precision(part, 8, 7)
         low = lax.reduce_precision(part - high, 8, 7)
         sent = [high.astype(BF16), low.astype(BF16)]
         if distance > alone:
             sent = buffers + sent
         sent = jnp.concatenate(sent)
-        if distance == 2 and late is not None:
-            sent = tied(sent, late)
+        if distance in late:
+            sent = tied(sent, late[distance])
         other = swapped(sent, distance)
         end = sent.shape[0] - 2 * rows
         if distance > alone:
             buffers = [sent[:end], other[:end]]
+            whole = [sent, other]
+        if distance == 1:
+            return buffers, whole, (sent, other)
         part = (high + low) + (other[end : end + rows].astype(F32) + other[end + rows :].astype(F32))
         distance //= 2
-    return buffers, part
 
 
 def on_device(signal, codes, dictionary, thresholds):
@@ -312,40 +322,29 @@
     taps, part = call(
         functools.partial(first_kernel, factor), (taps_shape, part_shape), sums, at, dictionary, by_atom, signal_rows
     )
-    before, first = exchanged(taps, part, 2)
-    atoms, taps, next_codes, part, frames = call(
+    before, _, first = exchanged(taps, part, 2)
+    kept = slabs + 3 + pl.cdiv((2 * per - 1) * (LANES // owned), per)
+    taps, kept, part = call(
         functools.partial(second_kernel, factor),
-        (
-            atoms_shape,
-            taps_shape,
-            jax.ShapeDtypeStruct((slabs + 1, owned, width), BF16),
-            part_shape,
-            jax.ShapeDtypeStruct((2 * per - 1, LANES, LANES), BF16),
-        ),
+        [taps_shape, jax.ShapeDtypeStruct((kept, owned, width), BF16), part_shape],
         windows + sums,
-        at, first, dictionary, by_atom, own_thresholds, signal_rows,
+        at, *first, dictionary, by_atom, own_thresholds, signal_rows,
     )
     all_thresholds = thresholds.reshape(atom_count, 1)
     mine = jnp.concatenate(before)
     other = swapped(tied(mine, part), 2)
     before = [mine, other, swapped(mine, 1), swapped(other, 1)]
-    after, second = exchanged(taps, part, 1, other)
+    _, after, second = exchanged(taps, part, 1, {4: other})
     after = after + [swapped(buffer, 1) for buffer in after]
-    values = call(
-        functools.partial(shrink_kernel, factor, slabs, owned),
-        jax.ShapeDtypeStruct((atom_count, width), F32),
-        [],
-        at, frames, codes, all_thresholds, *before,
-    )
     atoms, residual, codes = call(
-        functools.partial(third_kernel, factor),
-        (
+        functools.partial(third_kernel, factor, len(after)),
+        [
             atoms_shape,
             jax.ShapeDtypeStruct((per, LANES), F32),
             jax.ShapeDtypeStruct((atom_count, width), BF16),
-        ),
+        ],
         windows,
-        at, second, atoms, next_codes, values, all_thresholds, *after,
+        at, *second, kept, codes, all_thresholds, *before, *after,
     )
     return codes[None], atoms, residual.reshape(1, width)
 

time: 92.3 us -> 88.1 us (0.954)
  waiting for transfers between devices: 59.5 us -> 53.5 us
  starting transfers between devices: 16.2 us -> 20.2 us
  local copies, waits for them, and re-layouts: 2.15 us -> 0.46 us
    ppermute x13, waiting for transfers between devices: 36.6 us -> 30.5 us  [swapped(): return lax.ppermute(block, 'tm', [(i, i ^ distance) for i in range(count)])]
    ppermute x13, starting transfers between devices: 8.71 us -> 12.7 us  [swapped(): return lax.ppermute(block, 'tm', [(i, i ^ distance) for i in range(count)])]
    unnamed x20 -> x8, local copies, waits for them, and re-layouts: 1.68 us -> 0.02 us
    pallas_call x4 -> x3, Pallas kernels: 12 us -> 11.1 us  [call(): pl.pallas_call(kernel, out_shape=tuple(outs), in_specs=[pl.BlockSpec(memo...]
  transfers between devices with their start and end apart: 14 -> 14, of which waited for: 9 -> 10; matrix products, arithmetic and copies ran while one was open for 1% -> 2% of each run, Pallas kernels for 2% -> 0%
where the time goes in v4:
time: 88.1 us; the launch traced here: 87.8 us
  waiting for transfers between devices  53.5 us (61%)
  starting transfers between devices  20.2 us (23%)
  Pallas kernels  11.1 us (13%)
  other arithmetic  1.73 us (2%)
  between operations  0.89 us (1%)
    ppermute x13, waiting for transfers between devices, swapped(): return lax.ppermute(block, 'tm', [(i, i ^ distance) for i in range(count)])  30.5 us
    all_to_all x1, waiting for transfers between devices, on_device(): lax.all_to_all(codes.reshape(slabs, owned, width), 'tm', 0, 0, tiled=True)  22.9 us
    ppermute x13, starting transfers between devices, swapped(): return lax.ppermute(block, 'tm', [(i, i ^ distance) for i in range(count)])  12.7 us
    pallas_call x3, Pallas kernels, call(): pl.pallas_call(kernel, out_shape=tuple(outs), in_specs=[pl.BlockSpec(memo...  11.1 us
    all_to_all x1, starting transfers between devices, on_device(): lax.all_to_all(codes.reshape(slabs, owned, width), 'tm', 0, 0, tiled=True)  7.53 us
  transfers between devices with their start and end apart: 14, of which 10 were waited for; matrix products, arithmetic and copies ran while one was open for 2% of the time, Pallas kernels for 0%

profile of v4, /device:TPU:0, one launch (start us, length us, event | category | flops | bytes accessed | tf_op | source)
XLA Modules:
  0.0 87.8 jit_solution(8093888545498619617)
XLA Ops:
  0.6 0.0 copy-start.1
  0.6 0.0 copy-start.2
  0.6 7.5 %all-to-all-start = ((bf16[16,64,512]{2,1,0:T(8,128)(2,1)}), bf16[16,64,512]{2,1,0:T(8,128)(2,1)S(1)}, u32[]{:S(2)}, u32[]{:S(2)}) async-start(bf16[16,64,512]{2,1,0:T(8,128)(2,1)} %bitcast.9), calls=%async_computation | async-start | bytes 2097152 | tf_op jit(solution)/shard_map/all_to_all | solution.py:310
  8.2 0.0 copy-start.3
  8.2 22.9 %all-to-all-done.codes_ref = bf16[16,64,512]{2,1,0:T(8,128)(2,1)S(1)} async-done(((bf16[16,64,512]{2,1,0:T(8,128)(2,1)}), bf16[16,64,512]{2,1,0:T(8,128)(2,1)S(1)}, u32[]{:S(2)}, u32[]{:S(2)}) %all-to-all-start) | async-done | bytes 1048608 | tf_op jit(solution)/shard_map/all_to_all | solution.py:310
  31.1 0.0 copy-done.1
  31.1 0.0 copy-done.2
  31.1 1.4 %shard_map.67 = (bf16[256,128]{1,0:T(8,128)(2,1)S(1)}, f32[64,128]{1,0:T(8,128)S(1)}) custom-call(s32[1]{0:T(128)} %bitcast.me_ref, f32[64,512]{1,0:T(8,128)S(1)} %copy-done.1, bf16[16,64,512]{2,1,0:T(8,128)(2,1)S(1)} %all-to-all-done.codes_ref, f32[4,128]{1,0:T(4,128)S(1)} %bitcast.11), custom_call_target="tpu_custom_call" | custom-call | tf_op jit(solution)/shard_map/pallas_call | solution.py:254
  32.6 5.1 %collective-permute-start = (bf16[384,128]{1,0:T(8,128)(2,1)S(1)}, bf16[384,128]{1,0:T(8,128)(2,1)S(1)}, u32[]{:S(2)}, u32[]{:S(2)}) collective-permute-start(bf16[384,128]{1,0:T(8,128)(2,1)S(1)} %pad_maximum_fusion.4), channel_id=1, source_target_pairs={{0,8},{1,9},{2,10},{3,11},{4,12},{5,13},{6,14},{7,15},{8,0},{9,1},... | collective-permute-start | bytes 294920 | tf_op jit(solution)/shard_map/ppermute | solution.py:266
  37.7 4.7 %collective-permute-done = bf16[384,128]{1,0:T(8,128)(2,1)S(1)} collective-permute-done((bf16[384,128]{1,0:T(8,128)(2,1)S(1)}, bf16[384,128]{1,0:T(8,128)(2,1)S(1)}, u32[]{:S(2)}, u32[]{:S(2)}) %collective-permute-start) | collective-permute-done | bytes 98336 | tf_op jit(solution)/shard_map/ppermute | solution.py:266
  42.5 0.1 collective-permute-start.1
  42.6 5.3 %collective-permute-done.1 = bf16[640,128]{1,0:T(8,128)(2,1)S(1)} collective-permute-done((bf16[640,128]{1,0:T(8,128)(2,1)S(1)}, bf16[640,128]{1,0:T(8,128)(2,1)S(1)}, u32[]{:S(2)}, u32[]{:S(2)}) %collective-permute-start.1) | collective-permute-done | bytes 163872 | tf_op jit(solution)/shard_map/ppermute | solution.py:266
  47.9 0.1 collective-permute-start.2
  48.0 3.9 %collective-permute-done.2 = bf16[128,128]{1,0:T(8,128)(2,1)S(1)} collective-permute-done((bf16[128,128]{1,0:T(8,128)(2,1)S(1)}, bf16[128,128]{1,0:T(8,128)(2,1)S(1)}, u32[]{:S(2)}, u32[]{:S(2)}) %collective-permute-start.2) | collective-permute-done | bytes 32800 | tf_op jit(solution)/shard_map/ppermute | solution.py:266
  51.9 0.1 collective-permute-start.3
  52.0 0.0 copy-done.3
  52.0 0.1 dynamic-slice_bitcast_fusion
  52.1 0.1 copy.8.thresholds_ref
  52.2 1.0 %collective-permute-done.3.other_ref = bf16[128,128]{1,0:T(8,128)(2,1)S(1)} collective-permute-done((bf16[128,128]{1,0:T(8,128)(2,1)S(1)}, bf16[128,128]{1,0:T(8,128)(2,1)S(1)}, u32[]{:S(2)}, u32[]{:S(2)}) %collective-permute-start.3) | collective-permute-done | bytes 32800 | tf_op jit(solution)/shard_map/ppermute | solution.py:266
  53.2 3.4 %shard_map.68 = (bf16[256,128]{1,0:T(8,128)(2,1)S(1)}, bf16[23,64,512]{2,1,0:T(8,128)(2,1)S(1)}, f32[64,128]{1,0:T(8,128)S(1)}) custom-call(s32[1]{0:T(128)} %bitcast.me_ref, bf16[128,128]{1,0:T(8,128)(2,1)S(1)} %pad_maximum_fusion.7.sent_ref, bf16[128,128]{1,0:T(8,128)(2,1)S(1)} %collective-permute-done.3.other_ref, f32[64,512]{1,0:T(8,128)S(1)} %copy-done.1, ...), custom_call_target="tpu_custom_call" | custom-call | tf_op jit(solution)/shard_map/pallas_call | solution.py:254
  56.6 0.0 copy-start
  56.6 0.9 collective-permute-start.4
  57.5 0.7 pad_maximum_fusion.1.refs_0_
  58.2 1.8 %collective-permute-start.5 = (bf16[1024,128]{1,0:T(8,128)(2,1)}, bf16[1024,128]{1,0:T(8,128)(2,1)}, u32[]{:S(2)}, u32[]{:S(2)}) collective-permute-start(bf16[1024,128]{1,0:T(8,128)(2,1)} %pad_maximum_fusion.1.refs_0_), channel_id=1, source_target_pairs={{0,2},{1,3},{2,0},{3,1},{4,6},{5,7},{6,4},{7,5},{8,10},{9,11},{10,... | collective-permute-start | bytes 786440 | tf_op jit(solution)/shard_map/ppermute | solution.py:266
  60.1 4.5 %collective-permute-done.4 = bf16[384,128]{1,0:T(8,128)(2,1)S(1)} collective-permute-done((bf16[384,128]{1,0:T(8,128)(2,1)S(1)}, bf16[384,128]{1,0:T(8,128)(2,1)S(1)}, u32[]{:S(2)}, u32[]{:S(2)}) %collective-permute-start.4) | collective-permute-done | bytes 98336 | tf_op jit(solution)/shard_map/ppermute | solution.py:266
  64.6 2.1 %collective-permute-done.5.refs_1_ = bf16[1024,128]{1,0:T(8,128)(2,1)} collective-permute-done((bf16[1024,128]{1,0:T(8,128)(2,1)}, bf16[1024,128]{1,0:T(8,128)(2,1)}, u32[]{:S(2)}, u32[]{:S(2)}) %collective-permute-start.5) | collective-permute-done | bytes 262176 | tf_op jit(solution)/shard_map/ppermute | solution.py:266
  66.7 1.7 %collective-permute-start.6 = (bf16[640,128]{1,0:T(8,128)(2,1)S(1)}, bf16[640,128]{1,0:T(8,128)(2,1)S(1)}, u32[]{:S(2)}, u32[]{:S(2)}) collective-permute-start(bf16[640,128]{1,0:T(8,128)(2,1)S(1)} %pad_maximum_fusion.3), channel_id=1, source_target_pairs={{0,4},{1,5},{2,6},{3,7},{4,0},{5,1},{6,2},{7,3},{8,12},{9,13},{10,... | collective-permute-start | bytes 491528 | tf_op jit(solution)/shard_map/ppermute | solution.py:266
  68.5 3.6 %collective-permute-done.6 = bf16[640,128]{1,0:T(8,128)(2,1)S(1)} collective-permute-done((bf16[640,128]{1,0:T(8,128)(2,1)S(1)}, bf16[640,128]{1,0:T(8,128)(2,1)S(1)}, u32[]{:S(2)}, u32[]{:S(2)}) %collective-permute-start.6) | collective-permute-done | bytes 163872 | tf_op jit(solution)/shard_map/ppermute | solution.py:266
  72.2 1.8 %collective-permute-start.7 = (bf16[1152,128]{1,0:T(8,128)(2,1)S(1)}, bf16[1152,128]{1,0:T(8,128)(2,1)}, u32[]{:S(2)}, u32[]{:S(2)}) collective-permute-start(bf16[1152,128]{1,0:T(8,128)(2,1)S(1)} %pad_maximum_fusion.refs_4_), channel_id=1, source_target_pairs={{0,2},{1,3},{2,0},{3,1},{4,6},{5,7},{6,4},{7,5},{8,10},{9,11},{10,... | collective-permute-start | bytes 884744 | tf_op jit(solution)/shard_map/ppermute | solution.py:266
  74.0 0.0 collective-permute-start.9
  74.0 0.5 collective-permute-start.10
  74.5 0.0 collective-permute-start.11
  74.5 4.8 %collective-permute-done.7.refs_5_ = bf16[1152,128]{1,0:T(8,128)(2,1)} collective-permute-done((bf16[1152,128]{1,0:T(8,128)(2,1)S(1)}, bf16[1152,128]{1,0:T(8,128)(2,1)}, u32[]{:S(2)}, u32[]{:S(2)}) %collective-permute-start.7) | collective-permute-done | bytes 294944 | tf_op jit(solution)/shard_map/ppermute | solution.py:266
  79.3 0.0 collective-permute-start.12
  79.3 0.8 reduce-precision_convert_fusion
  80.1 0.6 collective-permute-start.8
  80.7 0.2 copy.9.thresholds_ref
  80.9 0.0 collective-permute-done.9.refs_2_
  80.9 0.0 collective-permute-done.10.refs_3_
  80.9 0.0 collective-permute-done.11.refs_6_
  80.9 0.6 collective-permute-done.8.other_ref
  81.5 0.0 collective-permute-done.12.refs_7_
  81.5 0.0 copy-done
  81.5 6.3 %shard_map.69 = (f32[64,512]{1,0:T(8,128)}, f32[4,128]{1,0:T(4,128)}, bf16[1024,512]{1,0:T(8,128)(2,1)}) custom-call(s32[1]{0:T(128)} %bitcast.me_ref, bf16[128,128]{1,0:T(8,128)(2,1)S(1)} %pad_maximum_fusion.8.sent_ref, bf16[128,128]{1,0:T(8,128)(2,1)S(1)} %collective-permute-done.8.other_ref, bf16[23,64,512]{2,1,0:T(8,128)(2,1)S(1)} %get-tuple-element.19.kept_ref, ...), custom_call_target="tpu_custom_call" | custom-call | tf_op jit(solution)/shard_map/pallas_call | solution.py:254
  (22 shorter events, 0.3 us)
Async XLA Ops:
  0.6 30.5 %copy-start.1 = (f32[64,512]{1,0:T(8,128)S(1)}, f32[64,512]{1,0:T(8,128)}, u32[]{:S(2)}) copy-start(f32[64,512]{1,0:T(8,128)} %atoms_ref.3) | copy-start | bytes 393220
  0.6 30.5 %copy-start.2 = (f32[1,512]{1,0:T(1,128)S(1)}, f32[1,512]{1,0:T(1,128)}, u32[]{:S(2)}) copy-start(f32[1,512]{1,0:T(1,128)} %param.4) | copy-start | bytes 6148
  0.6 30.5 %all-to-all-start = ((bf16[16,64,512]{2,1,0:T(8,128)(2,1)}), bf16[16,64,512]{2,1,0:T(8,128)(2,1)S(1)}, u32[]{:S(2)}, u32[]{:S(2)}) async-start(bf16[16,64,512]{2,1,0:T(8,128)(2,1)} %bitcast.9), calls=%async_computation | async-start | bytes 2097152 | tf_op jit(solution)/shard_map/all_to_all | solution.py:310
  8.2 43.8 %copy-start.3 = (f32[1024]{0:T(1024)S(1)}, f32[1024]{0:T(1024)}, u32[]{:S(2)}) copy-start(f32[1024]{0:T(1024)} %param.7) | copy-start | bytes 12292
  32.6 9.8 %collective-permute-start = (bf16[384,128]{1,0:T(8,128)(2,1)S(1)}, bf16[384,128]{1,0:T(8,128)(2,1)S(1)}, u32[]{:S(2)}, u32[]{:S(2)}) collective-permute-start(bf16[384,128]{1,0:T(8,128)(2,1)S(1)} %pad_maximum_fusion.4), channel_id=1, source_target_pairs={{0,8},{1,9},{2,10},{3,11},{4,12},{5,13},{6,14},{7,15},{8,0},{9,1},... | collective-permute-start | bytes 294920 | tf_op jit(solution)/shard_map/ppermute | solution.py:266
  42.5 5.4 %collective-permute-start.1 = (bf16[640,128]{1,0:T(8,128)(2,1)S(1)}, bf16[640,128]{1,0:T(8,128)(2,1)S(1)}, u32[]{:S(2)}, u32[]{:S(2)}) collective-permute-start(bf16[640,128]{1,0:T(8,128)(2,1)S(1)} %pad_maximum_fusion.2), channel_id=1, source_target_pairs={{0,4},{1,5},{2,6},{3,7},{4,0},{5,1},{6,2},{7,3},{8,12},{9,13},{10,... | collective-permute-start | bytes 491528 | tf_op jit(solution)/shard_map/ppermute | solution.py:266
  47.9 4.0 %collective-permute-start.2 = (bf16[128,128]{1,0:T(8,128)(2,1)S(1)}, bf16[128,128]{1,0:T(8,128)(2,1)S(1)}, u32[]{:S(2)}, u32[]{:S(2)}) collective-permute-start(bf16[128,128]{1,0:T(8,128)(2,1)S(1)} %pad_maximum_fusion.6), channel_id=1, source_target_pairs={{0,2},{1,3},{2,0},{3,1},{4,6},{5,7},{6,4},{7,5},{8,10},{9,11},{10,... | collective-permute-start | bytes 98312 | tf_op jit(solution)/shard_map/ppermute | solution.py:266
  51.9 1.3 %collective-permute-start.3 = (bf16[128,128]{1,0:T(8,128)(2,1)S(1)}, bf16[128,128]{1,0:T(8,128)(2,1)S(1)}, u32[]{:S(2)}, u32[]{:S(2)}) collective-permute-start(bf16[128,128]{1,0:T(8,128)(2,1)S(1)} %pad_maximum_fusion.7.sent_ref), channel_id=1, source_target_pairs={{0,1},{1,0},{2,3},{3,2},{4,5},{5,4},{6,7},{7,6},{8,9},{9,8},{10,11... | collective-permute-start | bytes 98312 | tf_op jit(solution)/shard_map/ppermute | solution.py:266
  56.6 24.9 %copy-start = (bf16[1,1024,512]{2,1,0:T(8,128)(2,1)S(1)}, bf16[1,1024,512]{2,1,0:T(8,128)(2,1)}, u32[]{:S(2)}) copy-start(bf16[1,1024,512]{2,1,0:T(8,128)(2,1)} %param.5) | copy-start | bytes 3145732
  56.6 7.9 %collective-permute-start.4 = (bf16[384,128]{1,0:T(8,128)(2,1)S(1)}, bf16[384,128]{1,0:T(8,128)(2,1)S(1)}, u32[]{:S(2)}, u32[]{:S(2)}) collective-permute-start(bf16[384,128]{1,0:T(8,128)(2,1)S(1)} %pad_maximum_fusion.5), channel_id=1, source_target_pairs={{0,8},{1,9},{2,10},{3,11},{4,12},{5,13},{6,14},{7,15},{8,0},{9,1},... | collective-permute-start | bytes 294920 | tf_op jit(solution)/shard_map/ppermute | solution.py:266
  58.2 8.5 %collective-permute-start.5 = (bf16[1024,128]{1,0:T(8,128)(2,1)}, bf16[1024,128]{1,0:T(8,128)(2,1)}, u32[]{:S(2)}, u32[]{:S(2)}) collective-permute-start(bf16[1024,128]{1,0:T(8,128)(2,1)} %pad_maximum_fusion.1.refs_0_), channel_id=1, source_target_pairs={{0,2},{1,3},{2,0},{3,1},{4,6},{5,7},{6,4},{7,5},{8,10},{9,11},{10,... | collective-permute-start | bytes 786440 | tf_op jit(solution)/shard_map/ppermute | solution.py:266
  66.7 5.3 %collective-permute-start.6 = (bf16[640,128]{1,0:T(8,128)(2,1)S(1)}, bf16[640,128]{1,0:T(8,128)(2,1)S(1)}, u32[]{:S(2)}, u32[]{:S(2)}) collective-permute-start(bf16[640,128]{1,0:T(8,128)(2,1)S(1)} %pad_maximum_fusion.3), channel_id=1, source_target_pairs={{0,4},{1,5},{2,6},{3,7},{4,0},{5,1},{6,2},{7,3},{8,12},{9,13},{10,... | collective-permute-start | bytes 491528 | tf_op jit(solution)/shard_map/ppermute | solution.py:266
  72.2 7.1 %collective-permute-start.7 = (bf16[1152,128]{1,0:T(8,128)(2,1)S(1)}, bf16[1152,128]{1,0:T(8,128)(2,1)}, u32[]{:S(2)}, u32[]{:S(2)}) collective-permute-start(bf16[1152,128]{1,0:T(8,128)(2,1)S(1)} %pad_maximum_fusion.refs_4_), channel_id=1, source_target_pairs={{0,2},{1,3},{2,0},{3,1},{4,6},{5,7},{6,4},{7,5},{8,10},{9,11},{10,... | collective-permute-start | bytes 884744 | tf_op jit(solution)/shard_map/ppermute | solution.py:266
  74.0 6.9 %collective-permute-start.9 = (bf16[1024,128]{1,0:T(8,128)(2,1)}, bf16[1024,128]{1,0:T(8,128)(2,1)}, u32[]{:S(2)}, u32[]{:S(2)}) collective-permute-start(bf16[1024,128]{1,0:T(8,128)(2,1)} %pad_maximum_fusion.1.refs_0_), channel_id=1, source_target_pairs={{0,1},{1,0},{2,3},{3,2},{4,5},{5,4},{6,7},{7,6},{8,9},{9,8},{10,11... | collective-permute-start | bytes 786440 | tf_op jit(solution)/shard_map/ppermute | solution.py:266
  74.0 6.9 %collective-permute-start.10 = (bf16[1024,128]{1,0:T(8,128)(2,1)}, bf16[1024,128]{1,0:T(8,128)(2,1)}, u32[]{:S(2)}, u32[]{:S(2)}) collective-permute-start(bf16[1024,128]{1,0:T(8,128)(2,1)} %collective-permute-done.5.refs_1_), channel_id=1, source_target_pairs={{0,1},{1,0},{2,3},{3,2},{4,5},{5,4},{6,7},{7,6},{8,9},{9,8},{10,11... | collective-permute-start | bytes 786440 | tf_op jit(solution)/shard_map/ppermute | solution.py:266
  74.5 6.4 %collective-permute-start.11 = (bf16[1152,128]{1,0:T(8,128)(2,1)S(1)}, bf16[1152,128]{1,0:T(8,128)(2,1)}, u32[]{:S(2)}, u32[]{:S(2)}) collective-permute-start(bf16[1152,128]{1,0:T(8,128)(2,1)S(1)} %pad_maximum_fusion.refs_4_), channel_id=1, source_target_pairs={{0,1},{1,0},{2,3},{3,2},{4,5},{5,4},{6,7},{7,6},{8,9},{9,8},{10,11... | collective-permute-start | bytes 884744 | tf_op jit(solution)/shard_map/ppermute | solution.py:266
  79.3 2.2 %collective-permute-start.12 = (bf16[1152,128]{1,0:T(8,128)(2,1)}, bf16[1152,128]{1,0:T(8,128)(2,1)}, u32[]{:S(2)}, u32[]{:S(2)}) collective-permute-start(bf16[1152,128]{1,0:T(8,128)(2,1)} %collective-permute-done.7.refs_5_), channel_id=1, source_target_pairs={{0,1},{1,0},{2,3},{3,2},{4,5},{5,4},{6,7},{7,6},{8,9},{9,8},{10,11... | collective-permute-start | bytes 884744 | tf_op jit(solution)/shard_map/ppermute | solution.py:266
  80.1 1.4 %collective-permute-start.8 = (bf16[128,128]{1,0:T(8,128)(2,1)S(1)}, bf16[128,128]{1,0:T(8,128)(2,1)S(1)}, u32[]{:S(2)}, u32[]{:S(2)}) collective-permute-start(bf16[128,128]{1,0:T(8,128)(2,1)S(1)} %pad_maximum_fusion.8.sent_ref), channel_id=1, source_target_pairs={{0,1},{1,0},{2,3},{3,2},{4,5},{5,4},{6,7},{7,6},{8,9},{9,8},{10,11... | collective-permute-start | bytes 98312 | tf_op jit(solution)/shard_map/ppermute | solution.py:266

commit v5 on v4

--- a/solution.py
+++ b/solution.py
@@ -207,33 +207,54 @@
     return [range(start, start + together) for start in range(0, each, together)]
 
 
-def third_kernel(
-    factor, buffers, me_ref, sent_ref, other_ref, kept_ref, codes_ref, thresholds_ref, *refs
-):
-    before_refs, after_refs = refs[:buffers], refs[buffers : 2 * buffers]
-    atoms_out, residual_out, codes_out = refs[2 * buffers : 2 * buffers + 3]
-    rows_ref, turned_rows_ref, hankel_ref, gradient_ref = refs[2 * buffers + 3 :]
+def spread(thresholds_ref, cutoffs_ref):
+    count = thresholds_ref.shape[0]
+    filled = jnp.concatenate([thresholds_ref[...], jnp.zeros((LANES - count, LANES), F32)], axis=0)
+    columns = CODE_STEP * filled.T
+    for m in range(count):
+        cutoffs_ref[m * LANES : (m + 1) * LANES, :] = columns[:, m : m + 1]
+
+
+def shrink_kernel(factor, owned, me_ref, kept_ref, codes_ref, thresholds_ref, *refs):
+    buffers, values_out, cutoffs_ref = refs[:-2], refs[-2], refs[-1]
+    atom_count, width = codes_ref.shape
+    slabs, per, reach = atom_count // owned, width // LANES, width // LANES
+    spread(thresholds_ref, cutoffs_ref)
+    each = LANES // owned
+    pieces = [kept_at(piece, slabs, per) for piece in range((2 * per - 1) * each)]
+    pieces = [kept_ref[slab, :, lane] for slab, lane in pieces]
+    frames = windows_of([jnp.concatenate(pieces[i : i + each], axis=0) for i in range(0, len(pieces), each)], 0, width)
+    each = slabs // len(buffers)
+    for i, ref in enumerate(buffers):
+        for places in batches(each, owned):
+            there = rows_at(me_ref[0], i * each, places, owned, slabs)
+            value = jnp.concatenate([codes_ref[own, :] for own in there], axis=0).astype(F32)
+            cutoff = jnp.concatenate([cutoffs_ref[own, :] for own in there], axis=0)
+            value += (CODE_STEP * factor) * dot(atoms_at(ref, places, owned, reach), frames, ((1,), (0,)))
+            first = (i * each + places[0]) * owned
+            values_out[first : first + value.shape[0], :] = soft(value, cutoff).astype(values_out.dtype)
+
+
+def third_kernel(factor, me_ref, sent_ref, other_ref, kept_ref, values_ref, thresholds_ref, *refs):
+    buffers = refs[:-8]
+    atoms_out, residual_out, codes_out, rows_ref, turned_rows_ref, hankel_ref, gradient_ref, cutoffs_ref = refs[-8:]
     owned, lag_count = atoms_out.shape
-    atom_count, width = codes_ref.shape
+    atom_count, width = values_ref.shape
     slabs, per, reach = atom_count // owned, width // LANES, lag_count // LANES
     me = me_ref[0]
     residual = whole_residual((sent_ref, other_ref))
     round_rows(residual, rows_ref)
     fill_hankel(rows_ref, turned_rows_ref, hankel_ref)
-    pieces = [kept_at(piece, slabs, per) for piece in range((2 * per - 1) * (LANES // owned))]
-    pieces = [kept_ref[slab, :, lane] for slab, lane in pieces]
-    blocks = [jnp.concatenate(pieces[i : i + LANES // owned], axis=0) for i in range(0, len(pieces), LANES // owned)]
-    frames = windows_of(blocks, 0, width), windows_of(hankel_ref, me, width)
-    each = slabs // buffers
-    for i in range(buffers):
+    spread(thresholds_ref, cutoffs_ref)
+    frames = windows_of(hankel_ref, me, width)
+    each = slabs // len(buffers)
+    for i, ref in enumerate(buffers):
         for places in batches(each, owned):
             there = rows_at(me, i * each, places, owned, slabs)
-            cutoff = CODE_STEP * jnp.concatenate([thresholds_ref[own, :] for own in there], axis=0)
-            value = jnp.concatenate([codes_ref[own, :] for own in there], axis=0).astype(F32)
-            for ref, frame in ((before_refs[i], frames[0]), (after_refs[i], frames[1])):
-                change = dot(atoms_at(ref, places, owned, reach), frame, ((1,), (0,)))
-                value = soft(value + (CODE_STEP * factor) * change, cutoff)
-            value = value.astype(BF16)
+            cutoff = jnp.concatenate([cutoffs_ref[own, :] for own in there], axis=0)
+            change = (CODE_STEP * factor) * dot(atoms_at(ref, places, owned, reach), frames, ((1,), (0,)))
+            first = (i * each + places[0]) * owned
+            value = soft(values_ref[first : first + change.shape[0], :].astype(F32) + change, cutoff).astype(BF16)
             for b, own in enumerate(there):
                 codes_out[own, :] = value[b * owned : (b + 1) * owned]
     gradient_ref[...] = jnp.zeros_like(gradient_ref)
@@ -330,21 +351,28 @@
         windows + sums,
         at, *first, dictionary, by_atom, own_thresholds, signal_rows,
     )
-    all_thresholds = thresholds.reshape(atom_count, 1)
+    all_thresholds = thresholds.reshape(-1, LANES)
+    cutoffs = pltpu.VMEM((atom_count, 1), F32)
     mine = jnp.concatenate(before)
     other = swapped(tied(mine, part), 2)
     before = [mine, other, swapped(mine, 1), swapped(other, 1)]
-    _, after, second = exchanged(taps, part, 1, {4: other})
+    (values,) = call(
+        functools.partial(shrink_kernel, factor, owned),
+        [jax.ShapeDtypeStruct((atom_count, width), F32)],
+        [cutoffs],
+        at, kept, codes, all_thresholds, *before,
+    )
+    _, after, second = exchanged(taps, part, 1, {4: other, 1: values})
     after = after + [swapped(buffer, 1) for buffer in after]
     atoms, residual, codes = call(
-        functools.partial(third_kernel, factor, len(after)),
+        functools.partial(third_kernel, factor),
         [
             atoms_shape,
             jax.ShapeDtypeStruct((per, LANES), F32),
             jax.ShapeDtypeStruct((atom_count, width), BF16),
         ],
-        windows,
-        at, *second, kept, codes, all_thresholds, *before, *after,
+        [*windows, cutoffs],
+        at, *second, kept, values, all_thresholds, *after,
     )
     return codes[None], atoms, residual.reshape(1, width)
 

time: 88.1 us -> 84.4 us (0.958)
  other arithmetic: 1.73 us -> 0.28 us
  Pallas kernels: 11.1 us -> 10 us
  waiting for transfers between devices: 53.5 us -> 52.5 us
    pallas_call x3 -> x4, Pallas kernels: 11.1 us -> 10 us  [call(): pl.pallas_call(kernel, out_shape=tuple(outs), in_specs=[pl.BlockSpec(memo...]
    ppermute x13, waiting for transfers between devices: 30.5 us -> 29.6 us  [swapped(): return lax.ppermute(block, 'tm', [(i, i ^ distance) for i in range(count)])]
  transfers between devices with their start and end apart: 14 -> 14, of which waited for: 10 -> 12; matrix products, arithmetic and copies ran while one was open for 2% -> 0% of each run, Pallas kernels for 0% -> 1%
where the time goes in v5:
time: 84.4 us; the launch traced here: 84.2 us
  waiting for transfers between devices  52.5 us (62%)
  starting transfers between devices  20.3 us (24%)
  Pallas kernels  10 us (12%)
  between operations  0.86 us (1%)
    ppermute x13, waiting for transfers between devices, swapped(): return lax.ppermute(block, 'tm', [(i, i ^ distance) for i in range(count)])  29.6 us
    all_to_all x1, waiting for transfers between devices, on_device(): lax.all_to_all(codes.reshape(slabs, owned, width), 'tm', 0, 0, tiled=True)  22.9 us
    ppermute x13, starting transfers between devices, swapped(): return lax.ppermute(block, 'tm', [(i, i ^ distance) for i in range(count)])  12.7 us
    pallas_call x4, Pallas kernels, call(): pl.pallas_call(kernel, out_shape=tuple(outs), in_specs=[pl.BlockSpec(memo...  10 us
    all_to_all x1, starting transfers between devices, on_device(): lax.all_to_all(codes.reshape(slabs, owned, width), 'tm', 0, 0, tiled=True)  7.53 us
  transfers between devices with their start and end apart: 14, of which 12 were waited for; matrix products, arithmetic and copies ran while one was open for 0% of the time, Pallas kernels for 1%

profile of v5, /device:TPU:0, one launch (start us, length us, event | category | flops | bytes accessed | tf_op | source)
XLA Modules:
  0.0 84.2 jit_solution(10205926947955464448)
XLA Ops:
  0.6 0.0 copy-start.1
  0.6 0.0 copy-start.3
  0.7 0.0 copy-start.2
  0.7 7.5 %all-to-all-start = ((bf16[16,64,512]{2,1,0:T(8,128)(2,1)}), bf16[16,64,512]{2,1,0:T(8,128)(2,1)S(1)}, u32[]{:S(2)}, u32[]{:S(2)}) async-start(bf16[16,64,512]{2,1,0:T(8,128)(2,1)} %bitcast.9), calls=%async_computation | async-start | bytes 2097152 | tf_op jit(solution)/shard_map/all_to_all | solution.py:331
  8.2 22.9 %all-to-all-done.codes_ref = bf16[16,64,512]{2,1,0:T(8,128)(2,1)S(1)} async-done(((bf16[16,64,512]{2,1,0:T(8,128)(2,1)}), bf16[16,64,512]{2,1,0:T(8,128)(2,1)S(1)}, u32[]{:S(2)}, u32[]{:S(2)}) %all-to-all-start) | async-done | bytes 1048608 | tf_op jit(solution)/shard_map/all_to_all | solution.py:331
  31.1 0.0 copy-done.1
  31.1 0.0 copy-done.3
  31.1 1.4 %shard_map.67 = (bf16[256,128]{1,0:T(8,128)(2,1)S(1)}, f32[64,128]{1,0:T(8,128)S(1)}) custom-call(s32[1]{0:T(128)} %bitcast.me_ref, f32[64,512]{1,0:T(8,128)S(1)} %copy-done.1, bf16[16,64,512]{2,1,0:T(8,128)(2,1)S(1)} %all-to-all-done.codes_ref, f32[4,128]{1,0:T(4,128)S(1)} %bitcast.13), custom_call_target="tpu_custom_call" | custom-call | tf_op jit(solution)/shard_map/pallas_call | solution.py:275
  32.6 5.1 %collective-permute-start = (bf16[384,128]{1,0:T(8,128)(2,1)S(1)}, bf16[384,128]{1,0:T(8,128)(2,1)S(1)}, u32[]{:S(2)}, u32[]{:S(2)}) collective-permute-start(bf16[384,128]{1,0:T(8,128)(2,1)S(1)} %pad_maximum_fusion.4), channel_id=1, source_target_pairs={{0,8},{1,9},{2,10},{3,11},{4,12},{5,13},{6,14},{7,15},{8,0},{9,1},... | collective-permute-start | bytes 294920 | tf_op jit(solution)/shard_map/ppermute | solution.py:287
  37.7 4.7 %collective-permute-done = bf16[384,128]{1,0:T(8,128)(2,1)S(1)} collective-permute-done((bf16[384,128]{1,0:T(8,128)(2,1)S(1)}, bf16[384,128]{1,0:T(8,128)(2,1)S(1)}, u32[]{:S(2)}, u32[]{:S(2)}) %collective-permute-start) | collective-permute-done | bytes 98336 | tf_op jit(solution)/shard_map/ppermute | solution.py:287
  42.5 0.1 collective-permute-start.1
  42.6 5.3 %collective-permute-done.1 = bf16[640,128]{1,0:T(8,128)(2,1)S(1)} collective-permute-done((bf16[640,128]{1,0:T(8,128)(2,1)S(1)}, bf16[640,128]{1,0:T(8,128)(2,1)S(1)}, u32[]{:S(2)}, u32[]{:S(2)}) %collective-permute-start.1) | collective-permute-done | bytes 163872 | tf_op jit(solution)/shard_map/ppermute | solution.py:287
  47.9 0.1 collective-permute-start.2
  48.0 3.9 %collective-permute-done.2 = bf16[128,128]{1,0:T(8,128)(2,1)S(1)} collective-permute-done((bf16[128,128]{1,0:T(8,128)(2,1)S(1)}, bf16[128,128]{1,0:T(8,128)(2,1)S(1)}, u32[]{:S(2)}, u32[]{:S(2)}) %collective-permute-start.2) | collective-permute-done | bytes 32800 | tf_op jit(solution)/shard_map/ppermute | solution.py:287
  51.9 0.1 collective-permute-start.3
  52.0 0.0 copy-done.2
  52.0 0.1 dynamic-slice_bitcast_fusion
  52.1 0.1 copy.7.thresholds_ref
  52.2 0.0 copy-start
  52.2 1.0 %collective-permute-done.3.other_ref = bf16[128,128]{1,0:T(8,128)(2,1)S(1)} collective-permute-done((bf16[128,128]{1,0:T(8,128)(2,1)S(1)}, bf16[128,128]{1,0:T(8,128)(2,1)S(1)}, u32[]{:S(2)}, u32[]{:S(2)}) %collective-permute-start.3) | collective-permute-done | bytes 32800 | tf_op jit(solution)/shard_map/ppermute | solution.py:287
  53.2 3.4 %shard_map.68 = (bf16[256,128]{1,0:T(8,128)(2,1)S(1)}, bf16[23,64,512]{2,1,0:T(8,128)(2,1)S(1)}, f32[64,128]{1,0:T(8,128)S(1)}) custom-call(s32[1]{0:T(128)} %bitcast.me_ref, bf16[128,128]{1,0:T(8,128)(2,1)S(1)} %pad_maximum_fusion.7.sent_ref, bf16[128,128]{1,0:T(8,128)(2,1)S(1)} %collective-permute-done.3.other_ref, f32[64,512]{1,0:T(8,128)S(1)} %copy-done.1, ...), custom_call_target="tpu_custom_call" | custom-call | tf_op jit(solution)/shard_map/pallas_call | solution.py:275
  56.6 0.9 %collective-permute-start.4 = (bf16[384,128]{1,0:T(8,128)(2,1)S(1)}, bf16[384,128]{1,0:T(8,128)(2,1)S(1)}, u32[]{:S(2)}, u32[]{:S(2)}) collective-permute-start(bf16[384,128]{1,0:T(8,128)(2,1)S(1)} %pad_maximum_fusion.5), channel_id=1, source_target_pairs={{0,8},{1,9},{2,10},{3,11},{4,12},{5,13},{6,14},{7,15},{8,0},{9,1},... | collective-permute-start | bytes 294920 | tf_op jit(solution)/shard_map/ppermute | solution.py:287
  57.5 1.9 %collective-permute-start.5 = (bf16[1024,128]{1,0:T(8,128)(2,1)S(1)}, bf16[1024,128]{1,0:T(8,128)(2,1)S(1)}, u32[]{:S(2)}, u32[]{:S(2)}) collective-permute-start(bf16[1024,128]{1,0:T(8,128)(2,1)S(1)} %pad_maximum_fusion.1.refs_0_), channel_id=1, source_target_pairs={{0,2},{1,3},{2,0},{3,1},{4,6},{5,7},{6,4},{7,5},{8,10},{9,11},{10,... | collective-permute-start | bytes 786440 | tf_op jit(solution)/shard_map/ppermute | solution.py:287
  59.4 5.1 %collective-permute-done.4 = bf16[384,128]{1,0:T(8,128)(2,1)S(1)} collective-permute-done((bf16[384,128]{1,0:T(8,128)(2,1)S(1)}, bf16[384,128]{1,0:T(8,128)(2,1)S(1)}, u32[]{:S(2)}, u32[]{:S(2)}) %collective-permute-start.4) | collective-permute-done | bytes 98336 | tf_op jit(solution)/shard_map/ppermute | solution.py:287
  64.6 1.2 %collective-permute-done.5.refs_1_ = bf16[1024,128]{1,0:T(8,128)(2,1)S(1)} collective-permute-done((bf16[1024,128]{1,0:T(8,128)(2,1)S(1)}, bf16[1024,128]{1,0:T(8,128)(2,1)S(1)}, u32[]{:S(2)}, u32[]{:S(2)}) %collective-permute-start.5) | collective-permute-done | bytes 262176 | tf_op jit(solution)/shard_map/ppermute | solution.py:287
  65.8 1.7 %collective-permute-start.6 = (bf16[640,128]{1,0:T(8,128)(2,1)S(1)}, bf16[640,128]{1,0:T(8,128)(2,1)S(1)}, u32[]{:S(2)}, u32[]{:S(2)}) collective-permute-start(bf16[640,128]{1,0:T(8,128)(2,1)S(1)} %pad_maximum_fusion.3), channel_id=1, source_target_pairs={{0,4},{1,5},{2,6},{3,7},{4,0},{5,1},{6,2},{7,3},{8,12},{9,13},{10,... | collective-permute-start | bytes 491528 | tf_op jit(solution)/shard_map/ppermute | solution.py:287
  67.5 3.6 %collective-permute-done.6 = bf16[640,128]{1,0:T(8,128)(2,1)S(1)} collective-permute-done((bf16[640,128]{1,0:T(8,128)(2,1)S(1)}, bf16[640,128]{1,0:T(8,128)(2,1)S(1)}, u32[]{:S(2)}, u32[]{:S(2)}) %collective-permute-start.6) | collective-permute-done | bytes 163872 | tf_op jit(solution)/shard_map/ppermute | solution.py:287
  71.2 1.8 %collective-permute-start.7 = (bf16[1152,128]{1,0:T(8,128)(2,1)S(1)}, bf16[1152,128]{1,0:T(8,128)(2,1)S(1)}, u32[]{:S(2)}, u32[]{:S(2)}) collective-permute-start(bf16[1152,128]{1,0:T(8,128)(2,1)S(1)} %pad_maximum_fusion.refs_0_), channel_id=1, source_target_pairs={{0,2},{1,3},{2,0},{3,1},{4,6},{5,7},{6,4},{7,5},{8,10},{9,11},{10,... | collective-permute-start | bytes 884744 | tf_op jit(solution)/shard_map/ppermute | solution.py:287
  73.0 0.0 collective-permute-start.8
  73.0 0.5 collective-permute-start.9
  73.5 0.0 collective-permute-start.11
  73.5 1.0 %collective-permute-done.8.refs_2_ = bf16[1024,128]{1,0:T(8,128)(2,1)S(1)} collective-permute-done((bf16[1024,128]{1,0:T(8,128)(2,1)S(1)}, bf16[1024,128]{1,0:T(8,128)(2,1)S(1)}, u32[]{:S(2)}, u32[]{:S(2)}) %collective-permute-start.8) | collective-permute-done | bytes 262176 | tf_op jit(solution)/shard_map/ppermute | solution.py:287
  74.5 0.4 collective-permute-done.9.refs_3_
  74.9 0.0 copy-done
  74.9 0.9 %shard_map.69.values_ref = f32[1024,512]{1,0:T(8,128)S(1)} custom-call(s32[1]{0:T(128)} %bitcast.me_ref, bf16[23,64,512]{2,1,0:T(8,128)(2,1)S(1)} %get-tuple-element.20.kept_ref, bf16[1024,512]{1,0:T(8,128)(2,1)S(1)} %bitcast.10, f32[8,128]{1,0:T(8,128)S(1)} %bitcast.11, bf16[1024,128]{1,0:T(8,128)(2,1)S(1)} %pad_maximum_fusion.1.refs_0_, ...), custom_call_target="tpu_custom_call" | custom-call | tf_op jit(solution)/shard_map/pallas_call | solution.py:275
  75.8 2.4 %collective-permute-done.7.refs_1_ = bf16[1152,128]{1,0:T(8,128)(2,1)S(1)} collective-permute-done((bf16[1152,128]{1,0:T(8,128)(2,1)S(1)}, bf16[1152,128]{1,0:T(8,128)(2,1)S(1)}, u32[]{:S(2)}, u32[]{:S(2)}) %collective-permute-start.7) | collective-permute-done | bytes 294944 | tf_op jit(solution)/shard_map/ppermute | solution.py:287
  78.2 0.0 collective-permute-start.12
  78.3 0.6 collective-permute-start.10
  78.9 0.0 collective-permute-done.11.refs_2_
  78.9 1.0 %collective-permute-done.10.other_ref = bf16[128,128]{1,0:T(8,128)(2,1)S(1)} collective-permute-done((bf16[128,128]{1,0:T(8,128)(2,1)S(1)}, bf16[128,128]{1,0:T(8,128)(2,1)S(1)}, u32[]{:S(2)}, u32[]{:S(2)}) %collective-permute-start.10) | collective-permute-done | bytes 32800 | tf_op jit(solution)/shard_map/ppermute | solution.py:287
  79.9 0.0 collective-permute-done.12.refs_3_
  79.9 4.3 %shard_map.70 = (f32[64,512]{1,0:T(8,128)}, f32[4,128]{1,0:T(4,128)}, bf16[1024,512]{1,0:T(8,128)(2,1)}) custom-call(s32[1]{0:T(128)} %bitcast.me_ref, bf16[128,128]{1,0:T(8,128)(2,1)S(1)} %pad_maximum_fusion.8.sent_ref, bf16[128,128]{1,0:T(8,128)(2,1)S(1)} %collective-permute-done.10.other_ref, bf16[23,64,512]{2,1,0:T(8,128)(2,1)S(1)} %get-tuple-element.20.kept_ref, ...), custom_call_target="tpu_custom_call" | custom-call | tf_op jit(solution)/shard_map/pallas_call | solution.py:275
  (24 shorter events, 0.3 us)
Async XLA Ops:
  0.6 30.5 %copy-start.1 = (f32[64,512]{1,0:T(8,128)S(1)}, f32[64,512]{1,0:T(8,128)}, u32[]{:S(2)}) copy-start(f32[64,512]{1,0:T(8,128)} %atoms_ref.3) | copy-start | bytes 393220
  0.6 30.5 %copy-start.3 = (f32[1,512]{1,0:T(1,128)S(1)}, f32[1,512]{1,0:T(1,128)}, u32[]{:S(2)}) copy-start(f32[1,512]{1,0:T(1,128)} %param.4) | copy-start | bytes 6148
  0.7 51.4 %copy-start.2 = (f32[1024]{0:T(1024)S(1)}, f32[1024]{0:T(1024)}, u32[]{:S(2)}) copy-start(f32[1024]{0:T(1024)} %param.7) | copy-start | bytes 12292
  0.7 30.5 %all-to-all-start = ((bf16[16,64,512]{2,1,0:T(8,128)(2,1)}), bf16[16,64,512]{2,1,0:T(8,128)(2,1)S(1)}, u32[]{:S(2)}, u32[]{:S(2)}) async-start(bf16[16,64,512]{2,1,0:T(8,128)(2,1)} %bitcast.9), calls=%async_computation | async-start | bytes 2097152 | tf_op jit(solution)/shard_map/all_to_all | solution.py:331
  32.6 9.8 %collective-permute-start = (bf16[384,128]{1,0:T(8,128)(2,1)S(1)}, bf16[384,128]{1,0:T(8,128)(2,1)S(1)}, u32[]{:S(2)}, u32[]{:S(2)}) collective-permute-start(bf16[384,128]{1,0:T(8,128)(2,1)S(1)} %pad_maximum_fusion.4), channel_id=1, source_target_pairs={{0,8},{1,9},{2,10},{3,11},{4,12},{5,13},{6,14},{7,15},{8,0},{9,1},... | collective-permute-start | bytes 294920 | tf_op jit(solution)/shard_map/ppermute | solution.py:287
  42.5 5.4 %collective-permute-start.1 = (bf16[640,128]{1,0:T(8,128)(2,1)S(1)}, bf16[640,128]{1,0:T(8,128)(2,1)S(1)}, u32[]{:S(2)}, u32[]{:S(2)}) collective-permute-start(bf16[640,128]{1,0:T(8,128)(2,1)S(1)} %pad_maximum_fusion.2), channel_id=1, source_target_pairs={{0,4},{1,5},{2,6},{3,7},{4,0},{5,1},{6,2},{7,3},{8,12},{9,13},{10,... | collective-permute-start | bytes 491528 | tf_op jit(solution)/shard_map/ppermute | solution.py:287
  47.9 4.0 %collective-permute-start.2 = (bf16[128,128]{1,0:T(8,128)(2,1)S(1)}, bf16[128,128]{1,0:T(8,128)(2,1)S(1)}, u32[]{:S(2)}, u32[]{:S(2)}) collective-permute-start(bf16[128,128]{1,0:T(8,128)(2,1)S(1)} %pad_maximum_fusion.6), channel_id=1, source_target_pairs={{0,2},{1,3},{2,0},{3,1},{4,6},{5,7},{6,4},{7,5},{8,10},{9,11},{10,... | collective-permute-start | bytes 98312 | tf_op jit(solution)/shard_map/ppermute | solution.py:287
  51.9 1.3 %collective-permute-start.3 = (bf16[128,128]{1,0:T(8,128)(2,1)S(1)}, bf16[128,128]{1,0:T(8,128)(2,1)S(1)}, u32[]{:S(2)}, u32[]{:S(2)}) collective-permute-start(bf16[128,128]{1,0:T(8,128)(2,1)S(1)} %pad_maximum_fusion.7.sent_ref), channel_id=1, source_target_pairs={{0,1},{1,0},{2,3},{3,2},{4,5},{5,4},{6,7},{7,6},{8,9},{9,8},{10,11... | collective-permute-start | bytes 98312 | tf_op jit(solution)/shard_map/ppermute | solution.py:287
  52.2 22.7 %copy-start = (bf16[1,1024,512]{2,1,0:T(8,128)(2,1)S(1)}, bf16[1,1024,512]{2,1,0:T(8,128)(2,1)}, u32[]{:S(2)}) copy-start(bf16[1,1024,512]{2,1,0:T(8,128)(2,1)} %param.5) | copy-start | bytes 3145732
  56.6 7.9 %collective-permute-start.4 = (bf16[384,128]{1,0:T(8,128)(2,1)S(1)}, bf16[384,128]{1,0:T(8,128)(2,1)S(1)}, u32[]{:S(2)}, u32[]{:S(2)}) collective-permute-start(bf16[384,128]{1,0:T(8,128)(2,1)S(1)} %pad_maximum_fusion.5), channel_id=1, source_target_pairs={{0,8},{1,9},{2,10},{3,11},{4,12},{5,13},{6,14},{7,15},{8,0},{9,1},... | collective-permute-start | bytes 294920 | tf_op jit(solution)/shard_map/ppermute | solution.py:287
  57.5 8.2 %collective-permute-start.5 = (bf16[1024,128]{1,0:T(8,128)(2,1)S(1)}, bf16[1024,128]{1,0:T(8,128)(2,1)S(1)}, u32[]{:S(2)}, u32[]{:S(2)}) collective-permute-start(bf16[1024,128]{1,0:T(8,128)(2,1)S(1)} %pad_maximum_fusion.1.refs_0_), channel_id=1, source_target_pairs={{0,2},{1,3},{2,0},{3,1},{4,6},{5,7},{6,4},{7,5},{8,10},{9,11},{10,... | collective-permute-start | bytes 786440 | tf_op jit(solution)/shard_map/ppermute | solution.py:287
  65.8 5.3 %collective-permute-start.6 = (bf16[640,128]{1,0:T(8,128)(2,1)S(1)}, bf16[640,128]{1,0:T(8,128)(2,1)S(1)}, u32[]{:S(2)}, u32[]{:S(2)}) collective-permute-start(bf16[640,128]{1,0:T(8,128)(2,1)S(1)} %pad_maximum_fusion.3), channel_id=1, source_target_pairs={{0,4},{1,5},{2,6},{3,7},{4,0},{5,1},{6,2},{7,3},{8,12},{9,13},{10,... | collective-permute-start | bytes 491528 | tf_op jit(solution)/shard_map/ppermute | solution.py:287
  71.2 7.0 %collective-permute-start.7 = (bf16[1152,128]{1,0:T(8,128)(2,1)S(1)}, bf16[1152,128]{1,0:T(8,128)(2,1)S(1)}, u32[]{:S(2)}, u32[]{:S(2)}) collective-permute-start(bf16[1152,128]{1,0:T(8,128)(2,1)S(1)} %pad_maximum_fusion.refs_0_), channel_id=1, source_target_pairs={{0,2},{1,3},{2,0},{3,1},{4,6},{5,7},{6,4},{7,5},{8,10},{9,11},{10,... | collective-permute-start | bytes 884744 | tf_op jit(solution)/shard_map/ppermute | solution.py:287
  73.0 1.5 %collective-permute-start.8 = (bf16[1024,128]{1,0:T(8,128)(2,1)S(1)}, bf16[1024,128]{1,0:T(8,128)(2,1)S(1)}, u32[]{:S(2)}, u32[]{:S(2)}) collective-permute-start(bf16[1024,128]{1,0:T(8,128)(2,1)S(1)} %pad_maximum_fusion.1.refs_0_), channel_id=1, source_target_pairs={{0,1},{1,0},{2,3},{3,2},{4,5},{5,4},{6,7},{7,6},{8,9},{9,8},{10,11... | collective-permute-start | bytes 786440 | tf_op jit(solution)/shard_map/ppermute | solution.py:287
  73.0 1.9 %collective-permute-start.9 = (bf16[1024,128]{1,0:T(8,128)(2,1)S(1)}, bf16[1024,128]{1,0:T(8,128)(2,1)S(1)}, u32[]{:S(2)}, u32[]{:S(2)}) collective-permute-start(bf16[1024,128]{1,0:T(8,128)(2,1)S(1)} %collective-permute-done.5.refs_1_), channel_id=1, source_target_pairs={{0,1},{1,0},{2,3},{3,2},{4,5},{5,4},{6,7},{7,6},{8,9},{9,8},{10,11... | collective-permute-start | bytes 786440 | tf_op jit(solution)/shard_map/ppermute | solution.py:287
  73.5 5.4 %collective-permute-start.11 = (bf16[1152,128]{1,0:T(8,128)(2,1)S(1)}, bf16[1152,128]{1,0:T(8,128)(2,1)S(1)}, u32[]{:S(2)}, u32[]{:S(2)}) collective-permute-start(bf16[1152,128]{1,0:T(8,128)(2,1)S(1)} %pad_maximum_fusion.refs_0_), channel_id=1, source_target_pairs={{0,1},{1,0},{2,3},{3,2},{4,5},{5,4},{6,7},{7,6},{8,9},{9,8},{10,11... | collective-permute-start | bytes 884744 | tf_op jit(solution)/shard_map/ppermute | solution.py:287
  78.2 1.6 %collective-permute-start.12 = (bf16[1152,128]{1,0:T(8,128)(2,1)S(1)}, bf16[1152,128]{1,0:T(8,128)(2,1)S(1)}, u32[]{:S(2)}, u32[]{:S(2)}) collective-permute-start(bf16[1152,128]{1,0:T(8,128)(2,1)S(1)} %collective-permute-done.7.refs_1_), channel_id=1, source_target_pairs={{0,1},{1,0},{2,3},{3,2},{4,5},{5,4},{6,7},{7,6},{8,9},{9,8},{10,11... | collective-permute-start | bytes 884744 | tf_op jit(solution)/shard_map/ppermute | solution.py:287
  78.3 1.6 %collective-permute-start.10 = (bf16[128,128]{1,0:T(8,128)(2,1)S(1)}, bf16[128,128]{1,0:T(8,128)(2,1)S(1)}, u32[]{:S(2)}, u32[]{:S(2)}) collective-permute-start(bf16[128,128]{1,0:T(8,128)(2,1)S(1)} %pad_maximum_fusion.8.sent_ref), channel_id=1, source_target_pairs={{0,1},{1,0},{2,3},{3,2},{4,5},{5,4},{6,7},{7,6},{8,9},{9,8},{10,11... | collective-permute-start | bytes 98312 | tf_op jit(solution)/shard_map/ppermute | solution.py:287

commit v6 on v5

--- a/solution.py
+++ b/solution.py
@@ -34,10 +34,8 @@
     return lax.broadcasted_iota(jnp.int32, shape, 0), lax.broadcasted_iota(jnp.int32, shape, 1)
 
 
-def fill_hankel(rows_ref, turned_ref, hankel_ref):
-    count = hankel_ref.shape[0]
+def turn_rows(rows_ref, turned_ref, count):
     q = lax.broadcasted_iota(jnp.int32, (8, LANES), 0)
-    v = lax.broadcasted_iota(jnp.int32, (8, LANES), 1)
 
     def turn(m):
         group = jnp.broadcast_to(rows_ref[pl.ds(m, 1), :], (8, LANES))
@@ -45,21 +43,33 @@
             group = jnp.where((q & bit) != 0, pltpu.roll(group, LANES - bit, 1), group)
         turned_ref[m] = group
 
-    repeat(count + 1, turn)
+    repeat(count, turn)
+
+
+def fill_hankel(turned_ref, hankel_ref, first, count):
+    q = lax.broadcasted_iota(jnp.int32, (8, LANES), 0)
+    v = lax.broadcasted_iota(jnp.int32, (8, LANES), 1)
     for a in range(0, LANES, 16):
         keeps = [q + v + (a + b) < LANES for b in (0, 8)]
 
         def groups(m):
             group = turned_ref[m]
-            return tuple(pltpu.roll(group, LANES - a - b, 1) if a + b else group for b in (0, 8))
-
-        def place(m, here):
+            return [pltpu.roll(group, LANES - a - b, 1) if a + b else group for b in (0, 8)]
+
+        here = groups(first)
+        for m in range(first, first + count):
             after = groups(m + 1)
             pair = [jnp.where(keep, old, new) for keep, old, new in zip(keeps, here, after)]
             hankel_ref[m, a : a + 16, :] = jnp.concatenate(pair, axis=0).astype(BF16)
-            return after
-
-        repeat(count, place, groups(0))
+            here = after
+
+
+def over_slabs(turned_ref, hankel_ref, slabs, per, body):
+    fill_hankel(turned_ref, hankel_ref, 0, 2 * per - 1)
+    for n in range(slabs):
+        if n + 1 < slabs:
+            fill_hankel(turned_ref, hankel_ref, (n + 2) * per - 1, per)
+        body(n)
 
 
 def windows_of(hankel_ref, slab, width):
@@ -162,12 +172,7 @@
     slabs, owned, width = codes_ref.shape
     per = width // LANES
     round_rows(whole_residual((sent_ref, other_ref)), rows_ref)
-    fill_hankel(rows_ref, turned_rows_ref, hankel_ref)
-    for m in range(2 * per - 1):
-        block = hankel_ref[me_ref[0] * per + m]
-        for h in range(LANES // owned):
-            slab, lane = kept_at(m * (LANES // owned) + h, slabs, per)
-            codes_out[slab, :, lane] = block[h * owned : (h + 1) * owned, :]
+    turn_rows(rows_ref, turned_rows_ref, hankel_ref.shape[0] + 1)
     atoms = atoms_ref[...]
     atoms_b = atoms.astype(BF16)
     cutoff = CODE_STEP * thresholds_ref[...]
@@ -182,7 +187,12 @@
         value = code.astype(F32) + (CODE_STEP * factor) * both[:owned]
         codes_out[n + 1] = soft(value, cutoff).astype(BF16)
 
-    repeat(slabs, body)
+    over_slabs(turned_rows_ref, hankel_ref, slabs, per, body)
+    for m in range(2 * per - 1):
+        block = hankel_ref[me_ref[0] * per + m]
+        for h in range(LANES // owned):
+            slab, lane = kept_at(m * (LANES // owned) + h, slabs, per)
+            codes_out[slab, :, lane] = block[h * owned : (h + 1) * owned, :]
     after = normalised(atoms + factor * gradient_ref[...])
     after_b = after.astype(BF16)
     codes_out[slabs + 1] = after_b
@@ -244,8 +254,18 @@
     me = me_ref[0]
     residual = whole_residual((sent_ref, other_ref))
     round_rows(residual, rows_ref)
-    fill_hankel(rows_ref, turned_rows_ref, hankel_ref)
+    turn_rows(rows_ref, turned_rows_ref, hankel_ref.shape[0] + 1)
     spread(thresholds_ref, cutoffs_ref)
+    gradient_ref[...] = jnp.zeros_like(gradient_ref)
+
+    def body(n):
+        gradient_ref[...] += dot(kept_ref[n + 1], windows_of(hankel_ref, n, width), ((1,), (0,)))
+
+    over_slabs(turned_rows_ref, hankel_ref, slabs, per, body)
+    atoms = kept_ref[slabs + 1].astype(F32) + kept_ref[slabs + 2].astype(F32)
+    atoms_out[...] = normalised(atoms + factor * gradient_ref[...])
+    rows_ref[: slabs * per, :] = residual
+    residual_out[...] = rows_ref[pl.ds(me * per, per), :]
     frames = windows_of(hankel_ref, me, width)
     each = slabs // len(buffers)
     for i, ref in enumerate(buffers):
@@ -257,16 +277,6 @@
             value = soft(values_ref[first : first + change.shape[0], :].astype(F32) + change, cutoff).astype(BF16)
             for b, own in enumerate(there):
                 codes_out[own, :] = value[b * owned : (b + 1) * owned]
-    gradient_ref[...] = jnp.zeros_like(gradient_ref)
-
-    def body(n):
-        gradient_ref[...] += dot(kept_ref[n + 1], windows_of(hankel_ref, n, width), ((1,), (0,)))
-
-    repeat(slabs, body)
-    atoms = kept_ref[slabs + 1].astype(F32) + kept_ref[slabs + 2].astype(F32)
-    atoms_out[...] = normalised(atoms + factor * gradient_ref[...])
-    rows_ref[: slabs * per, :] = residual
-    residual_out[...] = rows_ref[pl.ds(me * per, per), :]
 
 
 def call(kernel, outs, scratch, *args):

time: 84.4 us -> 83.8 us (level)
  no operation moved by 1% of the time
where the time goes in v6:
time: 83.8 us; the launch traced here: 83.6 us
  waiting for transfers between devices  52.6 us (63%)
  starting transfers between devices  20.3 us (24%)
  Pallas kernels  9.44 us (11%)
  between operations  0.86 us (1%)
    ppermute x13, waiting for transfers between devices, swapped(): return lax.ppermute(block, 'tm', [(i, i ^ distance) for i in range(count)])  29.6 us
    all_to_all x1, waiting for transfers between devices, on_device(): lax.all_to_all(codes.reshape(slabs, owned, width), 'tm', 0, 0, tiled=True)  22.9 us
    ppermute x13, starting transfers between devices, swapped(): return lax.ppermute(block, 'tm', [(i, i ^ distance) for i in range(count)])  12.7 us
    pallas_call x4, Pallas kernels, call(): pl.pallas_call(kernel, out_shape=tuple(outs), in_specs=[pl.BlockSpec(memo...  9.44 us
    all_to_all x1, starting transfers between devices, on_device(): lax.all_to_all(codes.reshape(slabs, owned, width), 'tm', 0, 0, tiled=True)  7.53 us
  transfers between devices with their start and end apart: 14, of which 12 were waited for; matrix products, arithmetic and copies ran while one was open for 0% of the time, Pallas kernels for 1%

profile of v6, /device:TPU:0, one launch (start us, length us, event | category | flops | bytes accessed | tf_op | source)
XLA Modules:
  0.0 83.6 jit_solution(5632621444525109586)
XLA Ops:
  0.6 0.0 copy-start.1
  0.6 0.0 copy-start.3
  0.7 0.0 copy-start.2
  0.7 7.5 %all-to-all-start = ((bf16[16,64,512]{2,1,0:T(8,128)(2,1)}), bf16[16,64,512]{2,1,0:T(8,128)(2,1)S(1)}, u32[]{:S(2)}, u32[]{:S(2)}) async-start(bf16[16,64,512]{2,1,0:T(8,128)(2,1)} %bitcast.9), calls=%async_computation | async-start | bytes 2097152 | tf_op jit(solution)/shard_map/all_to_all | solution.py:341
  8.2 22.9 %all-to-all-done.codes_ref = bf16[16,64,512]{2,1,0:T(8,128)(2,1)S(1)} async-done(((bf16[16,64,512]{2,1,0:T(8,128)(2,1)}), bf16[16,64,512]{2,1,0:T(8,128)(2,1)S(1)}, u32[]{:S(2)}, u32[]{:S(2)}) %all-to-all-start) | async-done | bytes 1048608 | tf_op jit(solution)/shard_map/all_to_all | solution.py:341
  31.1 0.0 copy-done.1
  31.1 0.0 copy-done.3
  31.1 1.4 %shard_map.67 = (bf16[256,128]{1,0:T(8,128)(2,1)S(1)}, f32[64,128]{1,0:T(8,128)S(1)}) custom-call(s32[1]{0:T(128)} %bitcast.me_ref, f32[64,512]{1,0:T(8,128)S(1)} %copy-done.1, bf16[16,64,512]{2,1,0:T(8,128)(2,1)S(1)} %all-to-all-done.codes_ref, f32[4,128]{1,0:T(4,128)S(1)} %bitcast.13), custom_call_target="tpu_custom_call" | custom-call | tf_op jit(solution)/shard_map/pallas_call | solution.py:285
  32.6 5.1 %collective-permute-start = (bf16[384,128]{1,0:T(8,128)(2,1)S(1)}, bf16[384,128]{1,0:T(8,128)(2,1)S(1)}, u32[]{:S(2)}, u32[]{:S(2)}) collective-permute-start(bf16[384,128]{1,0:T(8,128)(2,1)S(1)} %pad_maximum_fusion.4), channel_id=1, source_target_pairs={{0,8},{1,9},{2,10},{3,11},{4,12},{5,13},{6,14},{7,15},{8,0},{9,1},... | collective-permute-start | bytes 294920 | tf_op jit(solution)/shard_map/ppermute | solution.py:297
  37.7 4.7 %collective-permute-done = bf16[384,128]{1,0:T(8,128)(2,1)S(1)} collective-permute-done((bf16[384,128]{1,0:T(8,128)(2,1)S(1)}, bf16[384,128]{1,0:T(8,128)(2,1)S(1)}, u32[]{:S(2)}, u32[]{:S(2)}) %collective-permute-start) | collective-permute-done | bytes 98336 | tf_op jit(solution)/shard_map/ppermute | solution.py:297
  42.5 0.1 collective-permute-start.1
  42.6 5.3 %collective-permute-done.1 = bf16[640,128]{1,0:T(8,128)(2,1)S(1)} collective-permute-done((bf16[640,128]{1,0:T(8,128)(2,1)S(1)}, bf16[640,128]{1,0:T(8,128)(2,1)S(1)}, u32[]{:S(2)}, u32[]{:S(2)}) %collective-permute-start.1) | collective-permute-done | bytes 163872 | tf_op jit(solution)/shard_map/ppermute | solution.py:297
  47.9 0.1 collective-permute-start.2
  48.0 3.9 %collective-permute-done.2 = bf16[128,128]{1,0:T(8,128)(2,1)S(1)} collective-permute-done((bf16[128,128]{1,0:T(8,128)(2,1)S(1)}, bf16[128,128]{1,0:T(8,128)(2,1)S(1)}, u32[]{:S(2)}, u32[]{:S(2)}) %collective-permute-start.2) | collective-permute-done | bytes 32800 | tf_op jit(solution)/shard_map/ppermute | solution.py:297
  51.9 0.1 collective-permute-start.3
  52.0 0.0 copy-done.2
  52.0 0.1 dynamic-slice_bitcast_fusion
  52.1 0.1 copy.7.thresholds_ref
  52.2 0.0 copy-start
  52.2 1.0 %collective-permute-done.3.other_ref = bf16[128,128]{1,0:T(8,128)(2,1)S(1)} collective-permute-done((bf16[128,128]{1,0:T(8,128)(2,1)S(1)}, bf16[128,128]{1,0:T(8,128)(2,1)S(1)}, u32[]{:S(2)}, u32[]{:S(2)}) %collective-permute-start.3) | collective-permute-done | bytes 32800 | tf_op jit(solution)/shard_map/ppermute | solution.py:297
  53.2 3.3 %shard_map.68 = (bf16[256,128]{1,0:T(8,128)(2,1)S(1)}, bf16[23,64,512]{2,1,0:T(8,128)(2,1)S(1)}, f32[64,128]{1,0:T(8,128)S(1)}) custom-call(s32[1]{0:T(128)} %bitcast.me_ref, bf16[128,128]{1,0:T(8,128)(2,1)S(1)} %pad_maximum_fusion.7.sent_ref, bf16[128,128]{1,0:T(8,128)(2,1)S(1)} %collective-permute-done.3.other_ref, f32[64,512]{1,0:T(8,128)S(1)} %copy-done.1, ...), custom_call_target="tpu_custom_call" | custom-call | tf_op jit(solution)/shard_map/pallas_call | solution.py:285
  56.6 0.9 %collective-permute-start.4 = (bf16[384,128]{1,0:T(8,128)(2,1)S(1)}, bf16[384,128]{1,0:T(8,128)(2,1)S(1)}, u32[]{:S(2)}, u32[]{:S(2)}) collective-permute-start(bf16[384,128]{1,0:T(8,128)(2,1)S(1)} %pad_maximum_fusion.5), channel_id=1, source_target_pairs={{0,8},{1,9},{2,10},{3,11},{4,12},{5,13},{6,14},{7,15},{8,0},{9,1},... | collective-permute-start | bytes 294920 | tf_op jit(solution)/shard_map/ppermute | solution.py:297
  57.5 1.9 %collective-permute-start.5 = (bf16[1024,128]{1,0:T(8,128)(2,1)S(1)}, bf16[1024,128]{1,0:T(8,128)(2,1)S(1)}, u32[]{:S(2)}, u32[]{:S(2)}) collective-permute-start(bf16[1024,128]{1,0:T(8,128)(2,1)S(1)} %pad_maximum_fusion.1.refs_0_), channel_id=1, source_target_pairs={{0,2},{1,3},{2,0},{3,1},{4,6},{5,7},{6,4},{7,5},{8,10},{9,11},{10,... | collective-permute-start | bytes 786440 | tf_op jit(solution)/shard_map/ppermute | solution.py:297
  59.3 5.1 %collective-permute-done.4 = bf16[384,128]{1,0:T(8,128)(2,1)S(1)} collective-permute-done((bf16[384,128]{1,0:T(8,128)(2,1)S(1)}, bf16[384,128]{1,0:T(8,128)(2,1)S(1)}, u32[]{:S(2)}, u32[]{:S(2)}) %collective-permute-start.4) | collective-permute-done | bytes 98336 | tf_op jit(solution)/shard_map/ppermute | solution.py:297
  64.5 1.2 %collective-permute-done.5.refs_1_ = bf16[1024,128]{1,0:T(8,128)(2,1)S(1)} collective-permute-done((bf16[1024,128]{1,0:T(8,128)(2,1)S(1)}, bf16[1024,128]{1,0:T(8,128)(2,1)S(1)}, u32[]{:S(2)}, u32[]{:S(2)}) %collective-permute-start.5) | collective-permute-done | bytes 262176 | tf_op jit(solution)/shard_map/ppermute | solution.py:297
  65.7 1.7 %collective-permute-start.6 = (bf16[640,128]{1,0:T(8,128)(2,1)S(1)}, bf16[640,128]{1,0:T(8,128)(2,1)S(1)}, u32[]{:S(2)}, u32[]{:S(2)}) collective-permute-start(bf16[640,128]{1,0:T(8,128)(2,1)S(1)} %pad_maximum_fusion.3), channel_id=1, source_target_pairs={{0,4},{1,5},{2,6},{3,7},{4,0},{5,1},{6,2},{7,3},{8,12},{9,13},{10,... | collective-permute-start | bytes 491528 | tf_op jit(solution)/shard_map/ppermute | solution.py:297
  67.4 3.6 %collective-permute-done.6 = bf16[640,128]{1,0:T(8,128)(2,1)S(1)} collective-permute-done((bf16[640,128]{1,0:T(8,128)(2,1)S(1)}, bf16[640,128]{1,0:T(8,128)(2,1)S(1)}, u32[]{:S(2)}, u32[]{:S(2)}) %collective-permute-start.6) | collective-permute-done | bytes 163872 | tf_op jit(solution)/shard_map/ppermute | solution.py:297
  71.1 1.8 %collective-permute-start.7 = (bf16[1152,128]{1,0:T(8,128)(2,1)S(1)}, bf16[1152,128]{1,0:T(8,128)(2,1)S(1)}, u32[]{:S(2)}, u32[]{:S(2)}) collective-permute-start(bf16[1152,128]{1,0:T(8,128)(2,1)S(1)} %pad_maximum_fusion.refs_0_), channel_id=1, source_target_pairs={{0,2},{1,3},{2,0},{3,1},{4,6},{5,7},{6,4},{7,5},{8,10},{9,11},{10,... | collective-permute-start | bytes 884744 | tf_op jit(solution)/shard_map/ppermute | solution.py:297
  72.9 0.0 collective-permute-start.8
  72.9 0.5 collective-permute-start.9
  73.4 0.0 collective-permute-start.11
  73.4 1.0 %collective-permute-done.8.refs_2_ = bf16[1024,128]{1,0:T(8,128)(2,1)S(1)} collective-permute-done((bf16[1024,128]{1,0:T(8,128)(2,1)S(1)}, bf16[1024,128]{1,0:T(8,128)(2,1)S(1)}, u32[]{:S(2)}, u32[]{:S(2)}) %collective-permute-start.8) | collective-permute-done | bytes 262176 | tf_op jit(solution)/shard_map/ppermute | solution.py:297
  74.4 0.4 collective-permute-done.9.refs_3_
  74.8 0.0 copy-done
  74.8 0.9 %shard_map.69.values_ref = f32[1024,512]{1,0:T(8,128)S(1)} custom-call(s32[1]{0:T(128)} %bitcast.me_ref, bf16[23,64,512]{2,1,0:T(8,128)(2,1)S(1)} %get-tuple-element.20.kept_ref, bf16[1024,512]{1,0:T(8,128)(2,1)S(1)} %bitcast.10, f32[8,128]{1,0:T(8,128)S(1)} %bitcast.11, bf16[1024,128]{1,0:T(8,128)(2,1)S(1)} %pad_maximum_fusion.1.refs_0_, ...), custom_call_target="tpu_custom_call" | custom-call | tf_op jit(solution)/shard_map/pallas_call | solution.py:285
  75.7 2.4 %collective-permute-done.7.refs_1_ = bf16[1152,128]{1,0:T(8,128)(2,1)S(1)} collective-permute-done((bf16[1152,128]{1,0:T(8,128)(2,1)S(1)}, bf16[1152,128]{1,0:T(8,128)(2,1)S(1)}, u32[]{:S(2)}, u32[]{:S(2)}) %collective-permute-start.7) | collective-permute-done | bytes 294944 | tf_op jit(solution)/shard_map/ppermute | solution.py:297
  78.2 0.0 collective-permute-start.12
  78.2 0.6 collective-permute-start.10
  78.8 0.0 collective-permute-done.11.refs_2_
  78.8 1.0 %collective-permute-done.10.other_ref = bf16[128,128]{1,0:T(8,128)(2,1)S(1)} collective-permute-done((bf16[128,128]{1,0:T(8,128)(2,1)S(1)}, bf16[128,128]{1,0:T(8,128)(2,1)S(1)}, u32[]{:S(2)}, u32[]{:S(2)}) %collective-permute-start.10) | collective-permute-done | bytes 32800 | tf_op jit(solution)/shard_map/ppermute | solution.py:297
  79.8 0.0 collective-permute-done.12.refs_3_
  79.8 3.8 %shard_map.70 = (f32[64,512]{1,0:T(8,128)}, f32[4,128]{1,0:T(4,128)}, bf16[1024,512]{1,0:T(8,128)(2,1)}) custom-call(s32[1]{0:T(128)} %bitcast.me_ref, bf16[128,128]{1,0:T(8,128)(2,1)S(1)} %pad_maximum_fusion.8.sent_ref, bf16[128,128]{1,0:T(8,128)(2,1)S(1)} %collective-permute-done.10.other_ref, bf16[23,64,512]{2,1,0:T(8,128)(2,1)S(1)} %get-tuple-element.20.kept_ref, ...), custom_call_target="tpu_custom_call" | custom-call | tf_op jit(solution)/shard_map/pallas_call | solution.py:285
  (24 shorter events, 0.3 us)
Async XLA Ops:
  0.6 30.5 %copy-start.1 = (f32[64,512]{1,0:T(8,128)S(1)}, f32[64,512]{1,0:T(8,128)}, u32[]{:S(2)}) copy-start(f32[64,512]{1,0:T(8,128)} %atoms_ref.3) | copy-start | bytes 393220
  0.6 30.5 %copy-start.3 = (f32[1,512]{1,0:T(1,128)S(1)}, f32[1,512]{1,0:T(1,128)}, u32[]{:S(2)}) copy-start(f32[1,512]{1,0:T(1,128)} %param.4) | copy-start | bytes 6148
  0.7 51.4 %copy-start.2 = (f32[1024]{0:T(1024)S(1)}, f32[1024]{0:T(1024)}, u32[]{:S(2)}) copy-start(f32[1024]{0:T(1024)} %param.7) | copy-start | bytes 12292
  0.7 30.5 %all-to-all-start = ((bf16[16,64,512]{2,1,0:T(8,128)(2,1)}), bf16[16,64,512]{2,1,0:T(8,128)(2,1)S(1)}, u32[]{:S(2)}, u32[]{:S(2)}) async-start(bf16[16,64,512]{2,1,0:T(8,128)(2,1)} %bitcast.9), calls=%async_computation | async-start | bytes 2097152 | tf_op jit(solution)/shard_map/all_to_all | solution.py:341
  32.6 9.8 %collective-permute-start = (bf16[384,128]{1,0:T(8,128)(2,1)S(1)}, bf16[384,128]{1,0:T(8,128)(2,1)S(1)}, u32[]{:S(2)}, u32[]{:S(2)}) collective-permute-start(bf16[384,128]{1,0:T(8,128)(2,1)S(1)} %pad_maximum_fusion.4), channel_id=1, source_target_pairs={{0,8},{1,9},{2,10},{3,11},{4,12},{5,13},{6,14},{7,15},{8,0},{9,1},... | collective-permute-start | bytes 294920 | tf_op jit(solution)/shard_map/ppermute | solution.py:297
  42.5 5.4 %collective-permute-start.1 = (bf16[640,128]{1,0:T(8,128)(2,1)S(1)}, bf16[640,128]{1,0:T(8,128)(2,1)S(1)}, u32[]{:S(2)}, u32[]{:S(2)}) collective-permute-start(bf16[640,128]{1,0:T(8,128)(2,1)S(1)} %pad_maximum_fusion.2), channel_id=1, source_target_pairs={{0,4},{1,5},{2,6},{3,7},{4,0},{5,1},{6,2},{7,3},{8,12},{9,13},{10,... | collective-permute-start | bytes 491528 | tf_op jit(solution)/shard_map/ppermute | solution.py:297
  47.9 4.0 %collective-permute-start.2 = (bf16[128,128]{1,0:T(8,128)(2,1)S(1)}, bf16[128,128]{1,0:T(8,128)(2,1)S(1)}, u32[]{:S(2)}, u32[]{:S(2)}) collective-permute-start(bf16[128,128]{1,0:T(8,128)(2,1)S(1)} %pad_maximum_fusion.6), channel_id=1, source_target_pairs={{0,2},{1,3},{2,0},{3,1},{4,6},{5,7},{6,4},{7,5},{8,10},{9,11},{10,... | collective-permute-start | bytes 98312 | tf_op jit(solution)/shard_map/ppermute | solution.py:297
  51.9 1.3 %collective-permute-start.3 = (bf16[128,128]{1,0:T(8,128)(2,1)S(1)}, bf16[128,128]{1,0:T(8,128)(2,1)S(1)}, u32[]{:S(2)}, u32[]{:S(2)}) collective-permute-start(bf16[128,128]{1,0:T(8,128)(2,1)S(1)} %pad_maximum_fusion.7.sent_ref), channel_id=1, source_target_pairs={{0,1},{1,0},{2,3},{3,2},{4,5},{5,4},{6,7},{7,6},{8,9},{9,8},{10,11... | collective-permute-start | bytes 98312 | tf_op jit(solution)/shard_map/ppermute | solution.py:297
  52.2 22.6 %copy-start = (bf16[1,1024,512]{2,1,0:T(8,128)(2,1)S(1)}, bf16[1,1024,512]{2,1,0:T(8,128)(2,1)}, u32[]{:S(2)}) copy-start(bf16[1,1024,512]{2,1,0:T(8,128)(2,1)} %param.5) | copy-start | bytes 3145732
  56.6 7.9 %collective-permute-start.4 = (bf16[384,128]{1,0:T(8,128)(2,1)S(1)}, bf16[384,128]{1,0:T(8,128)(2,1)S(1)}, u32[]{:S(2)}, u32[]{:S(2)}) collective-permute-start(bf16[384,128]{1,0:T(8,128)(2,1)S(1)} %pad_maximum_fusion.5), channel_id=1, source_target_pairs={{0,8},{1,9},{2,10},{3,11},{4,12},{5,13},{6,14},{7,15},{8,0},{9,1},... | collective-permute-start | bytes 294920 | tf_op jit(solution)/shard_map/ppermute | solution.py:297
  57.5 8.2 %collective-permute-start.5 = (bf16[1024,128]{1,0:T(8,128)(2,1)S(1)}, bf16[1024,128]{1,0:T(8,128)(2,1)S(1)}, u32[]{:S(2)}, u32[]{:S(2)}) collective-permute-start(bf16[1024,128]{1,0:T(8,128)(2,1)S(1)} %pad_maximum_fusion.1.refs_0_), channel_id=1, source_target_pairs={{0,2},{1,3},{2,0},{3,1},{4,6},{5,7},{6,4},{7,5},{8,10},{9,11},{10,... | collective-permute-start | bytes 786440 | tf_op jit(solution)/shard_map/ppermute | solution.py:297
  65.7 5.3 %collective-permute-start.6 = (bf16[640,128]{1,0:T(8,128)(2,1)S(1)}, bf16[640,128]{1,0:T(8,128)(2,1)S(1)}, u32[]{:S(2)}, u32[]{:S(2)}) collective-permute-start(bf16[640,128]{1,0:T(8,128)(2,1)S(1)} %pad_maximum_fusion.3), channel_id=1, source_target_pairs={{0,4},{1,5},{2,6},{3,7},{4,0},{5,1},{6,2},{7,3},{8,12},{9,13},{10,... | collective-permute-start | bytes 491528 | tf_op jit(solution)/shard_map/ppermute | solution.py:297
  71.1 7.0 %collective-permute-start.7 = (bf16[1152,128]{1,0:T(8,128)(2,1)S(1)}, bf16[1152,128]{1,0:T(8,128)(2,1)S(1)}, u32[]{:S(2)}, u32[]{:S(2)}) collective-permute-start(bf16[1152,128]{1,0:T(8,128)(2,1)S(1)} %pad_maximum_fusion.refs_0_), channel_id=1, source_target_pairs={{0,2},{1,3},{2,0},{3,1},{4,6},{5,7},{6,4},{7,5},{8,10},{9,11},{10,... | collective-permute-start | bytes 884744 | tf_op jit(solution)/shard_map/ppermute | solution.py:297
  72.9 1.5 %collective-permute-start.8 = (bf16[1024,128]{1,0:T(8,128)(2,1)S(1)}, bf16[1024,128]{1,0:T(8,128)(2,1)S(1)}, u32[]{:S(2)}, u32[]{:S(2)}) collective-permute-start(bf16[1024,128]{1,0:T(8,128)(2,1)S(1)} %pad_maximum_fusion.1.refs_0_), channel_id=1, source_target_pairs={{0,1},{1,0},{2,3},{3,2},{4,5},{5,4},{6,7},{7,6},{8,9},{9,8},{10,11... | collective-permute-start | bytes 786440 | tf_op jit(solution)/shard_map/ppermute | solution.py:297
  72.9 1.9 %collective-permute-start.9 = (bf16[1024,128]{1,0:T(8,128)(2,1)S(1)}, bf16[1024,128]{1,0:T(8,128)(2,1)S(1)}, u32[]{:S(2)}, u32[]{:S(2)}) collective-permute-start(bf16[1024,128]{1,0:T(8,128)(2,1)S(1)} %collective-permute-done.5.refs_1_), channel_id=1, source_target_pairs={{0,1},{1,0},{2,3},{3,2},{4,5},{5,4},{6,7},{7,6},{8,9},{9,8},{10,11... | collective-permute-start | bytes 786440 | tf_op jit(solution)/shard_map/ppermute | solution.py:297
  73.4 5.4 %collective-permute-start.11 = (bf16[1152,128]{1,0:T(8,128)(2,1)S(1)}, bf16[1152,128]{1,0:T(8,128)(2,1)S(1)}, u32[]{:S(2)}, u32[]{:S(2)}) collective-permute-start(bf16[1152,128]{1,0:T(8,128)(2,1)S(1)} %pad_maximum_fusion.refs_0_), channel_id=1, source_target_pairs={{0,1},{1,0},{2,3},{3,2},{4,5},{5,4},{6,7},{7,6},{8,9},{9,8},{10,11... | collective-permute-start | bytes 884744 | tf_op jit(solution)/shard_map/ppermute | solution.py:297
  78.2 1.6 %collective-permute-start.12 = (bf16[1152,128]{1,0:T(8,128)(2,1)S(1)}, bf16[1152,128]{1,0:T(8,128)(2,1)S(1)}, u32[]{:S(2)}, u32[]{:S(2)}) collective-permute-start(bf16[1152,128]{1,0:T(8,128)(2,1)S(1)} %collective-permute-done.7.refs_1_), channel_id=1, source_target_pairs={{0,1},{1,0},{2,3},{3,2},{4,5},{5,4},{6,7},{7,6},{8,9},{9,8},{10,11... | collective-permute-start | bytes 884744 | tf_op jit(solution)/shard_map/ppermute | solution.py:297
  78.2 1.6 %collective-permute-start.10 = (bf16[128,128]{1,0:T(8,128)(2,1)S(1)}, bf16[128,128]{1,0:T(8,128)(2,1)S(1)}, u32[]{:S(2)}, u32[]{:S(2)}) collective-permute-start(bf16[128,128]{1,0:T(8,128)(2,1)S(1)} %pad_maximum_fusion.8.sent_ref), channel_id=1, source_target_pairs={{0,1},{1,0},{2,3},{3,2},{4,5},{5,4},{6,7},{7,6},{8,9},{9,8},{10,11... | collective-permute-start | bytes 98312 | tf_op jit(solution)/shard_map/ppermute | solution.py:297

commit v7 on v6

--- a/solution.py
+++ b/solution.py
@@ -93,6 +93,14 @@
     return jnp.concatenate([atoms[:, i : i + LANES] for i in range(0, atoms.shape[1], LANES)], axis=0)
 
 
+def delayed(now, before):
+    width = now.shape[1]
+    rows = [now]
+    for late in range(LANES, width, LANES):
+        rows.append(jnp.concatenate([before[:, width - late :], now[:, : width - late]], axis=1))
+    return jnp.concatenate(rows, axis=0)
+
+
 def rebuild(taps, slab_of, slabs, width, turned_ref, sums_ref):
     per = width // LANES
     q, v = row_lane()
@@ -101,10 +109,7 @@
 
     def body(n):
         now, before = slab_of(n), slab_of(n - 1)
-        shifted = [now] + [
-            jnp.concatenate([before[:, width - LANES * p :], now[:, : width - LANES * p]], axis=1) for p in range(1, per)
-        ]
-        products = dot(taps, jnp.concatenate(shifted, axis=0), ((0,), (0,)))
+        products = dot(taps, delayed(now, before), ((0,), (0,)))
         last = turned_ref[...]
         for i in range(per):
             turned = pltpu.roll(products[:, LANES * i : LANES * (i + 1)], 0, 1, stride=1, stride_axis=0)
@@ -259,11 +264,13 @@
     gradient_ref[...] = jnp.zeros_like(gradient_ref)
 
     def body(n):
-        gradient_ref[...] += dot(kept_ref[n + 1], windows_of(hankel_ref, n, width), ((1,), (0,)))
+        blocks = [hankel_ref[n * per + i] for i in range(per)]
+        gradient_ref[...] += dot(delayed(kept_ref[n + 1], kept_ref[n]), jnp.concatenate(blocks, axis=0), ((1,), (0,)))
 
     over_slabs(turned_rows_ref, hankel_ref, slabs, per, body)
+    gradient = jnp.concatenate([gradient_ref[p * owned : (p + 1) * owned, :] for p in range(reach)], axis=1)
     atoms = kept_ref[slabs + 1].astype(F32) + kept_ref[slabs + 2].astype(F32)
-    atoms_out[...] = normalised(atoms + factor * gradient_ref[...])
+    atoms_out[...] = normalised(atoms + factor * gradient)
     rows_ref[: slabs * per, :] = residual
     residual_out[...] = rows_ref[pl.ds(me * per, per), :]
     frames = windows_of(hankel_ref, me, width)
@@ -381,7 +388,7 @@
             jax.ShapeDtypeStruct((per, LANES), F32),
             jax.ShapeDtypeStruct((atom_count, width), BF16),
         ],
-        [*windows, cutoffs],
+        [*windows[:-1], pltpu.VMEM(taps_shape.shape, F32), cutoffs],
         at, *second, kept, values, all_thresholds, *after,
     )
     return codes[None], atoms, residual.reshape(1, width)

time: 83.8 us -> 83.5 us (level)
  no operation moved by 1% of the time
where the time goes in v7:
time: 83.5 us; the launch traced here: 83.3 us
  waiting for transfers between devices  52.6 us (63%)
  starting transfers between devices  20.3 us (24%)
  Pallas kernels  9.11 us (11%)
  between operations  0.86 us (1%)
    ppermute x13, waiting for transfers between devices, swapped(): return lax.ppermute(block, 'tm', [(i, i ^ distance) for i in range(count)])  29.6 us
    all_to_all x1, waiting for transfers between devices, on_device(): lax.all_to_all(codes.reshape(slabs, owned, width), 'tm', 0, 0, tiled=True)  22.9 us
    ppermute x13, starting transfers between devices, swapped(): return lax.ppermute(block, 'tm', [(i, i ^ distance) for i in range(count)])  12.7 us
    pallas_call x4, Pallas kernels, call(): pl.pallas_call(kernel, out_shape=tuple(outs), in_specs=[pl.BlockSpec(memo...  9.11 us
    all_to_all x1, starting transfers between devices, on_device(): lax.all_to_all(codes.reshape(slabs, owned, width), 'tm', 0, 0, tiled=True)  7.53 us
  transfers between devices with their start and end apart: 14, of which 12 were waited for; matrix products, arithmetic and copies ran while one was open for 0% of the time, Pallas kernels for 1%

profile of v7, /device:TPU:0, one launch (start us, length us, event | category | flops | bytes accessed | tf_op | source)
XLA Modules:
  0.0 83.3 jit_solution(11743088034654980646)
XLA Ops:
  0.6 0.0 copy-start.1
  0.6 0.0 copy-start.3
  0.7 0.0 copy-start.2
  0.7 7.5 %all-to-all-start = ((bf16[16,64,512]{2,1,0:T(8,128)(2,1)}), bf16[16,64,512]{2,1,0:T(8,128)(2,1)S(1)}, u32[]{:S(2)}, u32[]{:S(2)}) async-start(bf16[16,64,512]{2,1,0:T(8,128)(2,1)} %bitcast.9), calls=%async_computation | async-start | bytes 2097152 | tf_op jit(solution)/shard_map/all_to_all | solution.py:348
  8.2 22.9 %all-to-all-done.codes_ref = bf16[16,64,512]{2,1,0:T(8,128)(2,1)S(1)} async-done(((bf16[16,64,512]{2,1,0:T(8,128)(2,1)}), bf16[16,64,512]{2,1,0:T(8,128)(2,1)S(1)}, u32[]{:S(2)}, u32[]{:S(2)}) %all-to-all-start) | async-done | bytes 1048608 | tf_op jit(solution)/shard_map/all_to_all | solution.py:348
  31.1 0.0 copy-done.1
  31.1 0.0 copy-done.3
  31.1 1.4 %shard_map.67 = (bf16[256,128]{1,0:T(8,128)(2,1)S(1)}, f32[64,128]{1,0:T(8,128)S(1)}) custom-call(s32[1]{0:T(128)} %bitcast.me_ref, f32[64,512]{1,0:T(8,128)S(1)} %copy-done.1, bf16[16,64,512]{2,1,0:T(8,128)(2,1)S(1)} %all-to-all-done.codes_ref, f32[4,128]{1,0:T(4,128)S(1)} %bitcast.13), custom_call_target="tpu_custom_call" | custom-call | tf_op jit(solution)/shard_map/pallas_call | solution.py:292
  32.6 5.1 %collective-permute-start = (bf16[384,128]{1,0:T(8,128)(2,1)S(1)}, bf16[384,128]{1,0:T(8,128)(2,1)S(1)}, u32[]{:S(2)}, u32[]{:S(2)}) collective-permute-start(bf16[384,128]{1,0:T(8,128)(2,1)S(1)} %pad_maximum_fusion.4), channel_id=1, source_target_pairs={{0,8},{1,9},{2,10},{3,11},{4,12},{5,13},{6,14},{7,15},{8,0},{9,1},... | collective-permute-start | bytes 294920 | tf_op jit(solution)/shard_map/ppermute | solution.py:304
  37.7 4.7 %collective-permute-done = bf16[384,128]{1,0:T(8,128)(2,1)S(1)} collective-permute-done((bf16[384,128]{1,0:T(8,128)(2,1)S(1)}, bf16[384,128]{1,0:T(8,128)(2,1)S(1)}, u32[]{:S(2)}, u32[]{:S(2)}) %collective-permute-start) | collective-permute-done | bytes 98336 | tf_op jit(solution)/shard_map/ppermute | solution.py:304
  42.5 0.1 collective-permute-start.1
  42.6 5.3 %collective-permute-done.1 = bf16[640,128]{1,0:T(8,128)(2,1)S(1)} collective-permute-done((bf16[640,128]{1,0:T(8,128)(2,1)S(1)}, bf16[640,128]{1,0:T(8,128)(2,1)S(1)}, u32[]{:S(2)}, u32[]{:S(2)}) %collective-permute-start.1) | collective-permute-done | bytes 163872 | tf_op jit(solution)/shard_map/ppermute | solution.py:304
  47.9 0.1 collective-permute-start.2
  48.0 3.9 %collective-permute-done.2 = bf16[128,128]{1,0:T(8,128)(2,1)S(1)} collective-permute-done((bf16[128,128]{1,0:T(8,128)(2,1)S(1)}, bf16[128,128]{1,0:T(8,128)(2,1)S(1)}, u32[]{:S(2)}, u32[]{:S(2)}) %collective-permute-start.2) | collective-permute-done | bytes 32800 | tf_op jit(solution)/shard_map/ppermute | solution.py:304
  51.9 0.1 collective-permute-start.3
  52.0 0.0 copy-done.2
  52.0 0.1 dynamic-slice_bitcast_fusion
  52.1 0.1 copy.7.thresholds_ref
  52.2 0.0 copy-start
  52.2 1.0 %collective-permute-done.3.other_ref = bf16[128,128]{1,0:T(8,128)(2,1)S(1)} collective-permute-done((bf16[128,128]{1,0:T(8,128)(2,1)S(1)}, bf16[128,128]{1,0:T(8,128)(2,1)S(1)}, u32[]{:S(2)}, u32[]{:S(2)}) %collective-permute-start.3) | collective-permute-done | bytes 32800 | tf_op jit(solution)/shard_map/ppermute | solution.py:304
  53.2 3.3 %shard_map.68 = (bf16[256,128]{1,0:T(8,128)(2,1)S(1)}, bf16[23,64,512]{2,1,0:T(8,128)(2,1)S(1)}, f32[64,128]{1,0:T(8,128)S(1)}) custom-call(s32[1]{0:T(128)} %bitcast.me_ref, bf16[128,128]{1,0:T(8,128)(2,1)S(1)} %pad_maximum_fusion.7.sent_ref, bf16[128,128]{1,0:T(8,128)(2,1)S(1)} %collective-permute-done.3.other_ref, f32[64,512]{1,0:T(8,128)S(1)} %copy-done.1, ...), custom_call_target="tpu_custom_call" | custom-call | tf_op jit(solution)/shard_map/pallas_call | solution.py:292
  56.6 0.9 %collective-permute-start.4 = (bf16[384,128]{1,0:T(8,128)(2,1)S(1)}, bf16[384,128]{1,0:T(8,128)(2,1)S(1)}, u32[]{:S(2)}, u32[]{:S(2)}) collective-permute-start(bf16[384,128]{1,0:T(8,128)(2,1)S(1)} %pad_maximum_fusion.5), channel_id=1, source_target_pairs={{0,8},{1,9},{2,10},{3,11},{4,12},{5,13},{6,14},{7,15},{8,0},{9,1},... | collective-permute-start | bytes 294920 | tf_op jit(solution)/shard_map/ppermute | solution.py:304
  57.5 1.9 %collective-permute-start.5 = (bf16[1024,128]{1,0:T(8,128)(2,1)S(1)}, bf16[1024,128]{1,0:T(8,128)(2,1)S(1)}, u32[]{:S(2)}, u32[]{:S(2)}) collective-permute-start(bf16[1024,128]{1,0:T(8,128)(2,1)S(1)} %pad_maximum_fusion.1.refs_0_), channel_id=1, source_target_pairs={{0,2},{1,3},{2,0},{3,1},{4,6},{5,7},{6,4},{7,5},{8,10},{9,11},{10,... | collective-permute-start | bytes 786440 | tf_op jit(solution)/shard_map/ppermute | solution.py:304
  59.3 5.1 %collective-permute-done.4 = bf16[384,128]{1,0:T(8,128)(2,1)S(1)} collective-permute-done((bf16[384,128]{1,0:T(8,128)(2,1)S(1)}, bf16[384,128]{1,0:T(8,128)(2,1)S(1)}, u32[]{:S(2)}, u32[]{:S(2)}) %collective-permute-start.4) | collective-permute-done | bytes 98336 | tf_op jit(solution)/shard_map/ppermute | solution.py:304
  64.5 1.2 %collective-permute-done.5.refs_1_ = bf16[1024,128]{1,0:T(8,128)(2,1)S(1)} collective-permute-done((bf16[1024,128]{1,0:T(8,128)(2,1)S(1)}, bf16[1024,128]{1,0:T(8,128)(2,1)S(1)}, u32[]{:S(2)}, u32[]{:S(2)}) %collective-permute-start.5) | collective-permute-done | bytes 262176 | tf_op jit(solution)/shard_map/ppermute | solution.py:304
  65.7 1.7 %collective-permute-start.6 = (bf16[640,128]{1,0:T(8,128)(2,1)S(1)}, bf16[640,128]{1,0:T(8,128)(2,1)S(1)}, u32[]{:S(2)}, u32[]{:S(2)}) collective-permute-start(bf16[640,128]{1,0:T(8,128)(2,1)S(1)} %pad_maximum_fusion.3), channel_id=1, source_target_pairs={{0,4},{1,5},{2,6},{3,7},{4,0},{5,1},{6,2},{7,3},{8,12},{9,13},{10,... | collective-permute-start | bytes 491528 | tf_op jit(solution)/shard_map/ppermute | solution.py:304
  67.4 3.6 %collective-permute-done.6 = bf16[640,128]{1,0:T(8,128)(2,1)S(1)} collective-permute-done((bf16[640,128]{1,0:T(8,128)(2,1)S(1)}, bf16[640,128]{1,0:T(8,128)(2,1)S(1)}, u32[]{:S(2)}, u32[]{:S(2)}) %collective-permute-start.6) | collective-permute-done | bytes 163872 | tf_op jit(solution)/shard_map/ppermute | solution.py:304
  71.1 1.8 %collective-permute-start.7 = (bf16[1152,128]{1,0:T(8,128)(2,1)S(1)}, bf16[1152,128]{1,0:T(8,128)(2,1)S(1)}, u32[]{:S(2)}, u32[]{:S(2)}) collective-permute-start(bf16[1152,128]{1,0:T(8,128)(2,1)S(1)} %pad_maximum_fusion.refs_0_), channel_id=1, source_target_pairs={{0,2},{1,3},{2,0},{3,1},{4,6},{5,7},{6,4},{7,5},{8,10},{9,11},{10,... | collective-permute-start | bytes 884744 | tf_op jit(solution)/shard_map/ppermute | solution.py:304
  72.9 0.0 collective-permute-start.8
  72.9 0.5 collective-permute-start.9
  73.4 0.0 collective-permute-start.11
  73.4 1.0 %collective-permute-done.8.refs_2_ = bf16[1024,128]{1,0:T(8,128)(2,1)S(1)} collective-permute-done((bf16[1024,128]{1,0:T(8,128)(2,1)S(1)}, bf16[1024,128]{1,0:T(8,128)(2,1)S(1)}, u32[]{:S(2)}, u32[]{:S(2)}) %collective-permute-start.8) | collective-permute-done | bytes 262176 | tf_op jit(solution)/shard_map/ppermute | solution.py:304
  74.4 0.4 collective-permute-done.9.refs_3_
  74.8 0.0 copy-done
  74.8 0.9 %shard_map.69.values_ref = f32[1024,512]{1,0:T(8,128)S(1)} custom-call(s32[1]{0:T(128)} %bitcast.me_ref, bf16[23,64,512]{2,1,0:T(8,128)(2,1)S(1)} %get-tuple-element.20.kept_ref, bf16[1024,512]{1,0:T(8,128)(2,1)S(1)} %bitcast.10, f32[8,128]{1,0:T(8,128)S(1)} %bitcast.11, bf16[1024,128]{1,0:T(8,128)(2,1)S(1)} %pad_maximum_fusion.1.refs_0_, ...), custom_call_target="tpu_custom_call" | custom-call | tf_op jit(solution)/shard_map/pallas_call | solution.py:292
  75.7 2.4 %collective-permute-done.7.refs_1_ = bf16[1152,128]{1,0:T(8,128)(2,1)S(1)} collective-permute-done((bf16[1152,128]{1,0:T(8,128)(2,1)S(1)}, bf16[1152,128]{1,0:T(8,128)(2,1)S(1)}, u32[]{:S(2)}, u32[]{:S(2)}) %collective-permute-start.7) | collective-permute-done | bytes 294944 | tf_op jit(solution)/shard_map/ppermute | solution.py:304
  78.2 0.0 collective-permute-start.12
  78.2 0.6 collective-permute-start.10
  78.8 0.0 collective-permute-done.11.refs_2_
  78.8 1.0 %collective-permute-done.10.other_ref = bf16[128,128]{1,0:T(8,128)(2,1)S(1)} collective-permute-done((bf16[128,128]{1,0:T(8,128)(2,1)S(1)}, bf16[128,128]{1,0:T(8,128)(2,1)S(1)}, u32[]{:S(2)}, u32[]{:S(2)}) %collective-permute-start.10) | collective-permute-done | bytes 32800 | tf_op jit(solution)/shard_map/ppermute | solution.py:304
  79.8 0.0 collective-permute-done.12.refs_3_
  79.8 3.5 %shard_map.70 = (f32[64,512]{1,0:T(8,128)}, f32[4,128]{1,0:T(4,128)}, bf16[1024,512]{1,0:T(8,128)(2,1)}) custom-call(s32[1]{0:T(128)} %bitcast.me_ref, bf16[128,128]{1,0:T(8,128)(2,1)S(1)} %pad_maximum_fusion.8.sent_ref, bf16[128,128]{1,0:T(8,128)(2,1)S(1)} %collective-permute-done.10.other_ref, bf16[23,64,512]{2,1,0:T(8,128)(2,1)S(1)} %get-tuple-element.20.kept_ref, ...), custom_call_target="tpu_custom_call" | custom-call | tf_op jit(solution)/shard_map/pallas_call | solution.py:292
  (24 shorter events, 0.3 us)
Async XLA Ops:
  0.6 30.5 %copy-start.1 = (f32[64,512]{1,0:T(8,128)S(1)}, f32[64,512]{1,0:T(8,128)}, u32[]{:S(2)}) copy-start(f32[64,512]{1,0:T(8,128)} %atoms_ref.3) | copy-start | bytes 393220
  0.6 30.5 %copy-start.3 = (f32[1,512]{1,0:T(1,128)S(1)}, f32[1,512]{1,0:T(1,128)}, u32[]{:S(2)}) copy-start(f32[1,512]{1,0:T(1,128)} %param.4) | copy-start | bytes 6148
  0.7 51.4 %copy-start.2 = (f32[1024]{0:T(1024)S(1)}, f32[1024]{0:T(1024)}, u32[]{:S(2)}) copy-start(f32[1024]{0:T(1024)} %param.7) | copy-start | bytes 12292
  0.7 30.5 %all-to-all-start = ((bf16[16,64,512]{2,1,0:T(8,128)(2,1)}), bf16[16,64,512]{2,1,0:T(8,128)(2,1)S(1)}, u32[]{:S(2)}, u32[]{:S(2)}) async-start(bf16[16,64,512]{2,1,0:T(8,128)(2,1)} %bitcast.9), calls=%async_computation | async-start | bytes 2097152 | tf_op jit(solution)/shard_map/all_to_all | solution.py:348
  32.6 9.8 %collective-permute-start = (bf16[384,128]{1,0:T(8,128)(2,1)S(1)}, bf16[384,128]{1,0:T(8,128)(2,1)S(1)}, u32[]{:S(2)}, u32[]{:S(2)}) collective-permute-start(bf16[384,128]{1,0:T(8,128)(2,1)S(1)} %pad_maximum_fusion.4), channel_id=1, source_target_pairs={{0,8},{1,9},{2,10},{3,11},{4,12},{5,13},{6,14},{7,15},{8,0},{9,1},... | collective-permute-start | bytes 294920 | tf_op jit(solution)/shard_map/ppermute | solution.py:304
  42.5 5.4 %collective-permute-start.1 = (bf16[640,128]{1,0:T(8,128)(2,1)S(1)}, bf16[640,128]{1,0:T(8,128)(2,1)S(1)}, u32[]{:S(2)}, u32[]{:S(2)}) collective-permute-start(bf16[640,128]{1,0:T(8,128)(2,1)S(1)} %pad_maximum_fusion.2), channel_id=1, source_target_pairs={{0,4},{1,5},{2,6},{3,7},{4,0},{5,1},{6,2},{7,3},{8,12},{9,13},{10,... | collective-permute-start | bytes 491528 | tf_op jit(solution)/shard_map/ppermute | solution.py:304
  47.9 4.0 %collective-permute-start.2 = (bf16[128,128]{1,0:T(8,128)(2,1)S(1)}, bf16[128,128]{1,0:T(8,128)(2,1)S(1)}, u32[]{:S(2)}, u32[]{:S(2)}) collective-permute-start(bf16[128,128]{1,0:T(8,128)(2,1)S(1)} %pad_maximum_fusion.6), channel_id=1, source_target_pairs={{0,2},{1,3},{2,0},{3,1},{4,6},{5,7},{6,4},{7,5},{8,10},{9,11},{10,... | collective-permute-start | bytes 98312 | tf_op jit(solution)/shard_map/ppermute | solution.py:304
  51.9 1.3 %collective-permute-start.3 = (bf16[128,128]{1,0:T(8,128)(2,1)S(1)}, bf16[128,128]{1,0:T(8,128)(2,1)S(1)}, u32[]{:S(2)}, u32[]{:S(2)}) collective-permute-start(bf16[128,128]{1,0:T(8,128)(2,1)S(1)} %pad_maximum_fusion.7.sent_ref), channel_id=1, source_target_pairs={{0,1},{1,0},{2,3},{3,2},{4,5},{5,4},{6,7},{7,6},{8,9},{9,8},{10,11... | collective-permute-start | bytes 98312 | tf_op jit(solution)/shard_map/ppermute | solution.py:304
  52.2 22.6 %copy-start = (bf16[1,1024,512]{2,1,0:T(8,128)(2,1)S(1)}, bf16[1,1024,512]{2,1,0:T(8,128)(2,1)}, u32[]{:S(2)}) copy-start(bf16[1,1024,512]{2,1,0:T(8,128)(2,1)} %param.5) | copy-start | bytes 3145732
  56.6 7.9 %collective-permute-start.4 = (bf16[384,128]{1,0:T(8,128)(2,1)S(1)}, bf16[384,128]{1,0:T(8,128)(2,1)S(1)}, u32[]{:S(2)}, u32[]{:S(2)}) collective-permute-start(bf16[384,128]{1,0:T(8,128)(2,1)S(1)} %pad_maximum_fusion.5), channel_id=1, source_target_pairs={{0,8},{1,9},{2,10},{3,11},{4,12},{5,13},{6,14},{7,15},{8,0},{9,1},... | collective-permute-start | bytes 294920 | tf_op jit(solution)/shard_map/ppermute | solution.py:304
  57.5 8.2 %collective-permute-start.5 = (bf16[1024,128]{1,0:T(8,128)(2,1)S(1)}, bf16[1024,128]{1,0:T(8,128)(2,1)S(1)}, u32[]{:S(2)}, u32[]{:S(2)}) collective-permute-start(bf16[1024,128]{1,0:T(8,128)(2,1)S(1)} %pad_maximum_fusion.1.refs_0_), channel_id=1, source_target_pairs={{0,2},{1,3},{2,0},{3,1},{4,6},{5,7},{6,4},{7,5},{8,10},{9,11},{10,... | collective-permute-start | bytes 786440 | tf_op jit(solution)/shard_map/ppermute | solution.py:304
  65.7 5.3 %collective-permute-start.6 = (bf16[640,128]{1,0:T(8,128)(2,1)S(1)}, bf16[640,128]{1,0:T(8,128)(2,1)S(1)}, u32[]{:S(2)}, u32[]{:S(2)}) collective-permute-start(bf16[640,128]{1,0:T(8,128)(2,1)S(1)} %pad_maximum_fusion.3), channel_id=1, source_target_pairs={{0,4},{1,5},{2,6},{3,7},{4,0},{5,1},{6,2},{7,3},{8,12},{9,13},{10,... | collective-permute-start | bytes 491528 | tf_op jit(solution)/shard_map/ppermute | solution.py:304
  71.1 7.0 %collective-permute-start.7 = (bf16[1152,128]{1,0:T(8,128)(2,1)S(1)}, bf16[1152,128]{1,0:T(8,128)(2,1)S(1)}, u32[]{:S(2)}, u32[]{:S(2)}) collective-permute-start(bf16[1152,128]{1,0:T(8,128)(2,1)S(1)} %pad_maximum_fusion.refs_0_), channel_id=1, source_target_pairs={{0,2},{1,3},{2,0},{3,1},{4,6},{5,7},{6,4},{7,5},{8,10},{9,11},{10,... | collective-permute-start | bytes 884744 | tf_op jit(solution)/shard_map/ppermute | solution.py:304
  72.9 1.5 %collective-permute-start.8 = (bf16[1024,128]{1,0:T(8,128)(2,1)S(1)}, bf16[1024,128]{1,0:T(8,128)(2,1)S(1)}, u32[]{:S(2)}, u32[]{:S(2)}) collective-permute-start(bf16[1024,128]{1,0:T(8,128)(2,1)S(1)} %pad_maximum_fusion.1.refs_0_), channel_id=1, source_target_pairs={{0,1},{1,0},{2,3},{3,2},{4,5},{5,4},{6,7},{7,6},{8,9},{9,8},{10,11... | collective-permute-start | bytes 786440 | tf_op jit(solution)/shard_map/ppermute | solution.py:304
  72.9 1.9 %collective-permute-start.9 = (bf16[1024,128]{1,0:T(8,128)(2,1)S(1)}, bf16[1024,128]{1,0:T(8,128)(2,1)S(1)}, u32[]{:S(2)}, u32[]{:S(2)}) collective-permute-start(bf16[1024,128]{1,0:T(8,128)(2,1)S(1)} %collective-permute-done.5.refs_1_), channel_id=1, source_target_pairs={{0,1},{1,0},{2,3},{3,2},{4,5},{5,4},{6,7},{7,6},{8,9},{9,8},{10,11... | collective-permute-start | bytes 786440 | tf_op jit(solution)/shard_map/ppermute | solution.py:304
  73.4 5.4 %collective-permute-start.11 = (bf16[1152,128]{1,0:T(8,128)(2,1)S(1)}, bf16[1152,128]{1,0:T(8,128)(2,1)S(1)}, u32[]{:S(2)}, u32[]{:S(2)}) collective-permute-start(bf16[1152,128]{1,0:T(8,128)(2,1)S(1)} %pad_maximum_fusion.refs_0_), channel_id=1, source_target_pairs={{0,1},{1,0},{2,3},{3,2},{4,5},{5,4},{6,7},{7,6},{8,9},{9,8},{10,11... | collective-permute-start | bytes 884744 | tf_op jit(solution)/shard_map/ppermute | solution.py:304
  78.2 1.6 %collective-permute-start.12 = (bf16[1152,128]{1,0:T(8,128)(2,1)S(1)}, bf16[1152,128]{1,0:T(8,128)(2,1)S(1)}, u32[]{:S(2)}, u32[]{:S(2)}) collective-permute-start(bf16[1152,128]{1,0:T(8,128)(2,1)S(1)} %collective-permute-done.7.refs_1_), channel_id=1, source_target_pairs={{0,1},{1,0},{2,3},{3,2},{4,5},{5,4},{6,7},{7,6},{8,9},{9,8},{10,11... | collective-permute-start | bytes 884744 | tf_op jit(solution)/shard_map/ppermute | solution.py:304
  78.2 1.6 %collective-permute-start.10 = (bf16[128,128]{1,0:T(8,128)(2,1)S(1)}, bf16[128,128]{1,0:T(8,128)(2,1)S(1)}, u32[]{:S(2)}, u32[]{:S(2)}) collective-permute-start(bf16[128,128]{1,0:T(8,128)(2,1)S(1)} %pad_maximum_fusion.8.sent_ref), channel_id=1, source_target_pairs={{0,1},{1,0},{2,3},{3,2},{4,5},{5,4},{6,7},{7,6},{8,9},{9,8},{10,11... | collective-permute-start | bytes 98312 | tf_op jit(solution)/shard_map/ppermute | solution.py:304

commit v8 on v7

--- a/solution.py
+++ b/solution.py
@@ -101,24 +101,22 @@
     return jnp.concatenate(rows, axis=0)
 
 
-def rebuild(taps, slab_of, slabs, width, turned_ref, sums_ref):
+def rebuild(taps, slab_of, slabs, width, sums_ref):
     per = width // LANES
     q, v = row_lane()
     keep = v >= q
-    turned_ref[...] = jnp.zeros_like(turned_ref)
-
-    def body(n):
+
+    def body(n, last):
         now, before = slab_of(n), slab_of(n - 1)
         products = dot(taps, delayed(now, before), ((0,), (0,)))
-        last = turned_ref[...]
         for i in range(per):
             turned = pltpu.roll(products[:, LANES * i : LANES * (i + 1)], 0, 1, stride=1, stride_axis=0)
             placed = jnp.where(keep, turned, last)
             sums_ref[n * per + i] = placed.reshape(LANES // 8, 8, LANES).sum(axis=0)
             last = turned
-        turned_ref[...] = last
-
-    repeat(slabs, body)
+        return last
+
+    repeat(slabs, body, jnp.zeros((LANES, LANES), F32))
 
 
 def partial_residual(me, factor, signal_ref, sums_ref, out_ref):
@@ -137,7 +135,7 @@
     return me
 
 
-def first_kernel(factor, me_ref, atoms_ref, codes_ref, signal_ref, taps_out, part_out, turned_ref, sums_ref):
+def first_kernel(factor, me_ref, atoms_ref, codes_ref, signal_ref, taps_out, part_out, sums_ref):
     slabs, owned, width = codes_ref.shape
     taps = stacked_taps(atoms_ref[...].astype(BF16))
     taps_out[...] = taps
@@ -148,7 +146,7 @@
             return codes_ref[n] if n >= 0 else zero
         return jnp.where(n >= 0, codes_ref[jnp.maximum(n, 0)], zero)
 
-    rebuild(taps, slab_of, slabs, width, turned_ref, sums_ref)
+    rebuild(taps, slab_of, slabs, width, sums_ref)
     partial_residual(me_ref[0], factor, signal_ref, sums_ref, part_out)
 
 
@@ -172,7 +170,7 @@
 def second_kernel(
     factor, me_ref, sent_ref, other_ref, atoms_ref, codes_ref, thresholds_ref, signal_ref,
     taps_out, codes_out, part_out,
-    rows_ref, turned_rows_ref, hankel_ref, gradient_ref, turned_ref, sums_ref,
+    rows_ref, turned_rows_ref, hankel_ref, gradient_ref, sums_ref,
 ):
     slabs, owned, width = codes_ref.shape
     per = width // LANES
@@ -204,7 +202,7 @@
     codes_out[slabs + 2] = (after - after_b.astype(F32)).astype(BF16)
     taps = stacked_taps(after_b)
     taps_out[...] = taps
-    rebuild(taps, lambda n: codes_out[n + 1], slabs, width, turned_ref, sums_ref)
+    rebuild(taps, lambda n: codes_out[n + 1], slabs, width, sums_ref)
     partial_residual(me_ref[0], factor, signal_ref, sums_ref, part_out)
 
 
@@ -295,7 +293,7 @@
         in_specs=[pl.BlockSpec(memory_space=pltpu.SMEM)] + [vmem] * (len(args) - 1),
         out_specs=(vmem,) * len(outs),
         scratch_shapes=scratch,
-        compiler_params=pltpu.CompilerParams(vmem_limit_bytes=room + 6 * 1024 * 1024),
+        compiler_params=pltpu.CompilerParams(vmem_limit_bytes=room + 14 * 1024 * 1024),
     )(*args)
 
 
@@ -347,7 +345,7 @@
 
     by_atom = lax.all_to_all(codes.reshape(slabs, owned, width), "tm", 0, 0, tiled=True)
 
-    sums = [pltpu.VMEM((LANES, LANES), F32), pltpu.VMEM((blocks, 8, LANES), F32)]
+    sums = [pltpu.VMEM((blocks, 8, LANES), F32)]
     windows = [
         pltpu.VMEM((blocks + 8, LANES), F32),
         pltpu.VMEM((blocks + 8, 8, LANES), F32),

time: 83.5 us -> 83.5 us (level)
  no operation moved by 1% of the time
where the time goes in v8:
time: 83.5 us; the launch traced here: 83.3 us
  waiting for transfers between devices  52.5 us (63%)
  starting transfers between devices  20.3 us (24%)
  Pallas kernels  9.12 us (11%)
  between operations  0.86 us (1%)
    ppermute x13, waiting for transfers between devices, swapped(): return lax.ppermute(block, 'tm', [(i, i ^ distance) for i in range(count)])  29.6 us
    all_to_all x1, waiting for transfers between devices, on_device(): lax.all_to_all(codes.reshape(slabs, owned, width), 'tm', 0, 0, tiled=True)  22.9 us
    ppermute x13, starting transfers between devices, swapped(): return lax.ppermute(block, 'tm', [(i, i ^ distance) for i in range(count)])  12.7 us
    pallas_call x4, Pallas kernels, call(): pl.pallas_call(kernel, out_shape=tuple(outs), in_specs=[pl.BlockSpec(memo...  9.12 us
    all_to_all x1, starting transfers between devices, on_device(): lax.all_to_all(codes.reshape(slabs, owned, width), 'tm', 0, 0, tiled=True)  7.53 us
  transfers between devices with their start and end apart: 14, of which 12 were waited for; matrix products, arithmetic and copies ran while one was open for 0% of the time, Pallas kernels for 1%

profile of v8, /device:TPU:0, one launch (start us, length us, event | category | flops | bytes accessed | tf_op | source)
XLA Modules:
  0.0 83.3 jit_solution(6863933537364769553)
XLA Ops:
  0.6 0.0 copy-start.1
  0.6 0.0 copy-start.3
  0.7 0.0 copy-start.2
  0.7 7.5 %all-to-all-start = ((bf16[16,64,512]{2,1,0:T(8,128)(2,1)}), bf16[16,64,512]{2,1,0:T(8,128)(2,1)S(1)}, u32[]{:S(2)}, u32[]{:S(2)}) async-start(bf16[16,64,512]{2,1,0:T(8,128)(2,1)} %bitcast.9), calls=%async_computation | async-start | bytes 2097152 | tf_op jit(solution)/shard_map/all_to_all | solution.py:346
  8.2 22.9 %all-to-all-done.codes_ref = bf16[16,64,512]{2,1,0:T(8,128)(2,1)S(1)} async-done(((bf16[16,64,512]{2,1,0:T(8,128)(2,1)}), bf16[16,64,512]{2,1,0:T(8,128)(2,1)S(1)}, u32[]{:S(2)}, u32[]{:S(2)}) %all-to-all-start) | async-done | bytes 1048608 | tf_op jit(solution)/shard_map/all_to_all | solution.py:346
  31.1 0.0 copy-done.1
  31.1 0.0 copy-done.3
  31.1 1.4 %shard_map.67 = (bf16[256,128]{1,0:T(8,128)(2,1)S(1)}, f32[64,128]{1,0:T(8,128)S(1)}) custom-call(s32[1]{0:T(128)} %bitcast.me_ref, f32[64,512]{1,0:T(8,128)S(1)} %copy-done.1, bf16[16,64,512]{2,1,0:T(8,128)(2,1)S(1)} %all-to-all-done.codes_ref, f32[4,128]{1,0:T(4,128)S(1)} %bitcast.13), custom_call_target="tpu_custom_call" | custom-call | tf_op jit(solution)/shard_map/pallas_call | solution.py:290
  32.6 5.1 %collective-permute-start = (bf16[384,128]{1,0:T(8,128)(2,1)S(1)}, bf16[384,128]{1,0:T(8,128)(2,1)S(1)}, u32[]{:S(2)}, u32[]{:S(2)}) collective-permute-start(bf16[384,128]{1,0:T(8,128)(2,1)S(1)} %pad_maximum_fusion.4), channel_id=1, source_target_pairs={{0,8},{1,9},{2,10},{3,11},{4,12},{5,13},{6,14},{7,15},{8,0},{9,1},... | collective-permute-start | bytes 294920 | tf_op jit(solution)/shard_map/ppermute | solution.py:302
  37.7 4.7 %collective-permute-done = bf16[384,128]{1,0:T(8,128)(2,1)S(1)} collective-permute-done((bf16[384,128]{1,0:T(8,128)(2,1)S(1)}, bf16[384,128]{1,0:T(8,128)(2,1)S(1)}, u32[]{:S(2)}, u32[]{:S(2)}) %collective-permute-start) | collective-permute-done | bytes 98336 | tf_op jit(solution)/shard_map/ppermute | solution.py:302
  42.5 0.1 collective-permute-start.1
  42.6 5.3 %collective-permute-done.1 = bf16[640,128]{1,0:T(8,128)(2,1)S(1)} collective-permute-done((bf16[640,128]{1,0:T(8,128)(2,1)S(1)}, bf16[640,128]{1,0:T(8,128)(2,1)S(1)}, u32[]{:S(2)}, u32[]{:S(2)}) %collective-permute-start.1) | collective-permute-done | bytes 163872 | tf_op jit(solution)/shard_map/ppermute | solution.py:302
  47.9 0.1 collective-permute-start.2
  48.0 3.9 %collective-permute-done.2 = bf16[128,128]{1,0:T(8,128)(2,1)S(1)} collective-permute-done((bf16[128,128]{1,0:T(8,128)(2,1)S(1)}, bf16[128,128]{1,0:T(8,128)(2,1)S(1)}, u32[]{:S(2)}, u32[]{:S(2)}) %collective-permute-start.2) | collective-permute-done | bytes 32800 | tf_op jit(solution)/shard_map/ppermute | solution.py:302
  51.9 0.1 collective-permute-start.3
  52.0 0.0 copy-done.2
  52.0 0.1 dynamic-slice_bitcast_fusion
  52.1 0.1 copy.7.thresholds_ref
  52.2 0.0 copy-start
  52.2 1.0 %collective-permute-done.3.other_ref = bf16[128,128]{1,0:T(8,128)(2,1)S(1)} collective-permute-done((bf16[128,128]{1,0:T(8,128)(2,1)S(1)}, bf16[128,128]{1,0:T(8,128)(2,1)S(1)}, u32[]{:S(2)}, u32[]{:S(2)}) %collective-permute-start.3) | collective-permute-done | bytes 32800 | tf_op jit(solution)/shard_map/ppermute | solution.py:302
  53.2 3.3 %shard_map.68 = (bf16[256,128]{1,0:T(8,128)(2,1)S(1)}, bf16[23,64,512]{2,1,0:T(8,128)(2,1)S(1)}, f32[64,128]{1,0:T(8,128)S(1)}) custom-call(s32[1]{0:T(128)} %bitcast.me_ref, bf16[128,128]{1,0:T(8,128)(2,1)S(1)} %pad_maximum_fusion.7.sent_ref, bf16[128,128]{1,0:T(8,128)(2,1)S(1)} %collective-permute-done.3.other_ref, f32[64,512]{1,0:T(8,128)S(1)} %copy-done.1, ...), custom_call_target="tpu_custom_call" | custom-call | tf_op jit(solution)/shard_map/pallas_call | solution.py:290
  56.6 0.9 %collective-permute-start.4 = (bf16[384,128]{1,0:T(8,128)(2,1)S(1)}, bf16[384,128]{1,0:T(8,128)(2,1)S(1)}, u32[]{:S(2)}, u32[]{:S(2)}) collective-permute-start(bf16[384,128]{1,0:T(8,128)(2,1)S(1)} %pad_maximum_fusion.5), channel_id=1, source_target_pairs={{0,8},{1,9},{2,10},{3,11},{4,12},{5,13},{6,14},{7,15},{8,0},{9,1},... | collective-permute-start | bytes 294920 | tf_op jit(solution)/shard_map/ppermute | solution.py:302
  57.5 1.9 %collective-permute-start.5 = (bf16[1024,128]{1,0:T(8,128)(2,1)S(1)}, bf16[1024,128]{1,0:T(8,128)(2,1)S(1)}, u32[]{:S(2)}, u32[]{:S(2)}) collective-permute-start(bf16[1024,128]{1,0:T(8,128)(2,1)S(1)} %pad_maximum_fusion.1.refs_0_), channel_id=1, source_target_pairs={{0,2},{1,3},{2,0},{3,1},{4,6},{5,7},{6,4},{7,5},{8,10},{9,11},{10,... | collective-permute-start | bytes 786440 | tf_op jit(solution)/shard_map/ppermute | solution.py:302
  59.3 5.1 %collective-permute-done.4 = bf16[384,128]{1,0:T(8,128)(2,1)S(1)} collective-permute-done((bf16[384,128]{1,0:T(8,128)(2,1)S(1)}, bf16[384,128]{1,0:T(8,128)(2,1)S(1)}, u32[]{:S(2)}, u32[]{:S(2)}) %collective-permute-start.4) | collective-permute-done | bytes 98336 | tf_op jit(solution)/shard_map/ppermute | solution.py:302
  64.5 1.2 %collective-permute-done.5.refs_1_ = bf16[1024,128]{1,0:T(8,128)(2,1)S(1)} collective-permute-done((bf16[1024,128]{1,0:T(8,128)(2,1)S(1)}, bf16[1024,128]{1,0:T(8,128)(2,1)S(1)}, u32[]{:S(2)}, u32[]{:S(2)}) %collective-permute-start.5) | collective-permute-done | bytes 262176 | tf_op jit(solution)/shard_map/ppermute | solution.py:302
  65.7 1.7 %collective-permute-start.6 = (bf16[640,128]{1,0:T(8,128)(2,1)S(1)}, bf16[640,128]{1,0:T(8,128)(2,1)S(1)}, u32[]{:S(2)}, u32[]{:S(2)}) collective-permute-start(bf16[640,128]{1,0:T(8,128)(2,1)S(1)} %pad_maximum_fusion.3), channel_id=1, source_target_pairs={{0,4},{1,5},{2,6},{3,7},{4,0},{5,1},{6,2},{7,3},{8,12},{9,13},{10,... | collective-permute-start | bytes 491528 | tf_op jit(solution)/shard_map/ppermute | solution.py:302
  67.4 3.6 %collective-permute-done.6 = bf16[640,128]{1,0:T(8,128)(2,1)S(1)} collective-permute-done((bf16[640,128]{1,0:T(8,128)(2,1)S(1)}, bf16[640,128]{1,0:T(8,128)(2,1)S(1)}, u32[]{:S(2)}, u32[]{:S(2)}) %collective-permute-start.6) | collective-permute-done | bytes 163872 | tf_op jit(solution)/shard_map/ppermute | solution.py:302
  71.1 1.8 %collective-permute-start.7 = (bf16[1152,128]{1,0:T(8,128)(2,1)S(1)}, bf16[1152,128]{1,0:T(8,128)(2,1)S(1)}, u32[]{:S(2)}, u32[]{:S(2)}) collective-permute-start(bf16[1152,128]{1,0:T(8,128)(2,1)S(1)} %pad_maximum_fusion.refs_0_), channel_id=1, source_target_pairs={{0,2},{1,3},{2,0},{3,1},{4,6},{5,7},{6,4},{7,5},{8,10},{9,11},{10,... | collective-permute-start | bytes 884744 | tf_op jit(solution)/shard_map/ppermute | solution.py:302
  72.9 0.0 collective-permute-start.8
  72.9 0.5 collective-permute-start.9
  73.4 0.0 collective-permute-start.11
  73.4 1.0 %collective-permute-done.8.refs_2_ = bf16[1024,128]{1,0:T(8,128)(2,1)S(1)} collective-permute-done((bf16[1024,128]{1,0:T(8,128)(2,1)S(1)}, bf16[1024,128]{1,0:T(8,128)(2,1)S(1)}, u32[]{:S(2)}, u32[]{:S(2)}) %collective-permute-start.8) | collective-permute-done | bytes 262176 | tf_op jit(solution)/shard_map/ppermute | solution.py:302
  74.4 0.4 collective-permute-done.9.refs_3_
  74.8 0.0 copy-done
  74.8 0.9 %shard_map.69.values_ref = f32[1024,512]{1,0:T(8,128)S(1)} custom-call(s32[1]{0:T(128)} %bitcast.me_ref, bf16[23,64,512]{2,1,0:T(8,128)(2,1)S(1)} %get-tuple-element.20.kept_ref, bf16[1024,512]{1,0:T(8,128)(2,1)S(1)} %bitcast.10, f32[8,128]{1,0:T(8,128)S(1)} %bitcast.11, bf16[1024,128]{1,0:T(8,128)(2,1)S(1)} %pad_maximum_fusion.1.refs_0_, ...), custom_call_target="tpu_custom_call" | custom-call | tf_op jit(solution)/shard_map/pallas_call | solution.py:290
  75.7 2.4 %collective-permute-done.7.refs_1_ = bf16[1152,128]{1,0:T(8,128)(2,1)S(1)} collective-permute-done((bf16[1152,128]{1,0:T(8,128)(2,1)S(1)}, bf16[1152,128]{1,0:T(8,128)(2,1)S(1)}, u32[]{:S(2)}, u32[]{:S(2)}) %collective-permute-start.7) | collective-permute-done | bytes 294944 | tf_op jit(solution)/shard_map/ppermute | solution.py:302
  78.2 0.0 collective-permute-start.12
  78.2 0.6 collective-permute-start.10
  78.8 0.0 collective-permute-done.11.refs_2_
  78.8 1.0 %collective-permute-done.10.other_ref = bf16[128,128]{1,0:T(8,128)(2,1)S(1)} collective-permute-done((bf16[128,128]{1,0:T(8,128)(2,1)S(1)}, bf16[128,128]{1,0:T(8,128)(2,1)S(1)}, u32[]{:S(2)}, u32[]{:S(2)}) %collective-permute-start.10) | collective-permute-done | bytes 32800 | tf_op jit(solution)/shard_map/ppermute | solution.py:302
  79.8 0.0 collective-permute-done.12.refs_3_
  79.8 3.5 %shard_map.70 = (f32[64,512]{1,0:T(8,128)}, f32[4,128]{1,0:T(4,128)}, bf16[1024,512]{1,0:T(8,128)(2,1)}) custom-call(s32[1]{0:T(128)} %bitcast.me_ref, bf16[128,128]{1,0:T(8,128)(2,1)S(1)} %pad_maximum_fusion.8.sent_ref, bf16[128,128]{1,0:T(8,128)(2,1)S(1)} %collective-permute-done.10.other_ref, bf16[23,64,512]{2,1,0:T(8,128)(2,1)S(1)} %get-tuple-element.20.kept_ref, ...), custom_call_target="tpu_custom_call" | custom-call | tf_op jit(solution)/shard_map/pallas_call | solution.py:290
  (24 shorter events, 0.3 us)
Async XLA Ops:
  0.6 30.5 %copy-start.1 = (f32[64,512]{1,0:T(8,128)S(1)}, f32[64,512]{1,0:T(8,128)}, u32[]{:S(2)}) copy-start(f32[64,512]{1,0:T(8,128)} %atoms_ref.3) | copy-start | bytes 393220
  0.6 30.5 %copy-start.3 = (f32[1,512]{1,0:T(1,128)S(1)}, f32[1,512]{1,0:T(1,128)}, u32[]{:S(2)}) copy-start(f32[1,512]{1,0:T(1,128)} %param.4) | copy-start | bytes 6148
  0.7 51.4 %copy-start.2 = (f32[1024]{0:T(1024)S(1)}, f32[1024]{0:T(1024)}, u32[]{:S(2)}) copy-start(f32[1024]{0:T(1024)} %param.7) | copy-start | bytes 12292
  0.7 30.5 %all-to-all-start = ((bf16[16,64,512]{2,1,0:T(8,128)(2,1)}), bf16[16,64,512]{2,1,0:T(8,128)(2,1)S(1)}, u32[]{:S(2)}, u32[]{:S(2)}) async-start(bf16[16,64,512]{2,1,0:T(8,128)(2,1)} %bitcast.9), calls=%async_computation | async-start | bytes 2097152 | tf_op jit(solution)/shard_map/all_to_all | solution.py:346
  32.6 9.8 %collective-permute-start = (bf16[384,128]{1,0:T(8,128)(2,1)S(1)}, bf16[384,128]{1,0:T(8,128)(2,1)S(1)}, u32[]{:S(2)}, u32[]{:S(2)}) collective-permute-start(bf16[384,128]{1,0:T(8,128)(2,1)S(1)} %pad_maximum_fusion.4), channel_id=1, source_target_pairs={{0,8},{1,9},{2,10},{3,11},{4,12},{5,13},{6,14},{7,15},{8,0},{9,1},... | collective-permute-start | bytes 294920 | tf_op jit(solution)/shard_map/ppermute | solution.py:302
  42.5 5.4 %collective-permute-start.1 = (bf16[640,128]{1,0:T(8,128)(2,1)S(1)}, bf16[640,128]{1,0:T(8,128)(2,1)S(1)}, u32[]{:S(2)}, u32[]{:S(2)}) collective-permute-start(bf16[640,128]{1,0:T(8,128)(2,1)S(1)} %pad_maximum_fusion.2), channel_id=1, source_target_pairs={{0,4},{1,5},{2,6},{3,7},{4,0},{5,1},{6,2},{7,3},{8,12},{9,13},{10,... | collective-permute-start | bytes 491528 | tf_op jit(solution)/shard_map/ppermute | solution.py:302
  47.9 4.0 %collective-permute-start.2 = (bf16[128,128]{1,0:T(8,128)(2,1)S(1)}, bf16[128,128]{1,0:T(8,128)(2,1)S(1)}, u32[]{:S(2)}, u32[]{:S(2)}) collective-permute-start(bf16[128,128]{1,0:T(8,128)(2,1)S(1)} %pad_maximum_fusion.6), channel_id=1, source_target_pairs={{0,2},{1,3},{2,0},{3,1},{4,6},{5,7},{6,4},{7,5},{8,10},{9,11},{10,... | collective-permute-start | bytes 98312 | tf_op jit(solution)/shard_map/ppermute | solution.py:302
  51.9 1.3 %collective-permute-start.3 = (bf16[128,128]{1,0:T(8,128)(2,1)S(1)}, bf16[128,128]{1,0:T(8,128)(2,1)S(1)}, u32[]{:S(2)}, u32[]{:S(2)}) collective-permute-start(bf16[128,128]{1,0:T(8,128)(2,1)S(1)} %pad_maximum_fusion.7.sent_ref), channel_id=1, source_target_pairs={{0,1},{1,0},{2,3},{3,2},{4,5},{5,4},{6,7},{7,6},{8,9},{9,8},{10,11... | collective-permute-start | bytes 98312 | tf_op jit(solution)/shard_map/ppermute | solution.py:302
  52.2 22.6 %copy-start = (bf16[1,1024,512]{2,1,0:T(8,128)(2,1)S(1)}, bf16[1,1024,512]{2,1,0:T(8,128)(2,1)}, u32[]{:S(2)}) copy-start(bf16[1,1024,512]{2,1,0:T(8,128)(2,1)} %param.5) | copy-start | bytes 3145732
  56.6 7.9 %collective-permute-start.4 = (bf16[384,128]{1,0:T(8,128)(2,1)S(1)}, bf16[384,128]{1,0:T(8,128)(2,1)S(1)}, u32[]{:S(2)}, u32[]{:S(2)}) collective-permute-start(bf16[384,128]{1,0:T(8,128)(2,1)S(1)} %pad_maximum_fusion.5), channel_id=1, source_target_pairs={{0,8},{1,9},{2,10},{3,11},{4,12},{5,13},{6,14},{7,15},{8,0},{9,1},... | collective-permute-start | bytes 294920 | tf_op jit(solution)/shard_map/ppermute | solution.py:302
  57.5 8.2 %collective-permute-start.5 = (bf16[1024,128]{1,0:T(8,128)(2,1)S(1)}, bf16[1024,128]{1,0:T(8,128)(2,1)S(1)}, u32[]{:S(2)}, u32[]{:S(2)}) collective-permute-start(bf16[1024,128]{1,0:T(8,128)(2,1)S(1)} %pad_maximum_fusion.1.refs_0_), channel_id=1, source_target_pairs={{0,2},{1,3},{2,0},{3,1},{4,6},{5,7},{6,4},{7,5},{8,10},{9,11},{10,... | collective-permute-start | bytes 786440 | tf_op jit(solution)/shard_map/ppermute | solution.py:302
  65.7 5.3 %collective-permute-start.6 = (bf16[640,128]{1,0:T(8,128)(2,1)S(1)}, bf16[640,128]{1,0:T(8,128)(2,1)S(1)}, u32[]{:S(2)}, u32[]{:S(2)}) collective-permute-start(bf16[640,128]{1,0:T(8,128)(2,1)S(1)} %pad_maximum_fusion.3), channel_id=1, source_target_pairs={{0,4},{1,5},{2,6},{3,7},{4,0},{5,1},{6,2},{7,3},{8,12},{9,13},{10,... | collective-permute-start | bytes 491528 | tf_op jit(solution)/shard_map/ppermute | solution.py:302
  71.1 7.0 %collective-permute-start.7 = (bf16[1152,128]{1,0:T(8,128)(2,1)S(1)}, bf16[1152,128]{1,0:T(8,128)(2,1)S(1)}, u32[]{:S(2)}, u32[]{:S(2)}) collective-permute-start(bf16[1152,128]{1,0:T(8,128)(2,1)S(1)} %pad_maximum_fusion.refs_0_), channel_id=1, source_target_pairs={{0,2},{1,3},{2,0},{3,1},{4,6},{5,7},{6,4},{7,5},{8,10},{9,11},{10,... | collective-permute-start | bytes 884744 | tf_op jit(solution)/shard_map/ppermute | solution.py:302
  72.9 1.5 %collective-permute-start.8 = (bf16[1024,128]{1,0:T(8,128)(2,1)S(1)}, bf16[1024,128]{1,0:T(8,128)(2,1)S(1)}, u32[]{:S(2)}, u32[]{:S(2)}) collective-permute-start(bf16[1024,128]{1,0:T(8,128)(2,1)S(1)} %pad_maximum_fusion.1.refs_0_), channel_id=1, source_target_pairs={{0,1},{1,0},{2,3},{3,2},{4,5},{5,4},{6,7},{7,6},{8,9},{9,8},{10,11... | collective-permute-start | bytes 786440 | tf_op jit(solution)/shard_map/ppermute | solution.py:302
  72.9 1.9 %collective-permute-start.9 = (bf16[1024,128]{1,0:T(8,128)(2,1)S(1)}, bf16[1024,128]{1,0:T(8,128)(2,1)S(1)}, u32[]{:S(2)}, u32[]{:S(2)}) collective-permute-start(bf16[1024,128]{1,0:T(8,128)(2,1)S(1)} %collective-permute-done.5.refs_1_), channel_id=1, source_target_pairs={{0,1},{1,0},{2,3},{3,2},{4,5},{5,4},{6,7},{7,6},{8,9},{9,8},{10,11... | collective-permute-start | bytes 786440 | tf_op jit(solution)/shard_map/ppermute | solution.py:302
  73.4 5.4 %collective-permute-start.11 = (bf16[1152,128]{1,0:T(8,128)(2,1)S(1)}, bf16[1152,128]{1,0:T(8,128)(2,1)S(1)}, u32[]{:S(2)}, u32[]{:S(2)}) collective-permute-start(bf16[1152,128]{1,0:T(8,128)(2,1)S(1)} %pad_maximum_fusion.refs_0_), channel_id=1, source_target_pairs={{0,1},{1,0},{2,3},{3,2},{4,5},{5,4},{6,7},{7,6},{8,9},{9,8},{10,11... | collective-permute-start | bytes 884744 | tf_op jit(solution)/shard_map/ppermute | solution.py:302
  78.2 1.6 %collective-permute-start.12 = (bf16[1152,128]{1,0:T(8,128)(2,1)S(1)}, bf16[1152,128]{1,0:T(8,128)(2,1)S(1)}, u32[]{:S(2)}, u32[]{:S(2)}) collective-permute-start(bf16[1152,128]{1,0:T(8,128)(2,1)S(1)} %collective-permute-done.7.refs_1_), channel_id=1, source_target_pairs={{0,1},{1,0},{2,3},{3,2},{4,5},{5,4},{6,7},{7,6},{8,9},{9,8},{10,11... | collective-permute-start | bytes 884744 | tf_op jit(solution)/shard_map/ppermute | solution.py:302
  78.2 1.6 %collective-permute-start.10 = (bf16[128,128]{1,0:T(8,128)(2,1)S(1)}, bf16[128,128]{1,0:T(8,128)(2,1)S(1)}, u32[]{:S(2)}, u32[]{:S(2)}) collective-permute-start(bf16[128,128]{1,0:T(8,128)(2,1)S(1)} %pad_maximum_fusion.8.sent_ref), channel_id=1, source_target_pairs={{0,1},{1,0},{2,3},{3,2},{4,5},{5,4},{6,7},{7,6},{8,9},{9,8},{10,11... | collective-permute-start | bytes 98312 | tf_op jit(solution)/shard_map/ppermute | solution.py:302
